TPU v7x, 32 devices: a whole 2x2x4 slice. The times are simulated.
32 devices in a mesh: node: 16 (over z, y, x), edge: 2 (over core).
Axes of the slice: x: 2, y: 2, z: 4, core: 2. Of those that a mesh axis runs over, the one named last changes fastest.
Arguments:
- embedding: bfloat16 [128, 128, 512], P('node'), may hold values from -6 to 6
- send_list: int32 [2, 16, 16], P('edge', 'node'), may hold values from -1 to 7, as said below
- edge_ends: int32 [2, 65536], P(None, ('node', 'edge')), may hold values from 0 to 16383, as said below
- pair_index: int32 [65536], P(('node', 'edge')), may hold values from 0 to 16383, as said below
- w_first: bfloat16 [1024, 512], replicated, may hold values from -0.1875 to 0.1875
- b_first: float32 [512], replicated, may hold values from -3 to 3
- w_second: bfloat16 [512], replicated, may hold values from -0.25 to 0.25
Outputs:
- edge_score: float32 [65536], P(('node', 'edge'))
- pair_cost: float32 [16384], P(('node', 'edge'))
Inputs may be any that keep to these rules, and one draw needn't show every extreme that they name: Each entry is -1 or a block index of the sending node index; send_list[e, k, k] is never -1. `edge_ends`: node ids; most ends lie in a block that the send list delivers to the edge's node group and edge index. `pair_index`: an edge of node group j has a pair in j * 1024 to (j + 1) * 1024 - 1.
All inputs are finite; a program needn't handle non-finite values.
Results may differ from a plain program's by a relative error of at most 0.0003.
Values may be sent and summed in bfloat16 or wider, within the bound.
No kernel may reach another device: no remote copies, remote signals or barrier semaphores. Data moves between devices by JAX's collectives and lax.ppermute only.
A program may use at most 64 MiB of HBM per device.

v0:
```python
import jax
import jax.numpy as jnp
from jax import lax
from jax.sharding import PartitionSpec as P

PAIRS_ROW = 1024


def body(embedding, send_list, edge_ends, pair_index, w_first, b_first, w_second):
    node_count = lax.axis_size("node")
    node_self = lax.axis_index("node")
    blocks_here = embedding.shape[0]
    block_rows = embedding.shape[1]
    feature_width = embedding.shape[2]
    wanted = send_list[0, 0]
    picked = jnp.take(embedding, jnp.clip(wanted, 0, blocks_here - 1), axis=0)
    picked = jnp.where((wanted >= 0)[:, None, None], picked, jnp.zeros_like(picked))
    labels = jnp.where(wanted >= 0, node_self * blocks_here + wanted, -1)
    arrived, slot_ids = (
        lax.all_to_all(picked, "node", split_axis=0, concat_axis=0, tiled=True),
        lax.all_to_all(labels, "node", split_axis=0, concat_axis=0, tiled=True),
    )
    flat_rows = arrived.reshape(node_count * block_rows, feature_width)
    target = edge_ends // block_rows
    within = edge_ends % block_rows
    matches = target[..., None] == slot_ids
    located = jnp.any(matches, axis=-1)
    slot_index = jnp.sum(jnp.where(matches, jnp.arange(node_count, dtype=jnp.int32), 0), axis=-1)
    position = slot_index * block_rows + within
    edge_total = edge_ends.shape[1]
    tile_rows = min(512, edge_total)
    tile_count = edge_total // tile_rows
    position = position.reshape(2, tile_count, tile_rows).transpose(1, 0, 2)
    located = located.reshape(2, tile_count, tile_rows).transpose(1, 0, 2)
    pair_ids = (pair_index - node_self * PAIRS_ROW).reshape(tile_count, tile_rows)
    upper = w_first[:feature_width]
    bottom = w_first[feature_width:]
    w_out = w_second.astype(jnp.float32)
    pair_range = jnp.arange(PAIRS_ROW, dtype=jnp.int32)

    def tile_step(pooled_sum, pieces):
        rows_at, present, pair_here = pieces
        end_rows = jnp.take(flat_rows, rows_at, axis=0)
        end_rows = jnp.where(present[..., None], end_rows, jnp.zeros_like(end_rows))
        preact = jnp.dot(end_rows[0], upper, preferred_element_type=jnp.float32)
        preact = preact + jnp.dot(end_rows[1], bottom, preferred_element_type=jnp.float32) + b_first
        hidden = jax.nn.gelu(preact, approximate=True)
        scores = jnp.dot(hidden, w_out, precision=lax.Precision.HIGHEST)
        onehot = (pair_here[:, None] == pair_range[None, :]).astype(jnp.float32)
        pooled_sum = pooled_sum + jnp.dot(scores, onehot, precision=lax.Precision.HIGHEST)
        return (pooled_sum, scores)

    pooled_sum, scores = lax.scan(
        tile_step, jnp.zeros((PAIRS_ROW,), jnp.float32), (position, located, pair_ids)
    )
    edge_score = scores.reshape(edge_total)
    pair_cost = lax.psum_scatter(pooled_sum, "edge", scatter_dimension=0, tiled=True)
    return (edge_score, pair_cost)


def solution(mesh):
    return jax.shard_map(
        body,
        mesh=mesh,
        in_specs=(
            P("node", None, None),
            P("edge", "node", None),
            P(None, ("node", "edge")),
            P(("node", "edge")),
            P(),
            P(),
            P(),
        ),
        out_specs=(P(("node", "edge")), P(("node", "edge"))),
        check_vma=False,
    )
```

profile of v0, /device:TPU:9, one launch (start us, length us, event | category | flops | bytes accessed | tf_op | source)
XLA Modules:
  0.0 110.9 jit_solution(11214065662693628821)
XLA Ops:
  0.6 0.0 copy-start
  0.6 0.7 fusion.17
  1.4 0.7 copy.11
  2.1 6.7 %all-to-all-start = ((s32[16,1,1]{2,1,0:T(1,128)}), s32[16,1,1]{2,1,0:T(1,128)S(1)}, u32[]{:S(2)}, u32[]{:S(2)}) async-start(s32[16,1,1]{2,1,0:T(1,128)} %copy.11), calls=%async_computation | async-start | bytes 16384 | tf_op jit(solution)/shard_map/all_to_all | solution.py:21
  8.7 0.7 fusion.18
  9.4 0.7 compare_and_fusion.1
  10.1 0.7 compare_bitcast_fusion
  10.7 0.7 gather_fusion.1
  11.4 1.6 %select_select_fusion.1 = bf16[16,128,512]{2,1,0:T(8,128)(2,1)} fusion(bf16[16,128,512]{2,1,0:T(8,128)(2,1)S(1)} %gather_fusion.1, pred[16]{0:T(512)(128)(4,1)S(1)} %compare_and_fusion.1, pred[16]{0:T(512)(128)(4,1)S(1)} %compare_bitcast_fusion), kind=kLoop, calls=%fused_computation.29 | loop fusion | flops 2097152 | bytes 4194336 | tf_op jit(solution)/shard_map/jit(_where)/select_n | solution.py:17
  13.1 0.6 all-to-all-done
  13.7 5.9 %all-to-all-start.1 = ((bf16[16,128,512]{2,1,0:T(8,128)(2,1)}), bf16[16,128,512]{2,1,0:T(8,128)(2,1)S(1)}, u32[]{:S(2)}, u32[]{:S(2)}) async-start(bf16[16,128,512]{2,1,0:T(8,128)(2,1)} %select_select_fusion.1), calls=%async_computation.1 | async-start | bytes 4194304 | tf_op jit(solution)/shard_map/all_to_all | solution.py:20
  19.6 0.0 copy-start.6
  19.7 0.6 dynamic-slice
  20.9 2.3 %fusion.19 = (bf16[512,512]{1,0:T(8,128)(2,1)}, bf16[512,512]{1,0:T(8,128)(2,1)}) fusion(bf16[1024,512]{1,0:T(8,128)(2,1)} %param.13), kind=kLoop, calls=%fused_computation.50 | loop fusion | bytes 2097152 | tf_op jit(solution)/shard_map/slice | solution.py:37
  23.3 0.4 reduce
  23.6 0.1 compare_reduce_fusion
  23.8 0.1 fusion.15
  24.0 41.9 %all-to-all-done.1 = bf16[16,128,512]{2,1,0:T(8,128)(2,1)S(1)} async-done(((bf16[16,128,512]{2,1,0:T(8,128)(2,1)}), bf16[16,128,512]{2,1,0:T(8,128)(2,1)S(1)}, u32[]{:S(2)}, u32[]{:S(2)}) %all-to-all-start.1) | async-done | bytes 2097184 | tf_op jit(solution)/shard_map/all_to_all | solution.py:20
  65.8 0.0 copy-done.6
  65.8 39.1 %while.13 = (s32[]{:T(128)}, f32[1024]{0:T(1024)S(1)}, f32[4,512]{1,0:T(4,128)S(1)}, pred[4,2,512]{2,1,0:T(4,128)(4,1)S(1)}, s32[4,2,512]{2,1,0:T(2,128)S(1)}, /...) while((s32[]{:T(128)}, f32[1024]{0:T(1024)S(1)}, ...), condition=%wide.region_3.4_spmd.clone, body=%wide.region_2.3_spmd.clone.sunk | while | flops 550514688 | bytes 14752979 | solution.py:53
  65.9 5.1 %gather_fusion = bf16[1024,512]{1,0:T(8,128)(2,1)} fusion(bf16[2048,512]{1,0:T(8,128)(2,1)S(1)} %get-tuple-element.227, s32[1024]{0:T(1024)S(1)} %broadcast_clamp_fusion.2), kind=kCustom, calls=%fused_computation.clone.clone.1 | custom fusion | bytes 2101248 | tf_op jit(solution)/shard_map/while/body/eval_jaxpr/jit(_take)/gather | solution.py:43
  71.0 0.0 copy-start.2
  71.0 1.6 %select_select_fusion.3 = bf16[2,512,512]{2,1,0:T(8,128)(2,1)S(1)} fusion(bf16[2,512,512]{2,1,0:T(8,128)(2,1)} %bitcast.81, pred[2,512]{1,0:T(4,128)(4,1)S(1)} %compare_and_fusion.3, pred[2,512]{1,0:T(4,128)(4,1)S(1)} %dynamic-slice_bitcast_fusion.2), kind=kLoop, calls=%fused_computation.16.clone.1 | loop fusion | flops 1048576 | bytes 2099200 | tf_op jit(solution)/shard_map/while/body/eval_jaxpr/jit(_where)/select_n | solution.py:44
  72.6 0.4 fusion.41
  73.0 0.7 fusion.42
  73.7 1.0 fusion.43
  74.8 0.8 fusion.44
  75.6 5.1 %gather_fusion = bf16[1024,512]{1,0:T(8,128)(2,1)} fusion(bf16[2048,512]{1,0:T(8,128)(2,1)S(1)} %get-tuple-element.227, s32[1024]{0:T(1024)S(1)} %broadcast_clamp_fusion.2), kind=kCustom, calls=%fused_computation.clone.clone.1 | custom fusion | bytes 2101248 | tf_op jit(solution)/shard_map/while/body/eval_jaxpr/jit(_take)/gather | solution.py:43
  80.8 1.6 %select_select_fusion.3 = bf16[2,512,512]{2,1,0:T(8,128)(2,1)S(1)} fusion(bf16[2,512,512]{2,1,0:T(8,128)(2,1)} %bitcast.81, pred[2,512]{1,0:T(4,128)(4,1)S(1)} %compare_and_fusion.3, pred[2,512]{1,0:T(4,128)(4,1)S(1)} %dynamic-slice_bitcast_fusion.2), kind=kLoop, calls=%fused_computation.16.clone.1 | loop fusion | flops 1048576 | bytes 2099200 | tf_op jit(solution)/shard_map/while/body/eval_jaxpr/jit(_where)/select_n | solution.py:44
  82.4 0.4 fusion.41
  82.8 0.7 fusion.42
  83.5 1.0 fusion.43
  84.6 0.8 fusion.44
  85.4 5.1 %gather_fusion = bf16[1024,512]{1,0:T(8,128)(2,1)} fusion(bf16[2048,512]{1,0:T(8,128)(2,1)S(1)} %get-tuple-element.227, s32[1024]{0:T(1024)S(1)} %broadcast_clamp_fusion.2), kind=kCustom, calls=%fused_computation.clone.clone.1 | custom fusion | bytes 2101248 | tf_op jit(solution)/shard_map/while/body/eval_jaxpr/jit(_take)/gather | solution.py:43
  90.6 1.6 %select_select_fusion.3 = bf16[2,512,512]{2,1,0:T(8,128)(2,1)S(1)} fusion(bf16[2,512,512]{2,1,0:T(8,128)(2,1)} %bitcast.81, pred[2,512]{1,0:T(4,128)(4,1)S(1)} %compare_and_fusion.3, pred[2,512]{1,0:T(4,128)(4,1)S(1)} %dynamic-slice_bitcast_fusion.2), kind=kLoop, calls=%fused_computation.16.clone.1 | loop fusion | flops 1048576 | bytes 2099200 | tf_op jit(solution)/shard_map/while/body/eval_jaxpr/jit(_where)/select_n | solution.py:44
  92.2 0.4 fusion.41
  92.6 0.7 fusion.42
  93.3 1.0 fusion.43
  94.4 0.8 fusion.44
  95.2 5.1 %gather_fusion = bf16[1024,512]{1,0:T(8,128)(2,1)} fusion(bf16[2048,512]{1,0:T(8,128)(2,1)S(1)} %get-tuple-element.227, s32[1024]{0:T(1024)S(1)} %broadcast_clamp_fusion.2), kind=kCustom, calls=%fused_computation.clone.clone.1 | custom fusion | bytes 2101248 | tf_op jit(solution)/shard_map/while/body/eval_jaxpr/jit(_take)/gather | solution.py:43
  100.3 1.6 %select_select_fusion.3 = bf16[2,512,512]{2,1,0:T(8,128)(2,1)S(1)} fusion(bf16[2,512,512]{2,1,0:T(8,128)(2,1)} %bitcast.81, pred[2,512]{1,0:T(4,128)(4,1)S(1)} %compare_and_fusion.3, pred[2,512]{1,0:T(4,128)(4,1)S(1)} %dynamic-slice_bitcast_fusion.2), kind=kLoop, calls=%fused_computation.16.clone.1 | loop fusion | flops 1048576 | bytes 2099200 | tf_op jit(solution)/shard_map/while/body/eval_jaxpr/jit(_where)/select_n | solution.py:44
  101.9 0.4 fusion.41
  102.4 0.7 fusion.42
  103.1 1.0 fusion.43
  104.1 0.8 fusion.44
  105.0 4.6 %all-reduce = f32[1024]{0:T(1024)S(1)} all-reduce(f32[1024]{0:T(1024)S(1)} %get-tuple-element.66), channel_id=2, replica_groups=mesh['node'=16,'edge'=2] {'edge'}, use_global_device_ids=true, to_apply=%region_4.5.clone | all-reduce | flops 1024 | bytes 8192
  109.6 0.6 copy.15
  110.2 0.6 dynamic-slice.1
  (64 shorter events, 0.5 us)
Async XLA Ops:
  0.6 10.1 %copy-start = (bf16[8,128,512]{2,1,0:T(8,128)(2,1)S(1)}, bf16[8,128,512]{2,1,0:T(8,128)(2,1)}, u32[]{:S(2)}) copy-start(bf16[8,128,512]{2,1,0:T(8,128)(2,1)} %param.9) | copy-start | bytes 3145732
  2.1 11.6 %all-to-all-start = ((s32[16,1,1]{2,1,0:T(1,128)}), s32[16,1,1]{2,1,0:T(1,128)S(1)}, u32[]{:S(2)}, u32[]{:S(2)}) async-start(s32[16,1,1]{2,1,0:T(1,128)} %copy.11), calls=%async_computation | async-start | bytes 16384 | tf_op jit(solution)/shard_map/all_to_all | solution.py:21
  13.1 6.6 %copy-start.4 = (s32[2048]{0:T(1024)S(1)}, s32[2048]{0:T(1024)}, u32[]{:S(2)}) copy-start(s32[2048]{0:T(1024)} %param.12) | copy-start | bytes 24580
  13.1 6.6 %copy-start.5 = (bf16[512]{0:T(512)(128)(2,1)S(1)}, bf16[512]{0:T(512)(128)(2,1)}, u32[]{:S(2)}) copy-start(bf16[512]{0:T(512)(128)(2,1)} %param.15) | copy-start | bytes 3076
  13.1 6.6 %copy-start.7 = (u32[32]{0:T(128)S(1)}, u32[32]{0:T(128)}, u32[]{:S(2)}) copy-start(u32[32]{0:T(128)} %constant.105) | copy-start | bytes 388
  13.7 52.1 %all-to-all-start.1 = ((bf16[16,128,512]{2,1,0:T(8,128)(2,1)}), bf16[16,128,512]{2,1,0:T(8,128)(2,1)S(1)}, u32[]{:S(2)}, u32[]{:S(2)}) async-start(bf16[16,128,512]{2,1,0:T(8,128)(2,1)} %select_select_fusion.1), calls=%async_computation.1 | async-start | bytes 4194304 | tf_op jit(solution)/shard_map/all_to_all | solution.py:20
  19.6 3.6 %copy-start.3 = (s32[2,2048]{1,0:T(2,128)S(1)}, s32[2,2048]{1,0:T(2,128)}, u32[]{:S(2)}) copy-start(s32[2,2048]{1,0:T(2,128)} %param.11) | copy-start | bytes 49156
  19.6 46.2 %copy-start.6 = (f32[512]{0:T(512)S(1)}, f32[512]{0:T(512)}, u32[]{:S(2)}) copy-start(f32[512]{0:T(512)} %param.14) | copy-start | bytes 6148
  71.0 1.6 %copy-start.1 = (bf16[512,512]{1,0:T(8,128)(2,1)S(1)}, bf16[512,512]{1,0:T(8,128)(2,1)}, u32[]{:S(2)}) copy-start(bf16[512,512]{1,0:T(8,128)(2,1)} %get-tuple-element.228) | copy-start | bytes 1572868 | tf_op jit(solution)/shard_map/while
  71.0 2.0 %copy-start.2 = (bf16[512,512]{1,0:T(8,128)(2,1)S(1)}, bf16[512,512]{1,0:T(8,128)(2,1)}, u32[]{:S(2)}) copy-start(bf16[512,512]{1,0:T(8,128)(2,1)} %get-tuple-element.229) | copy-start | bytes 1572868 | tf_op jit(solution)/shard_map/while
  80.7 1.6 %copy-start.1 = (bf16[512,512]{1,0:T(8,128)(2,1)S(1)}, bf16[512,512]{1,0:T(8,128)(2,1)}, u32[]{:S(2)}) copy-start(bf16[512,512]{1,0:T(8,128)(2,1)} %get-tuple-element.228) | copy-start | bytes 1572868 | tf_op jit(solution)/shard_map/while
  80.8 2.0 %copy-start.2 = (bf16[512,512]{1,0:T(8,128)(2,1)S(1)}, bf16[512,512]{1,0:T(8,128)(2,1)}, u32[]{:S(2)}) copy-start(bf16[512,512]{1,0:T(8,128)(2,1)} %get-tuple-element.229) | copy-start | bytes 1572868 | tf_op jit(solution)/shard_map/while
  90.5 1.6 %copy-start.1 = (bf16[512,512]{1,0:T(8,128)(2,1)S(1)}, bf16[512,512]{1,0:T(8,128)(2,1)}, u32[]{:S(2)}) copy-start(bf16[512,512]{1,0:T(8,128)(2,1)} %get-tuple-element.228) | copy-start | bytes 1572868 | tf_op jit(solution)/shard_map/while
  90.5 2.0 %copy-start.2 = (bf16[512,512]{1,0:T(8,128)(2,1)S(1)}, bf16[512,512]{1,0:T(8,128)(2,1)}, u32[]{:S(2)}) copy-start(bf16[512,512]{1,0:T(8,128)(2,1)} %get-tuple-element.229) | copy-start | bytes 1572868 | tf_op jit(solution)/shard_map/while
  100.3 1.6 %copy-start.1 = (bf16[512,512]{1,0:T(8,128)(2,1)S(1)}, bf16[512,512]{1,0:T(8,128)(2,1)}, u32[]{:S(2)}) copy-start(bf16[512,512]{1,0:T(8,128)(2,1)} %get-tuple-element.228) | copy-start | bytes 1572868 | tf_op jit(solution)/shard_map/while
  100.3 2.0 %copy-start.2 = (bf16[512,512]{1,0:T(8,128)(2,1)S(1)}, bf16[512,512]{1,0:T(8,128)(2,1)}, u32[]{:S(2)}) copy-start(bf16[512,512]{1,0:T(8,128)(2,1)} %get-tuple-element.229) | copy-start | bytes 1572868 | tf_op jit(solution)/shard_map/while
where the time goes:
time: 112 us; the launch traced here: 111 us
  waiting for transfers between devices  42.5 us (38%)
  local copies, waits for them, and re-layouts  26.2 us (23%)
  starting transfers between devices  12.5 us (11%)
  matrix products  11.7 us (10%)
  other arithmetic  11.5 us (10%)
  blocking collectives  4.65 us (4%)
  between operations  1.43 us (1%)
    all_to_all x1, waiting for transfers between devices, body(): lax.all_to_all(picked, 'node', split_axis=0, concat_axis=0, tiled=True)  41.9 us
    gather x4, local copies, waits for them, and re-layouts, tile_step(): end_rows = jnp.take(flat_rows, rows_at, axis=0)  20.3 us
    all_to_all x1, starting transfers between devices, body(): lax.all_to_all(labels, 'node', split_axis=0, concat_axis=0, tiled=True)  6.66 us
    select_n x4, other arithmetic, tile_step(): end_rows = jnp.where(present[..., None], end_rows, jnp.zeros_like(end_rows))  6.33 us
    all_to_all x1, starting transfers between devices, body(): lax.all_to_all(picked, 'node', split_axis=0, concat_axis=0, tiled=True)  5.87 us
    unnamed x1, blocking collectives  4.65 us
    dot_general x4, matrix products, tile_step(): scores = jnp.dot(hidden, w_out, precision=lax.Precision.HIGHEST)  3.93 us
    dot_general x4, matrix products, tile_step(): jnp.dot(scores, onehot, precision=lax.Precision.HIGHEST)  3.26 us
  transfers between devices with their start and end apart: 2, of which 2 were waited for; matrix products, arithmetic and copies ran while one was open for 7% of the time, Pallas kernels for 0%

commit v1 on v0

v1 whole, which is shorter than its diff:
```python
import functools

import jax
import jax.numpy as jnp
from jax import lax
from jax.experimental import pallas as pl
from jax.experimental.pallas import tpu as pltpu
from jax.sharding import PartitionSpec as P

PAIRS_ROW = 1024
LANES = 128
LEAD = 8


def scorer(
    edge_total,
    parts,
    rows_ref,
    offsets_hbm,
    pair_ref,
    weight_ref,
    bias_ref,
    out_weight_ref,
    score_ref,
    pooled_ref,
    first_table,
    second_table,
    terms,
    offsets,
    offsets_sem,
):
    row_total = rows_ref.shape[0]
    hidden_width = parts * LANES
    offsets_copy = pltpu.make_async_copy(offsets_hbm, offsets, offsets_sem)
    offsets_copy.start()

    tile = 256
    bias = bias_ref[...]
    last = LEAD + row_total * parts
    first_table[pl.ds(last, 8), :] = bias
    second_table[pl.ds(last, 8), :] = jnp.zeros((8, LANES), jnp.float32)

    def project(step, carry):
        start = pl.multiple_of(step * tile, tile)
        rows = rows_ref[pl.ds(start, tile), :]
        shares = jnp.dot(rows, weight_ref[...], preferred_element_type=jnp.float32)
        for part in range(parts):
            lower = shares[:, part * LANES : (part + 1) * LANES]
            upper = shares[:, hidden_width + part * LANES : hidden_width + (part + 1) * LANES]
            at = pl.ds(LEAD + start * parts + part, tile, stride=parts)
            first_table[at, :] = lower + bias[part : part + 1, :]
            second_table[at, :] = upper
        return carry

    lax.fori_loop(0, row_total // tile, project, 0)
    offsets_copy.wait()

    out_weight = out_weight_ref[...]
    early = lax.broadcasted_iota(jnp.int32, (8, LANES), 0) < parts
    group = 16

    def score_group(step, carry):
        for pair in range(group // 2):
            edge = step * group + 2 * pair
            first = jnp.where(
                early,
                first_table[pl.ds(offsets[edge], 8), :],
                first_table[pl.ds(offsets[edge + 1], 8), :],
            )
            second = jnp.where(
                early,
                second_table[pl.ds(offsets[edge_total + edge], 8), :],
                second_table[pl.ds(offsets[edge_total + edge + 1], 8), :],
            )
            x = first + second
            inner = x * (0.7978845608028654 + (0.7978845608028654 * 0.044715) * (x * x))
            weighted = x * out_weight
            terms[pl.ds(pl.multiple_of(edge * parts, 8), 8), :] = weighted + weighted * jnp.tanh(inner)
        return carry

    lax.fori_loop(0, edge_total // group, score_group, 0)

    sums = terms[pl.ds(0, edge_total, stride=parts), :]
    for part in range(1, parts):
        sums = sums + terms[pl.ds(part, edge_total, stride=parts), :]
    ones = jnp.ones((8, LANES), jnp.float32)
    scores = lax.dot_general(
        ones, sums, (((1,), (1,)), ((), ())), precision=lax.Precision.HIGHEST, preferred_element_type=jnp.float32
    )
    score_ref[...] = scores[0:1, :]

    pair = pair_ref[...]
    pair_rows = PAIRS_ROW // LANES
    high = lax.broadcasted_iota(jnp.int32, (pair_rows, edge_total), 0) == pair // LANES
    low = lax.broadcasted_iota(jnp.int32, (LANES, edge_total), 0) == pair % LANES
    spread = jnp.where(high, scores[:pair_rows], 0.0)
    pooled_ref[...] = lax.dot_general(
        spread,
        low.astype(jnp.float32),
        (((1,), (1,)), ((), ())),
        precision=lax.Precision.HIGHEST,
        preferred_element_type=jnp.float32,
    )


def body(embedding, send_list, edge_ends, pair_index, w_first, b_first, w_second):
    node_count = lax.axis_size("node")
    node_self = lax.axis_index("node")
    blocks_here, block_rows, feature_width = embedding.shape
    hidden_width = w_first.shape[1]
    parts = hidden_width // LANES
    edge_total = edge_ends.shape[1]
    row_total = node_count * block_rows

    wanted = send_list[0, 0]
    picked = jnp.take(embedding, jnp.clip(wanted, 0, blocks_here - 1), axis=0)
    arrived = lax.all_to_all(picked, "node", split_axis=0, concat_axis=0, tiled=True)
    rows = arrived.reshape(row_total, feature_width)

    lists = lax.all_gather(wanted, "node")
    block_here = lax.dynamic_index_in_dim(lists, node_self, 1, False)
    target = edge_ends // block_rows
    source = target // blocks_here
    sources = jnp.arange(node_count, dtype=jnp.int32)
    delivered = jnp.sum(jnp.where(source[..., None] == sources, block_here, 0), axis=-1)
    row = jnp.where(delivered == target % blocks_here, source * block_rows + edge_ends % block_rows, row_total)
    second_of_two = jnp.arange(edge_total, dtype=jnp.int32) % 2
    offsets = (LEAD + row * parts - second_of_two * parts).reshape(2 * edge_total)

    weight = jnp.concatenate([w_first[:feature_width], w_first[feature_width:]], axis=1)
    bias = jnp.tile(b_first.reshape(parts, LANES), (8 // parts, 1))
    out_weight = jnp.tile(0.5 * w_second.astype(jnp.float32).reshape(parts, LANES), (8 // parts, 1))
    pair_here = (pair_index - node_self * PAIRS_ROW).reshape(1, edge_total)

    table = pltpu.VMEM((LEAD + row_total * parts + 8, LANES), jnp.float32)
    vmem = pl.BlockSpec(memory_space=pltpu.VMEM)
    scores, pooled = pl.pallas_call(
        functools.partial(scorer, edge_total, parts),
        out_shape=(
            jax.ShapeDtypeStruct((1, edge_total), jnp.float32),
            jax.ShapeDtypeStruct((PAIRS_ROW // LANES, LANES), jnp.float32),
        ),
        in_specs=[vmem, pl.BlockSpec(memory_space=pl.ANY), vmem, vmem, vmem, vmem],
        out_specs=(vmem, vmem),
        scratch_shapes=[
            table,
            table,
            pltpu.VMEM((edge_total * parts, LANES), jnp.float32),
            pltpu.SMEM((2 * edge_total,), jnp.int32),
            pltpu.SemaphoreType.DMA,
        ],
        compiler_params=pltpu.CompilerParams(vmem_limit_bytes=56 * 2**20),
    )(rows, offsets, pair_here, weight, bias, out_weight)
    edge_score = scores.reshape(edge_total)
    pair_cost = lax.psum_scatter(pooled.reshape(PAIRS_ROW), "edge", scatter_dimension=0, tiled=True)
    return (edge_score, pair_cost)


def solution(mesh):
    return jax.shard_map(
        body,
        mesh=mesh,
        in_specs=(
            P("node", None, None),
            P("edge", "node", None),
            P(None, ("node", "edge")),
            P(("node", "edge")),
            P(),
            P(),
            P(),
        ),
        out_specs=(P(("node", "edge")), P(("node", "edge"))),
        check_vma=False,
    )
```

time: 112 us -> 107 us (0.955)
  blocking collectives: 4.65 us -> 72.9 us
  waiting for transfers between devices: 42.5 us -> 0.01 us
  local copies, waits for them, and re-layouts: 26.2 us -> 5.61 us
  Pallas kernels: 0 us -> 13.3 us
  matrix products: 11.7 us -> 0 us
  other arithmetic: 11.5 us -> 5.02 us
  starting transfers between devices: 12.5 us -> 6.8 us
    all_gather x0 -> x1, blocking collectives: none -> 63.5 us  [body(): lists = lax.all_gather(wanted, 'node')]
    all_to_all x1, waiting for transfers between devices: 41.9 us -> 0.01 us  [body(): lax.all_to_all(picked, 'node', split_axis=0, concat_axis=0, tiled=True)]
    gather x4 -> x0, local copies, waits for them, and re-layouts: 20.3 us -> none  [tile_step(): end_rows = jnp.take(flat_rows, rows_at, axis=0)]
    pallas_call x0 -> x1, Pallas kernels: none -> 13.3 us  [body(): pl.pallas_call(functools.partial(scorer, edge_total, parts), out_shape=(j...]
    dot_general x16 -> x0, matrix products: 11.7 us -> none  [the longest x4 3.93 us: tile_step(): scores = jnp.dot(hidden, w_out, precision=lax.Precision.HIGHEST)]
    select_n x7 -> x1, other arithmetic: 8.76 us -> 0.08 us  [body(): source = target // blocks_here]
    all_to_all x1 -> x0, starting transfers between devices: 6.66 us -> none  [body(): lax.all_to_all(labels, 'node', split_axis=0, concat_axis=0, tiled=True)]
    unnamed x1, blocking collectives: 4.65 us -> 9.45 us
  transfers between devices with their start and end apart: 2 -> 1, of which waited for: 2 -> 0; matrix products, arithmetic and copies ran while one was open for 7% -> 5% of each run, Pallas kernels for 0% -> 0%
where the time goes in v1:
time: 107 us; the launch traced here: 105 us
  blocking collectives  72.9 us (68%)
  Pallas kernels  13.3 us (12%)
  starting transfers between devices  6.8 us (6%)
  local copies, waits for them, and re-layouts  5.61 us (5%)
  other arithmetic  5.02 us (5%)
  between operations  1.39 us (1%)
    all_gather x1, blocking collectives, body(): lists = lax.all_gather(wanted, 'node')  63.5 us
    pallas_call x1, Pallas kernels, body(): pl.pallas_call(functools.partial(scorer, edge_total, parts), out_shape=(j...  13.3 us
    unnamed x1, blocking collectives  9.45 us
    all_to_all x1, starting transfers between devices, body(): lax.all_to_all(picked, 'node', split_axis=0, concat_axis=0, tiled=True)  6.8 us
    select_n x2, other arithmetic, body(): picked = jnp.take(embedding, jnp.clip(wanted, 0, blocks_here - 1), axis=0)  2.34 us
  transfers between devices with their start and end apart: 1, of which 0 were waited for; matrix products, arithmetic and copies ran while one was open for 5% of the time, Pallas kernels for 0%

profile of v1, /device:TPU:9, one launch (start us, length us, event | category | flops | bytes accessed | tf_op | source)
XLA Modules:
  0.0 105.1 jit_solution(8817498260486023598)
XLA Ops:
  0.6 0.0 copy-start
  0.6 0.7 fusion.5
  1.4 0.7 compare_and_fusion
  2.1 0.0 copy-done
  2.1 0.7 gather_fusion
  2.8 1.6 %broadcast_select_fusion = bf16[16,128,512]{2,1,0:T(8,128)(2,1)} fusion(bf16[16,128,512]{2,1,0:T(8,128)(2,1)S(1)} %gather_fusion, pred[16]{0:T(512)(128)(4,1)S(1)} %compare_and_fusion), kind=kLoop, calls=%fused_computation.1 | loop fusion | flops 1048576 | bytes 4194320 | tf_op jit(solution)/shard_map/jit(_take)/select_n | solution.py:116
  4.4 0.0 copy-start.6
  4.4 0.0 copy-start.2
  4.4 0.0 copy-start.7
  4.4 6.8 %all-to-all-start = ((bf16[16,128,512]{2,1,0:T(8,128)(2,1)}), bf16[16,128,512]{2,1,0:T(8,128)(2,1)S(1)}, u32[]{:S(2)}, u32[]{:S(2)}) async-start(bf16[16,128,512]{2,1,0:T(8,128)(2,1)} %broadcast_select_fusion), calls=%async_computation | async-start | bytes 4194304 | tf_op jit(solution)/shard_map/all_to_all | solution.py:117
  11.2 0.0 copy-done.6
  11.2 63.5 %all-gather = s32[16,1,16]{2,1,0:T(1,128)S(1)} all-gather(s32[1,1,16]{2,1,0:T(1,128)S(1)} %copy-done.6), channel_id=2, replica_groups=mesh['node'=16,'edge'=2] {'node'}, dimensions={0}, use_global_device_ids=true | all-gather | bytes 1088 | tf_op jit(solution)/shard_map/all_gather | solution.py:120
  74.6 0.4 dynamic-slice_reduce_fusion
  75.1 0.0 copy-done.2
  75.1 0.1 and_select_fusion.2
  75.2 0.1 select_reduce_fusion
  75.3 0.1 subtract_bitcast_fusion
  75.4 0.6 copy.9
  76.0 0.0 copy-done.7
  76.0 0.6 dynamic-slice.1
  77.2 0.0 copy-start.5
  77.2 0.0 copy-start.3
  77.2 0.0 copy-start.4
  77.3 1.3 %fusion.6 = (bf16[512,512]{1,0:T(8,128)(2,1)S(1)}, bf16[512,512]{1,0:T(8,128)(2,1)S(1)}) fusion(bf16[1024,512]{1,0:T(8,128)(2,1)} %param.11), kind=kLoop, calls=%fused_computation.36 | loop fusion | bytes 2097152 | tf_op jit(solution)/shard_map/slice | solution.py:130
  78.5 1.1 %pad_maximum_fusion.weight_ref = bf16[512,1024]{1,0:T(8,128)(2,1)} fusion(bf16[512,512]{1,0:T(8,128)(2,1)S(1)} %get-tuple-element.9, bf16[512,512]{1,0:T(8,128)(2,1)S(1)} %get-tuple-element.8), kind=kLoop, calls=%fused_computation.2 | loop fusion | flops 2097152 | bytes 2097152 | tf_op jit(solution)/shard_map/concatenate | solution.py:130
  79.7 0.0 copy-done.5
  79.7 0.0 copy-done.3
  79.7 0.6 broadcast_subtract_fusion
  80.3 0.0 all-to-all-done
  80.3 0.0 copy-start.1
  80.3 0.0 copy-done.4
  80.3 0.6 tile.20
  80.9 0.7 tile.22
  81.6 0.0 copy-done.1
  81.6 13.3 %shard_map.86 = (f32[1,2048]{1,0:T(1,128)}, f32[8,128]{1,0:T(8,128)}) custom-call(bf16[2048,512]{1,0:T(8,128)(2,1)} %bitcast.19, s32[4096]{0:T(1024)} %bitcast.20, s32[1,2048]{1,0:T(1,128)} %bitcast.21, bf16[512,1024]{1,0:T(8,128)(2,1)} %pad_maximum_fusion.weight_ref, f32[8,128]{1,0:T(8,128)} %bitcast.22, f32[8,128]{1,0:T(8,128)} %bitcast.23), custom_call_target="tpu_custom_call" | custom-call | tf_op jit(solution)/shard_map/pallas_call | solution.py:137
  95.0 9.5 %all-reduce = f32[1024]{0:T(1024)S(1)} all-reduce(f32[1024]{0:T(1024)} %bitcast.24), channel_id=3, replica_groups=mesh['node'=16,'edge'=2] {'edge'}, use_global_device_ids=true, to_apply=%region_1.2.clone | all-reduce | flops 1024 | bytes 8192
  104.4 0.7 dynamic-slice.2
  (3 shorter events, 0.0 us)
Async XLA Ops:
  0.6 1.4 %copy-start = (bf16[8,128,512]{2,1,0:T(8,128)(2,1)S(1)}, bf16[8,128,512]{2,1,0:T(8,128)(2,1)}, u32[]{:S(2)}) copy-start(bf16[8,128,512]{2,1,0:T(8,128)(2,1)} %param.7) | copy-start | bytes 3145732
  4.4 6.8 %copy-start.6 = (s32[1,1,16]{2,1,0:T(1,128)S(1)}, s32[1,1,16]{2,1,0:T(1,128)}, u32[]{:S(2)}) copy-start(s32[1,1,16]{2,1,0:T(1,128)} %param.8) | copy-start | bytes 196
  4.4 70.7 %copy-start.2 = (s32[2,2048]{1,0:T(2,128)S(1)}, s32[2,2048]{1,0:T(2,128)}, u32[]{:S(2)}) copy-start(s32[2,2048]{1,0:T(2,128)} %param.9) | copy-start | bytes 49156
  4.4 71.6 %copy-start.7 = (u32[32]{0:T(128)S(1)}, u32[32]{0:T(128)}, u32[]{:S(2)}) copy-start(u32[32]{0:T(128)} %constant.103) | copy-start | bytes 388
  4.4 75.9 %all-to-all-start = ((bf16[16,128,512]{2,1,0:T(8,128)(2,1)}), bf16[16,128,512]{2,1,0:T(8,128)(2,1)S(1)}, u32[]{:S(2)}, u32[]{:S(2)}) async-start(bf16[16,128,512]{2,1,0:T(8,128)(2,1)} %broadcast_select_fusion), calls=%async_computation | async-start | bytes 4194304 | tf_op jit(solution)/shard_map/all_to_all | solution.py:117
  77.2 2.4 %copy-start.5 = (bf16[512]{0:T(512)(128)(2,1)S(1)}, bf16[512]{0:T(512)(128)(2,1)}, u32[]{:S(2)}) copy-start(bf16[512]{0:T(512)(128)(2,1)} %param.13) | copy-start | bytes 3076
  77.2 2.4 %copy-start.3 = (s32[2048]{0:T(1024)S(1)}, s32[2048]{0:T(1024)}, u32[]{:S(2)}) copy-start(s32[2048]{0:T(1024)} %param.10) | copy-start | bytes 24580
  77.2 3.0 %copy-start.4 = (f32[512]{0:T(512)S(1)}, f32[512]{0:T(512)}, u32[]{:S(2)}) copy-start(f32[512]{0:T(512)} %param.12) | copy-start | bytes 6148
  80.3 1.3 %copy-start.1 = (bf16[16,128,512]{2,1,0:T(8,128)(2,1)}, bf16[16,128,512]{2,1,0:T(8,128)(2,1)S(1)}, u32[]{:S(2)}) copy-start(bf16[16,128,512]{2,1,0:T(8,128)(2,1)S(1)} %all-to-all-done) | copy-start | bytes 6291460

commit v2 on v1

v2 whole, which is shorter than its diff:
```python
import functools

import jax
import jax.numpy as jnp
from jax import lax
from jax.experimental import pallas as pl
from jax.experimental.pallas import tpu as pltpu
from jax.sharding import PartitionSpec as P

PAIRS_ROW = 1024
LANES = 128
LEAD = 8
LABEL_ROWS = 8
GELU_A = 0.7978845608028654
GELU_B = GELU_A * 0.044715


def bits(power_of_two):
    return power_of_two.bit_length() - 1


def pick(wanted_ref, embedding_ref, sent_ref, labels, block_sem, label_sem):
    node_count = sent_ref.shape[0]
    blocks_here, block_rows, feature_width = embedding_ref.shape
    groups = feature_width // LANES
    body_rows = groups * block_rows

    def start(node, carry):
        wanted = wanted_ref[0, 0, node]
        block = jnp.clip(wanted, 0, blocks_here - 1)
        for group in range(groups):
            pltpu.make_async_copy(
                embedding_ref.at[block, :, pl.ds(group * LANES, LANES)],
                sent_ref.at[node, pl.ds(group * block_rows, block_rows), :],
                block_sem,
            ).start()
        labels[node] = jnp.full((LABEL_ROWS, LANES), wanted.astype(jnp.float32)).astype(jnp.bfloat16)
        return carry

    lax.fori_loop(0, node_count, start, 0, unroll=4)
    label_copy = pltpu.make_async_copy(labels, sent_ref.at[:, pl.ds(body_rows, LABEL_ROWS), :], label_sem)
    label_copy.start()
    everything = sent_ref.at[:, pl.ds(0, body_rows), :]
    pltpu.make_async_copy(everything, everything, block_sem).wait()
    label_copy.wait()


def three_terms(x):
    high = x.astype(jnp.bfloat16)
    rest = x - high.astype(jnp.float32)
    middle = rest.astype(jnp.bfloat16)
    low = (rest - middle.astype(jnp.float32)).astype(jnp.bfloat16)
    return high, middle, low


def scorer(
    blocks_here,
    arrived_hbm,
    ends_hbm,
    pair_hbm,
    weight_hbm,
    bias_hbm,
    out_weight_hbm,
    score_ref,
    pooled_ref,
    arrived,
    labels,
    ends,
    pair_ref,
    weight,
    bias_ref,
    out_weight_ref,
    first_table,
    second_table,
    terms,
    offsets_near,
    offsets,
    chunk_sems,
    sems,
):
    node_count = arrived.shape[0]
    feature_width, hidden_width = weight.shape[1:]
    groups = feature_width // LANES
    block_rows = arrived.shape[1] // groups
    body_rows = groups * block_rows
    edge_total = ends.shape[1]
    parts = hidden_width // LANES
    row_total = node_count * block_rows
    chunk_blocks = 2
    chunk_count = node_count // chunk_blocks
    chunk_rows = chunk_blocks * block_rows

    def chunk_copy(chunk):
        at = pl.ds(chunk * chunk_blocks, chunk_blocks)
        return pltpu.make_async_copy(
            arrived_hbm.at[at, pl.ds(0, body_rows), :], arrived.at[at], chunk_sems.at[chunk]
        )

    label_copy = pltpu.make_async_copy(arrived_hbm.at[:, pl.ds(body_rows, LABEL_ROWS), :], labels, sems.at[0])
    ends_copy = pltpu.make_async_copy(ends_hbm, ends, sems.at[1])
    weight_copies = [pltpu.make_async_copy(weight_hbm.at[end], weight.at[end], sems.at[2 + end]) for end in range(2)]
    bias_copies = [
        pltpu.make_async_copy(bias_hbm, bias_ref.at[pl.ds(half * parts, parts)], sems.at[4 + half]) for half in range(2)
    ]
    out_weight_copies = [
        pltpu.make_async_copy(out_weight_hbm, out_weight_ref.at[pl.ds(half * parts, parts)], sems.at[6 + half])
        for half in range(2)
    ]
    pair_copy = pltpu.make_async_copy(pair_hbm, pair_ref, sems.at[8])
    offsets_copy = pltpu.make_async_copy(offsets_near, offsets, sems.at[9])

    label_copy.start()
    ends_copy.start()
    weight_copies[0].start()
    for copy in bias_copies:
        copy.start()

    def start_chunk(chunk, carry):
        chunk_copy(chunk).start()
        return carry

    lax.fori_loop(0, chunk_count, start_chunk, 0, unroll=True)
    weight_copies[1].start()
    for copy in out_weight_copies:
        copy.start()
    pair_copy.start()

    label_copy.wait()
    ends_copy.wait()
    ids = ends[...]
    target = ids >> bits(block_rows)
    source = target >> bits(blocks_here)

    def look_up(node, delivered):
        label = labels[node].astype(jnp.float32)[:2].astype(jnp.int32)
        label = jnp.concatenate([label] * (edge_total // LANES), axis=1)
        return jnp.where(source == node, label, delivered)

    delivered = lax.fori_loop(0, node_count, look_up, jnp.full(ids.shape, -1, jnp.int32), unroll=8)
    row = (source << bits(block_rows)) + (ids & (block_rows - 1))
    row = jnp.where(delivered == (target & (blocks_here - 1)), row, row_total)
    second_of_two = lax.broadcasted_iota(jnp.int32, ids.shape, 1) & 1
    offsets_near[...] = LEAD + (row - second_of_two) * parts
    offsets_copy.start()

    for copy in bias_copies:
        copy.wait()
    bias = bias_ref[...]
    absent = pl.ds(LEAD + row_total * parts, 8)
    first_table[absent, :] = bias
    second_table[absent, :] = jnp.zeros((8, LANES), jnp.float32)

    def shares_of(chunk, end):
        blocks = [arrived[chunk * chunk_blocks + block] for block in range(chunk_blocks)]
        rows = jnp.concatenate(
            [
                jnp.concatenate([block[group * block_rows : (group + 1) * block_rows] for group in range(groups)], axis=1)
                for block in blocks
            ],
            axis=0,
        )
        return jnp.dot(rows, weight[end], preferred_element_type=jnp.float32)

    def spread(chunk, part):
        return pl.ds(LEAD + chunk * (chunk_rows * parts) + part, chunk_rows, stride=parts)

    weight_copies[0].wait()

    def project_first(chunk, carry):
        chunk_copy(chunk).wait()
        shares = shares_of(chunk, 0)
        for part in range(parts):
            first_table[spread(chunk, part), :] = (
                shares[:, part * LANES : (part + 1) * LANES] + bias[part : part + 1, :]
            )
        return carry

    lax.fori_loop(0, chunk_count, project_first, 0)
    weight_copies[1].wait()
    offsets_copy.wait()

    early = lax.broadcasted_iota(jnp.int32, (8, LANES), 0) < parts

    def two_rows(table, end, edge):
        return jnp.where(
            early, table[pl.ds(offsets[end, edge], 8), :], table[pl.ds(offsets[end, edge + 1], 8), :]
        )

    def terms_at(edge):
        return pl.ds(pl.multiple_of(edge * parts, 8), 8)

    group_edges = edge_total // chunk_count

    def project_second(chunk, carry):
        shares = shares_of(chunk, 1)
        for part in range(parts):
            second_table[spread(chunk, part), :] = shares[:, part * LANES : (part + 1) * LANES]
        for pair in range(group_edges // 2):
            edge = chunk * group_edges + 2 * pair
            terms[terms_at(edge), :] = two_rows(first_table, 0, edge)
        return carry

    lax.fori_loop(0, chunk_count, project_second, 0)

    for copy in out_weight_copies:
        copy.wait()
    out_weight = 0.5 * out_weight_ref[...]
    score_edges = 128

    def score_group(step, carry):
        for pair in range(score_edges // 2):
            edge = step * score_edges + 2 * pair
            x = terms[terms_at(edge), :] + two_rows(second_table, 1, edge)
            weighted = x * out_weight
            terms[terms_at(edge), :] = weighted + weighted * jnp.tanh(x * (GELU_A + GELU_B * (x * x)))
        return carry

    lax.fori_loop(0, edge_total // score_edges, score_group, 0)

    sums = terms[pl.ds(0, edge_total, stride=parts), :]
    for part in range(1, parts):
        sums = sums + terms[pl.ds(part, edge_total, stride=parts), :]
    scores = lax.dot_general(
        jnp.ones((8, 3 * LANES), jnp.bfloat16),
        jnp.concatenate(three_terms(sums), axis=1),
        (((1,), (1,)), ((), ())),
        preferred_element_type=jnp.float32,
    )
    score_ref[...] = scores[0:1, :]

    pair_copy.wait()
    pair = pair_ref[...] & (PAIRS_ROW - 1)
    pair_rows = PAIRS_ROW // LANES
    high = lax.broadcasted_iota(jnp.int32, (pair_rows, edge_total), 0) == (pair >> bits(LANES))
    low = lax.broadcasted_iota(jnp.int32, (LANES, edge_total), 0) == (pair & (LANES - 1))
    placed = jnp.concatenate(
        [term.astype(jnp.float32) for term in three_terms(jnp.where(high, scores[:pair_rows], 0.0))], axis=0
    )
    pooled = lax.dot_general(
        placed.astype(jnp.bfloat16),
        low.astype(jnp.float32).astype(jnp.bfloat16),
        (((1,), (1,)), ((), ())),
        preferred_element_type=jnp.float32,
    )
    pooled_ref[...] = pooled[:pair_rows] + pooled[pair_rows : 2 * pair_rows] + pooled[2 * pair_rows :]


def body(embedding, send_list, edge_ends, pair_index, w_first, b_first, w_second):
    node_count = lax.axis_size("node")
    blocks_here, block_rows, feature_width = embedding.shape
    hidden_width = w_first.shape[1]
    parts = hidden_width // LANES
    body_rows = feature_width // LANES * block_rows
    edge_total = edge_ends.shape[1]
    table_rows = LEAD + node_count * block_rows * parts + 8
    anywhere = pl.BlockSpec(memory_space=pl.ANY)
    vmem = pl.BlockSpec(memory_space=pltpu.VMEM)

    sent = pl.pallas_call(
        pick,
        out_shape=jax.ShapeDtypeStruct((node_count, body_rows + LABEL_ROWS, LANES), jnp.bfloat16),
        in_specs=[pl.BlockSpec(memory_space=pltpu.SMEM), vmem],
        out_specs=anywhere,
        scratch_shapes=[
            pltpu.VMEM((node_count, LABEL_ROWS, LANES), jnp.bfloat16),
            pltpu.SemaphoreType.DMA,
            pltpu.SemaphoreType.DMA,
        ],
    )(send_list, embedding)
    arrived = lax.all_to_all(sent, "node", split_axis=0, concat_axis=0, tiled=True)

    scores, pooled = pl.pallas_call(
        functools.partial(scorer, blocks_here),
        out_shape=(
            jax.ShapeDtypeStruct((1, edge_total), jnp.float32),
            jax.ShapeDtypeStruct((PAIRS_ROW // LANES, LANES), jnp.float32),
        ),
        in_specs=[anywhere] * 6,
        out_specs=(vmem, vmem),
        scratch_shapes=[
            pltpu.VMEM((node_count, body_rows, LANES), jnp.bfloat16),
            pltpu.VMEM((node_count, LABEL_ROWS, LANES), jnp.bfloat16),
            pltpu.VMEM((2, edge_total), jnp.int32),
            pltpu.VMEM((1, edge_total), jnp.int32),
            pltpu.VMEM((2, feature_width, hidden_width), jnp.bfloat16),
            pltpu.VMEM((2 * parts, LANES), jnp.float32),
            pltpu.VMEM((2 * parts, LANES), jnp.float32),
            pltpu.VMEM((table_rows, LANES), jnp.float32),
            pltpu.VMEM((table_rows, LANES), jnp.float32),
            pltpu.VMEM((edge_total * parts, LANES), jnp.float32),
            pltpu.VMEM((2, edge_total), jnp.int32),
            pltpu.SMEM((2, edge_total), jnp.int32),
            pltpu.SemaphoreType.DMA((node_count // 2,)),
            pltpu.SemaphoreType.DMA((10,)),
        ],
        compiler_params=pltpu.CompilerParams(vmem_limit_bytes=56 * 2**20),
    )(
        arrived,
        edge_ends,
        pair_index.reshape(1, edge_total),
        w_first.reshape(2, feature_width, hidden_width),
        b_first.reshape(parts, LANES),
        w_second.astype(jnp.float32).reshape(parts, LANES),
    )
    edge_score = scores.reshape(edge_total)
    pooled = pooled.reshape(PAIRS_ROW)
    if lax.axis_size("edge") == 2:
        mine = PAIRS_ROW // 2
        whole = pooled + lax.ppermute(pooled, "edge", [(0, 1), (1, 0)])
        pair_cost = lax.dynamic_slice(whole, (lax.axis_index("edge") * mine,), (mine,))
    else:
        pair_cost = lax.psum_scatter(pooled, "edge", scatter_dimension=0, tiled=True)
    return (edge_score, pair_cost)


def solution(mesh):
    return jax.shard_map(
        body,
        mesh=mesh,
        in_specs=(
            P("node", None, None),
            P("edge", "node", None),
            P(None, ("node", "edge")),
            P(("node", "edge")),
            P(),
            P(),
            P(),
        ),
        out_specs=(P(("node", "edge")), P(("node", "edge"))),
        check_vma=False,
    )
```

time: 107 us -> 80.1 us (0.75)
  blocking collectives: 72.9 us -> 0 us
  waiting for transfers between devices: 0.01 us -> 47.1 us
  Pallas kernels: 13.3 us -> 18.7 us
  other arithmetic: 5.02 us -> 1.26 us
  local copies, waits for them, and re-layouts: 5.61 us -> 2.02 us
  starting transfers between devices: 6.8 us -> 9.25 us
    all_gather x1 -> x0, blocking collectives: 63.5 us -> none  [body(): lists = lax.all_gather(wanted, 'node')]
    all_to_all x1, waiting for transfers between devices: 0.01 us -> 46.1 us  [body(): lax.all_to_all(sent, 'node', split_axis=0, concat_axis=0, tiled=True)]
    unnamed x1 -> x0, blocking collectives: 9.45 us -> none
    pallas_call x1 -> x2, Pallas kernels: 13.3 us -> 18.7 us  [the longest x1 16.1 us: body(): pl.pallas_call(functools.partial(scorer, blocks_here), out_shape=(jax.Sha...]
    ppermute x0 -> x1, starting transfers between devices: none -> 2.57 us  [body(): whole = pooled + lax.ppermute(pooled, 'edge', [(0, 1), (1, 0)])]
    select_n x3 -> x0, other arithmetic: 2.42 us -> none  [the longest x2 2.34 us: body(): picked = jnp.take(embedding, jnp.clip(wanted, 0, blocks_here - 1), axis=0)]
    another operation x2 -> x0, local copies, waits for them, and re-layouts: 1.29 us -> none  [the longest x1 0.67 us: body(): jnp.tile(0.5 * w_second.astype(jnp.float32).reshape(parts, LANES), (8 //...]
    slice x1 -> x0, local copies, waits for them, and re-layouts: 1.28 us -> none  [body(): w_first[:feature_width]]
  transfers between devices with their start and end apart: 1 -> 2, of which waited for: 0 -> 2; matrix products, arithmetic and copies ran while one was open for 5% -> 1% of each run, Pallas kernels for 0% -> 0%
where the time goes in v2:
time: 80.1 us; the launch traced here: 79 us
  waiting for transfers between devices  47.1 us (59%)
  Pallas kernels  18.7 us (23%)
  starting transfers between devices  9.25 us (12%)
  local copies, waits for them, and re-layouts  2.02 us (3%)
  other arithmetic  1.26 us (2%)
    all_to_all x1, waiting for transfers between devices, body(): lax.all_to_all(sent, 'node', split_axis=0, concat_axis=0, tiled=True)  46.1 us
    pallas_call x1, Pallas kernels, body(): pl.pallas_call(functools.partial(scorer, blocks_here), out_shape=(jax.Sha...  16.1 us
    all_to_all x1, starting transfers between devices, body(): lax.all_to_all(sent, 'node', split_axis=0, concat_axis=0, tiled=True)  6.68 us
    pallas_call x1, Pallas kernels, body(): pl.pallas_call(pick, out_shape=jax.ShapeDtypeStruct((node_count, body_row...  2.62 us
    ppermute x1, starting transfers between devices, body(): whole = pooled + lax.ppermute(pooled, 'edge', [(0, 1), (1, 0)])  2.57 us
  transfers between devices with their start and end apart: 2, of which 2 were waited for; matrix products, arithmetic and copies ran while one was open for 1% of the time, Pallas kernels for 0%

profile of v2, /device:TPU:9, one launch (start us, length us, event | category | flops | bytes accessed | tf_op | source)
XLA Modules:
  0.0 79.0 jit_solution(13766613193009779765)
XLA Ops:
  0.6 2.6 %shard_map.86 = bf16[16,520,128]{2,1,0:T(8,128)(2,1)} custom-call(s32[1,1,16]{2,1,0:T(1,128)} %wanted_ref.1, bf16[8,128,512]{2,1,0:T(8,128)(2,1)} %embedding_ref.1), custom_call_target="tpu_custom_call" | custom-call | tf_op jit(solution)/shard_map/pallas_call | solution.py:259
  3.3 0.0 copy-start.1
  3.3 6.7 %all-to-all-start = ((bf16[16,520,128]{2,1,0:T(8,128)(2,1)}), bf16[16,520,128]{2,1,0:T(8,128)(2,1)S(1)}, u32[]{:S(2)}, u32[]{:S(2)}) async-start(bf16[16,520,128]{2,1,0:T(8,128)(2,1)} %shard_map.86), calls=%async_computation | async-start | bytes 4259840 | tf_op jit(solution)/shard_map/all_to_all | solution.py:270
  9.9 0.0 copy-done.1
  9.9 0.6 bitcast_convert_fusion.out_weight_hbm
  10.5 46.1 %all-to-all-done.arrived_hbm = bf16[16,520,128]{2,1,0:T(8,128)(2,1)S(1)} async-done(((bf16[16,520,128]{2,1,0:T(8,128)(2,1)}), bf16[16,520,128]{2,1,0:T(8,128)(2,1)S(1)}, u32[]{:S(2)}, u32[]{:S(2)}) %all-to-all-start) | async-done | bytes 2129952 | tf_op jit(solution)/shard_map/all_to_all | solution.py:270
  56.6 0.0 copy-start
  56.6 1.4 %copy-done = bf16[16,520,128]{2,1,0:T(8,128)(2,1)} copy-done((bf16[16,520,128]{2,1,0:T(8,128)(2,1)}, bf16[16,520,128]{2,1,0:T(8,128)(2,1)S(1)}, u32[]{:S(2)}) %copy-start) | copy-done | bytes 2129944
  58.0 16.1 %shard_map.87 = (f32[1,2048]{1,0:T(1,128)}, f32[8,128]{1,0:T(8,128)}) custom-call(bf16[16,520,128]{2,1,0:T(8,128)(2,1)} %copy-done, s32[2,2048]{1,0:T(2,128)} %ends_hbm.1, s32[1,2048]{1,0:T(1,128)} %bitcast.10, bf16[2,512,512]{2,1,0:T(8,128)(2,1)} %bitcast.9, f32[4,128]{1,0:T(4,128)} %bitcast.12, f32[4,128]{1,0:T(4,128)} %bitcast_convert_fusion.out_weight_hbm), custom_call_target="tpu_custom_call" | custom-call | tf_op jit(solution)/shard_map/pallas_call | solution.py:272
  74.0 2.6 %collective-permute-start = (f32[1024]{0:T(1024)}, f32[1024]{0:T(1024)S(1)}, u32[]{:S(2)}, u32[]{:S(2)}) collective-permute-start(f32[1024]{0:T(1024)} %bitcast.11), channel_id=1, source_target_pairs={{0,1},{1,0},{2,3},{3,2},{4,5},{5,4},{6,7},{7,6},{8,9},{9,8},{10,11... | collective-permute-start | bytes 12296 | tf_op jit(solution)/shard_map/ppermute | solution.py:309
  76.6 1.0 %collective-permute-done = f32[1024]{0:T(1024)S(1)} collective-permute-done((f32[1024]{0:T(1024)}, f32[1024]{0:T(1024)S(1)}, u32[]{:S(2)}, u32[]{:S(2)}) %collective-permute-start) | collective-permute-done | bytes 4128 | tf_op jit(solution)/shard_map/ppermute | solution.py:309
  77.6 0.7 bitcast_add_fusion
  78.3 0.7 dynamic_slice.3
Async XLA Ops:
  3.3 6.7 %copy-start.1 = (bf16[512]{0:T(512)(128)(2,1)S(1)}, bf16[512]{0:T(512)(128)(2,1)}, u32[]{:S(2)}) copy-start(bf16[512]{0:T(512)(128)(2,1)} %param.13) | copy-start | bytes 3076
  3.3 53.3 %all-to-all-start = ((bf16[16,520,128]{2,1,0:T(8,128)(2,1)}), bf16[16,520,128]{2,1,0:T(8,128)(2,1)S(1)}, u32[]{:S(2)}, u32[]{:S(2)}) async-start(bf16[16,520,128]{2,1,0:T(8,128)(2,1)} %shard_map.86), calls=%async_computation | async-start | bytes 4259840 | tf_op jit(solution)/shard_map/all_to_all | solution.py:270
  56.6 1.4 %copy-start = (bf16[16,520,128]{2,1,0:T(8,128)(2,1)}, bf16[16,520,128]{2,1,0:T(8,128)(2,1)S(1)}, u32[]{:S(2)}) copy-start(bf16[16,520,128]{2,1,0:T(8,128)(2,1)S(1)} %all-to-all-done.arrived_hbm) | copy-start | bytes 6389764
  74.0 3.6 %collective-permute-start = (f32[1024]{0:T(1024)}, f32[1024]{0:T(1024)S(1)}, u32[]{:S(2)}, u32[]{:S(2)}) collective-permute-start(f32[1024]{0:T(1024)} %bitcast.11), channel_id=1, source_target_pairs={{0,1},{1,0},{2,3},{3,2},{4,5},{5,4},{6,7},{7,6},{8,9},{9,8},{10,11... | collective-permute-start | bytes 12296 | tf_op jit(solution)/shard_map/ppermute | solution.py:309

commit v3 on v2

--- a/solution.py
+++ b/solution.py
@@ -11,6 +11,7 @@
 LANES = 128
 LEAD = 8
 LABEL_ROWS = 8
+CHUNK_BLOCKS = 8
 GELU_A = 0.7978845608028654
 GELU_B = GELU_A * 0.044715
 
@@ -55,6 +56,7 @@
 
 def scorer(
     blocks_here,
+    paired,
     arrived_hbm,
     ends_hbm,
     pair_hbm,
@@ -62,7 +64,8 @@
     bias_hbm,
     out_weight_hbm,
     score_ref,
-    pooled_ref,
+    mine_ref,
+    other_ref,
     arrived,
     labels,
     ends,
@@ -86,12 +89,11 @@
     edge_total = ends.shape[1]
     parts = hidden_width // LANES
     row_total = node_count * block_rows
-    chunk_blocks = 2
-    chunk_count = node_count // chunk_blocks
-    chunk_rows = chunk_blocks * block_rows
+    chunk_count = node_count // CHUNK_BLOCKS
+    chunk_rows = CHUNK_BLOCKS * block_rows
 
     def chunk_copy(chunk):
-        at = pl.ds(chunk * chunk_blocks, chunk_blocks)
+        at = pl.ds(chunk * CHUNK_BLOCKS, CHUNK_BLOCKS)
         return pltpu.make_async_copy(
             arrived_hbm.at[at, pl.ds(0, body_rows), :], arrived.at[at], chunk_sems.at[chunk]
         )
@@ -107,7 +109,7 @@
         for half in range(2)
     ]
     pair_copy = pltpu.make_async_copy(pair_hbm, pair_ref, sems.at[8])
-    offsets_copy = pltpu.make_async_copy(offsets_near, offsets, sems.at[9])
+    offsets_copies = [pltpu.make_async_copy(offsets_near.at[end], offsets.at[pl.ds(end * edge_total, edge_total)], sems.at[9 + end]) for end in range(2)]
 
     label_copy.start()
     ends_copy.start()
@@ -141,7 +143,8 @@
     row = jnp.where(delivered == (target & (blocks_here - 1)), row, row_total)
     second_of_two = lax.broadcasted_iota(jnp.int32, ids.shape, 1) & 1
     offsets_near[...] = LEAD + (row - second_of_two) * parts
-    offsets_copy.start()
+    for copy in offsets_copies:
+        copy.start()
 
     for copy in bias_copies:
         copy.wait()
@@ -150,8 +153,12 @@
     first_table[absent, :] = bias
     second_table[absent, :] = jnp.zeros((8, LANES), jnp.float32)
 
-    def shares_of(chunk, end):
-        blocks = [arrived[chunk * chunk_blocks + block] for block in range(chunk_blocks)]
+    for copy in weight_copies:
+        copy.wait()
+
+    def project(chunk, carry):
+        chunk_copy(chunk).wait()
+        blocks = [arrived[chunk * CHUNK_BLOCKS + block] for block in range(CHUNK_BLOCKS)]
         rows = jnp.concatenate(
             [
                 jnp.concatenate([block[group * block_rows : (group + 1) * block_rows] for group in range(groups)], axis=1)
@@ -159,48 +166,27 @@
             ],
             axis=0,
         )
-        return jnp.dot(rows, weight[end], preferred_element_type=jnp.float32)
-
-    def spread(chunk, part):
-        return pl.ds(LEAD + chunk * (chunk_rows * parts) + part, chunk_rows, stride=parts)
-
-    weight_copies[0].wait()
-
-    def project_first(chunk, carry):
-        chunk_copy(chunk).wait()
-        shares = shares_of(chunk, 0)
-        for part in range(parts):
-            first_table[spread(chunk, part), :] = (
-                shares[:, part * LANES : (part + 1) * LANES] + bias[part : part + 1, :]
-            )
+        for end, table in enumerate((first_table, second_table)):
+            shares = jnp.dot(rows, weight[end], preferred_element_type=jnp.float32)
+            for part in range(parts):
+                share = shares[:, part * LANES : (part + 1) * LANES]
+                at = pl.ds(LEAD + chunk * (chunk_rows * parts) + part, chunk_rows, stride=parts)
+                table[at, :] = share + bias[part : part + 1, :] if end == 0 else share
         return carry
 
-    lax.fori_loop(0, chunk_count, project_first, 0)
-    weight_copies[1].wait()
-    offsets_copy.wait()
+    lax.fori_loop(0, chunk_count, project, 0)
+    for copy in offsets_copies:
+        copy.wait()
 
     early = lax.broadcasted_iota(jnp.int32, (8, LANES), 0) < parts
 
     def two_rows(table, end, edge):
         return jnp.where(
-            early, table[pl.ds(offsets[end, edge], 8), :], table[pl.ds(offsets[end, edge + 1], 8), :]
+            early, table[pl.ds(offsets[end * edge_total + edge], 8), :], table[pl.ds(offsets[end * edge_total + edge + 1], 8), :]
         )
 
     def terms_at(edge):
         return pl.ds(pl.multiple_of(edge * parts, 8), 8)
-
-    group_edges = edge_total // chunk_count
-
-    def project_second(chunk, carry):
-        shares = shares_of(chunk, 1)
-        for part in range(parts):
-            second_table[spread(chunk, part), :] = shares[:, part * LANES : (part + 1) * LANES]
-        for pair in range(group_edges // 2):
-            edge = chunk * group_edges + 2 * pair
-            terms[terms_at(edge), :] = two_rows(first_table, 0, edge)
-        return carry
-
-    lax.fori_loop(0, chunk_count, project_second, 0)
 
     for copy in out_weight_copies:
         copy.wait()
@@ -210,7 +196,7 @@
     def score_group(step, carry):
         for pair in range(score_edges // 2):
             edge = step * score_edges + 2 * pair
-            x = terms[terms_at(edge), :] + two_rows(second_table, 1, edge)
+            x = two_rows(first_table, 0, edge) + two_rows(second_table, 1, edge)
             weighted = x * out_weight
             terms[terms_at(edge), :] = weighted + weighted * jnp.tanh(x * (GELU_A + GELU_B * (x * x)))
         return carry
@@ -242,7 +228,52 @@
         (((1,), (1,)), ((), ())),
         preferred_element_type=jnp.float32,
     )
-    pooled_ref[...] = pooled[:pair_rows] + pooled[pair_rows : 2 * pair_rows] + pooled[2 * pair_rows :]
+    pooled = pooled[:pair_rows] + pooled[pair_rows : 2 * pair_rows] + pooled[2 * pair_rows :]
+    half = pair_rows // 2
+    low_is_mine = True if not paired else lax.axis_index("edge") == 0
+    mine_ref[...] = jnp.where(low_is_mine, pooled[:half], pooled[half:])
+    other_ref[...] = jnp.where(low_is_mine, pooled[half:], pooled[:half])
+
+
+def call_scorer(blocks_here, paired, arrived, ends, pair, weight, bias, out_weight):
+    node_count = arrived.shape[0]
+    feature_width, hidden_width = weight.shape[1:]
+    parts = hidden_width // LANES
+    body_rows = arrived.shape[1] - LABEL_ROWS
+    block_rows = body_rows * LANES // feature_width
+    edge_total = ends.shape[1]
+    table_rows = LEAD + node_count * block_rows * parts + 8
+    needed = (2 * table_rows + edge_total * parts) * LANES * 4
+    needed += 2 * (node_count * body_rows * LANES + 2 * feature_width * hidden_width)
+    anywhere = pl.BlockSpec(memory_space=pl.ANY)
+    vmem = pl.BlockSpec(memory_space=pltpu.VMEM)
+    return pl.pallas_call(
+        functools.partial(scorer, blocks_here, paired),
+        out_shape=(
+            jax.ShapeDtypeStruct((1, edge_total), jnp.float32),
+            jax.ShapeDtypeStruct((PAIRS_ROW // LANES // 2, LANES), jnp.float32),
+            jax.ShapeDtypeStruct((PAIRS_ROW // LANES // 2, LANES), jnp.float32),
+        ),
+        in_specs=[anywhere] * 6,
+        out_specs=(vmem, vmem, vmem),
+        scratch_shapes=[
+            pltpu.VMEM((node_count, body_rows, LANES), jnp.bfloat16),
+            pltpu.VMEM((node_count, LABEL_ROWS, LANES), jnp.bfloat16),
+            pltpu.VMEM((2, edge_total), jnp.int32),
+            pltpu.VMEM((1, edge_total), jnp.int32),
+            pltpu.VMEM((2, feature_width, hidden_width), jnp.bfloat16),
+            pltpu.VMEM((2 * parts, LANES), jnp.float32),
+            pltpu.VMEM((2 * parts, LANES), jnp.float32),
+            pltpu.VMEM((table_rows, LANES), jnp.float32),
+            pltpu.VMEM((table_rows, LANES), jnp.float32),
+            pltpu.VMEM((edge_total * parts, LANES), jnp.float32),
+            pltpu.VMEM((2, edge_total), jnp.int32),
+            pltpu.SMEM((2 * edge_total,), jnp.int32),
+            pltpu.SemaphoreType.DMA((node_count // CHUNK_BLOCKS,)),
+            pltpu.SemaphoreType.DMA((11,)),
+        ],
+        compiler_params=pltpu.CompilerParams(vmem_limit_bytes=needed + 6 * 2**20),
+    )(arrived, ends, pair, weight, bias, out_weight)
 
 
 def body(embedding, send_list, edge_ends, pair_index, w_first, b_first, w_second):
@@ -252,7 +283,6 @@
     parts = hidden_width // LANES
     body_rows = feature_width // LANES * block_rows
     edge_total = edge_ends.shape[1]
-    table_rows = LEAD + node_count * block_rows * parts + 8
     anywhere = pl.BlockSpec(memory_space=pl.ANY)
     vmem = pl.BlockSpec(memory_space=pltpu.VMEM)
 
@@ -269,32 +299,10 @@
     )(send_list, embedding)
     arrived = lax.all_to_all(sent, "node", split_axis=0, concat_axis=0, tiled=True)
 
-    scores, pooled = pl.pallas_call(
-        functools.partial(scorer, blocks_here),
-        out_shape=(
-            jax.ShapeDtypeStruct((1, edge_total), jnp.float32),
-            jax.ShapeDtypeStruct((PAIRS_ROW // LANES, LANES), jnp.float32),
-        ),
-        in_specs=[anywhere] * 6,
-        out_specs=(vmem, vmem),
-        scratch_shapes=[
-            pltpu.VMEM((node_count, body_rows, LANES), jnp.bfloat16),
-            pltpu.VMEM((node_count, LABEL_ROWS, LANES), jnp.bfloat16),
-            pltpu.VMEM((2, edge_total), jnp.int32),
-            pltpu.VMEM((1, edge_total), jnp.int32),
-            pltpu.VMEM((2, feature_width, hidden_width), jnp.bfloat16),
-            pltpu.VMEM((2 * parts, LANES), jnp.float32),
-            pltpu.VMEM((2 * parts, LANES), jnp.float32),
-            pltpu.VMEM((table_rows, LANES), jnp.float32),
-            pltpu.VMEM((table_rows, LANES), jnp.float32),
-            pltpu.VMEM((edge_total * parts, LANES), jnp.float32),
-            pltpu.VMEM((2, edge_total), jnp.int32),
-            pltpu.SMEM((2, edge_total), jnp.int32),
-            pltpu.SemaphoreType.DMA((node_count // 2,)),
-            pltpu.SemaphoreType.DMA((10,)),
-        ],
-        compiler_params=pltpu.CompilerParams(vmem_limit_bytes=56 * 2**20),
-    )(
+    paired = lax.axis_size("edge") == 2
+    scores, mine, other = call_scorer(
+        blocks_here,
+        paired,
         arrived,
         edge_ends,
         pair_index.reshape(1, edge_total),
@@ -303,12 +311,10 @@
         w_second.astype(jnp.float32).reshape(parts, LANES),
     )
     edge_score = scores.reshape(edge_total)
-    pooled = pooled.reshape(PAIRS_ROW)
-    if lax.axis_size("edge") == 2:
-        mine = PAIRS_ROW // 2
-        whole = pooled + lax.ppermute(pooled, "edge", [(0, 1), (1, 0)])
-        pair_cost = lax.dynamic_slice(whole, (lax.axis_index("edge") * mine,), (mine,))
+    if paired:
+        pair_cost = (mine + lax.ppermute(other, "edge", [(0, 1), (1, 0)])).reshape(PAIRS_ROW // 2)
     else:
+        pooled = jnp.concatenate([mine, other]).reshape(PAIRS_ROW)
         pair_cost = lax.psum_scatter(pooled, "edge", scatter_dimension=0, tiled=True)
     return (edge_score, pair_cost)
 

time: 80.1 us -> 69.5 us (0.87)
  Pallas kernels: 18.7 us -> 10.3 us
  local copies, waits for them, and re-layouts: 2.02 us -> 0.03 us
    pallas_call x1, Pallas kernels: 16.1 us -> 7.72 us  [call_scorer(): pl.pallas_call(functools.partial(scorer, blocks_here, paired), out_shape=...]
    unnamed x4 -> x10, local copies, waits for them, and re-layouts: 1.36 us -> 0.03 us
  transfers between devices with their start and end apart: 2 -> 2, of which waited for: 2 -> 2; matrix products, arithmetic and copies ran while one was open for 1% -> 0% of each run, Pallas kernels for 0% -> 0%
where the time goes in v3:
time: 69.5 us; the launch traced here: 68.5 us
  waiting for transfers between devices  47.5 us (68%)
  Pallas kernels  10.3 us (15%)
  starting transfers between devices  9.38 us (13%)
  between operations  0.71 us (1%)
    all_to_all x1, waiting for transfers between devices, body(): lax.all_to_all(sent, 'node', split_axis=0, concat_axis=0, tiled=True)  46.6 us
    pallas_call x1, Pallas kernels, call_scorer(): pl.pallas_call(functools.partial(scorer, blocks_here, paired), out_shape=...  7.72 us
    all_to_all x1, starting transfers between devices, body(): lax.all_to_all(sent, 'node', split_axis=0, concat_axis=0, tiled=True)  6.81 us
    pallas_call x1, Pallas kernels, body(): pl.pallas_call(pick, out_shape=jax.ShapeDtypeStruct((node_count, body_row...  2.62 us
    ppermute x1, starting transfers between devices, body(): lax.ppermute(other, 'edge', [(0, 1), (1, 0)])  2.57 us
  transfers between devices with their start and end apart: 2, of which 2 were waited for; matrix products, arithmetic and copies ran while one was open for 0% of the time, Pallas kernels for 0%

profile of v3, /device:TPU:9, one launch (start us, length us, event | category | flops | bytes accessed | tf_op | source)
XLA Modules:
  0.0 68.5 jit_solution(7970317610659262271)
XLA Ops:
  0.6 2.6 %shard_map.86 = bf16[16,520,128]{2,1,0:T(8,128)(2,1)} custom-call(s32[1,1,16]{2,1,0:T(1,128)} %wanted_ref.1, bf16[8,128,512]{2,1,0:T(8,128)(2,1)} %embedding_ref.1), custom_call_target="tpu_custom_call" | custom-call | tf_op jit(solution)/shard_map/pallas_call | solution.py:289
  3.3 0.0 copy-start.4
  3.3 0.0 copy-start
  3.3 0.0 copy-start.1
  3.3 0.0 copy-start.2
  3.3 0.0 copy-start.3
  3.3 6.8 %all-to-all-start = ((bf16[16,520,128]{2,1,0:T(8,128)(2,1)}), bf16[16,520,128]{2,1,0:T(8,128)(2,1)S(1)}, u32[]{:S(2)}, u32[]{:S(2)}) async-start(bf16[16,520,128]{2,1,0:T(8,128)(2,1)} %shard_map.86), calls=%async_computation | async-start | bytes 4259840 | tf_op jit(solution)/shard_map/all_to_all | solution.py:300
  10.1 0.0 copy-done.4
  10.1 46.6 %all-to-all-done.arrived_hbm = bf16[16,520,128]{2,1,0:T(8,128)(2,1)S(1)} async-done(((bf16[16,520,128]{2,1,0:T(8,128)(2,1)}), bf16[16,520,128]{2,1,0:T(8,128)(2,1)S(1)}, u32[]{:S(2)}, u32[]{:S(2)}) %all-to-all-start) | async-done | bytes 2129952 | tf_op jit(solution)/shard_map/all_to_all | solution.py:300
  56.8 0.0 copy-done
  56.8 0.0 copy-done.1
  56.8 0.0 copy-done.2
  56.8 0.0 copy-done.3
  56.8 7.7 %shard_map.87 = (f32[1,2048]{1,0:T(1,128)}, f32[4,128]{1,0:T(4,128)S(1)}, f32[4,128]{1,0:T(4,128)S(1)}) custom-call(bf16[16,520,128]{2,1,0:T(8,128)(2,1)S(1)} %all-to-all-done.arrived_hbm, s32[2,2048]{1,0:T(2,128)S(1)} %copy-done.1, s32[1,2048]{1,0:T(1,128)S(1)} %bitcast.10, bf16[2,512,512]{2,1,0:T(8,128)(2,1)S(1)} %bitcast.9, f32[4,128]{1,0:T(4,128)S(1)} %bitcast.11, ...), custom_call_target="tpu_custom_call" | custom-call | tf_op jit(solution)/shard_map/pallas_call | solution.py:250
  64.5 2.6 %collective-permute-start = (f32[4,128]{1,0:T(4,128)S(1)}, f32[4,128]{1,0:T(4,128)S(1)}, u32[]{:S(2)}, u32[]{:S(2)}) collective-permute-start(f32[4,128]{1,0:T(4,128)S(1)} %get-tuple-element.7), channel_id=1, source_target_pairs={{0,1},{1,0},{2,3},{3,2},{4,5},{5,4},{6,7},{7,6},{8,9},{9,8},{10,11... | collective-permute-start | bytes 6152 | tf_op jit(solution)/shard_map/ppermute | solution.py:315
  67.1 0.8 %collective-permute-done = f32[4,128]{1,0:T(4,128)S(1)} collective-permute-done((f32[4,128]{1,0:T(4,128)S(1)}, f32[4,128]{1,0:T(4,128)S(1)}, u32[]{:S(2)}, u32[]{:S(2)}) %collective-permute-start) | collective-permute-done | bytes 2080 | tf_op jit(solution)/shard_map/ppermute | solution.py:315
  67.9 0.6 add_bitcast_fusion
  (1 shorter events, 0.0 us)
Async XLA Ops:
  3.3 6.9 %copy-start.4 = (bf16[512]{0:T(512)(128)(2,1)S(1)}, bf16[512]{0:T(512)(128)(2,1)}, u32[]{:S(2)}) copy-start(bf16[512]{0:T(512)(128)(2,1)} %param.13) | copy-start | bytes 3076
  3.3 53.5 %copy-start = (bf16[1024,512]{1,0:T(8,128)(2,1)S(1)}, bf16[1024,512]{1,0:T(8,128)(2,1)}, u32[]{:S(2)}) copy-start(bf16[1024,512]{1,0:T(8,128)(2,1)} %param.11) | copy-start | bytes 3145732
  3.3 53.5 %copy-start.1 = (s32[2,2048]{1,0:T(2,128)S(1)}, s32[2,2048]{1,0:T(2,128)}, u32[]{:S(2)}) copy-start(s32[2,2048]{1,0:T(2,128)} %ends_hbm.1) | copy-start | bytes 49156
  3.3 53.5 %copy-start.2 = (s32[2048]{0:T(1024)S(1)}, s32[2048]{0:T(1024)}, u32[]{:S(2)}) copy-start(s32[2048]{0:T(1024)} %param.10) | copy-start | bytes 24580
  3.3 53.5 %copy-start.3 = (f32[512]{0:T(512)S(1)}, f32[512]{0:T(512)}, u32[]{:S(2)}) copy-start(f32[512]{0:T(512)} %param.12) | copy-start | bytes 6148
  3.3 53.5 %all-to-all-start = ((bf16[16,520,128]{2,1,0:T(8,128)(2,1)}), bf16[16,520,128]{2,1,0:T(8,128)(2,1)S(1)}, u32[]{:S(2)}, u32[]{:S(2)}) async-start(bf16[16,520,128]{2,1,0:T(8,128)(2,1)} %shard_map.86), calls=%async_computation | async-start | bytes 4259840 | tf_op jit(solution)/shard_map/all_to_all | solution.py:300
  64.5 3.4 %collective-permute-start = (f32[4,128]{1,0:T(4,128)S(1)}, f32[4,128]{1,0:T(4,128)S(1)}, u32[]{:S(2)}, u32[]{:S(2)}) collective-permute-start(f32[4,128]{1,0:T(4,128)S(1)} %get-tuple-element.7), channel_id=1, source_target_pairs={{0,1},{1,0},{2,3},{3,2},{4,5},{5,4},{6,7},{7,6},{8,9},{9,8},{10,11... | collective-permute-start | bytes 6152 | tf_op jit(solution)/shard_map/ppermute | solution.py:315

commit v4 on v0

v4 whole, which is shorter than its diff:
```python
import functools

import jax
import jax.numpy as jnp
from jax import lax
from jax.experimental import pallas as pl
from jax.experimental.pallas import tpu as pltpu
from jax.sharding import PartitionSpec as P

PAIRS_ROW = 1024
LANES = 128
LEAD = 8
LABEL_ROWS = 8
IN_FLIGHT = 5
CHUNK = 4
GELU_A = 0.7978845608028654
GELU_B = GELU_A * 0.044715


def bits(power_of_two):
    return power_of_two.bit_length() - 1


def pick(node_ref, wanted_ref, embedding_ref, *sent_refs):
    blocks_here, block_rows, feature_width = embedding_ref.shape
    groups = feature_width // LANES
    for offset, sent_ref in enumerate(sent_refs):
        wanted = wanted_ref[0, 0, node_ref[0] ^ offset]
        block = jnp.clip(wanted, 0, blocks_here - 1)
        for group in range(groups):
            sent_ref[group * block_rows : (group + 1) * block_rows, :] = embedding_ref[
                block, :, group * LANES : (group + 1) * LANES
            ]
        label = jnp.full((LABEL_ROWS, LANES), wanted.astype(jnp.float32))
        sent_ref[groups * block_rows :, :] = label.astype(jnp.bfloat16)


def project(slots, block_refs, weight_ref, bias_ref, first_table, second_table):
    feature_width, hidden_width = weight_ref.shape[1:]
    groups = feature_width // LANES
    block_rows = (block_refs[0].shape[0] - LABEL_ROWS) // groups
    parts = hidden_width // LANES
    rows = jnp.concatenate(
        [
            jnp.concatenate([ref[group * block_rows : (group + 1) * block_rows, :] for group in range(groups)], axis=1)
            for ref in block_refs
        ],
        axis=0,
    )
    for end, table in enumerate((first_table, second_table)):
        shares = jnp.dot(rows, weight_ref[end], preferred_element_type=jnp.float32)
        for part in range(parts):
            share = shares[:, part * LANES : (part + 1) * LANES]
            if end == 0:
                share = share + bias_ref[part : part + 1, :]
            for place, slot in enumerate(slots):
                at = pl.ds(LEAD + slot * block_rows * parts + part, block_rows, stride=parts)
                table[at, :] = share[place * block_rows : (place + 1) * block_rows]


def open_tables(bias, first_table, second_table):
    absent = first_table.shape[0] - bias.shape[0]
    first_table[absent:, :] = bias[...]
    second_table[absent:, :] = jnp.zeros(bias.shape, jnp.float32)


def keep(weight_ref, bias_ref, out_weight_ref, ends_ref, pair_ref, weight, bias, out_weight, ends, pair):
    weight[...] = weight_ref[...]
    parts = bias_ref.shape[0]
    for copy in range(2):
        bias[copy * parts : (copy + 1) * parts, :] = bias_ref[...]
        out_weight[copy * parts : (copy + 1) * parts, :] = 0.5 * out_weight_ref[...]
    ends[...] = ends_ref[...]
    pair[...] = pair_ref[...]


def projector(slots, opening, *refs):
    count = len(slots)
    weight, bias = refs[count : count + 2]
    first_table, second_table = refs[-2:]
    if opening:
        open_tables(bias, first_table, second_table)
    project(slots, refs[:count], weight, bias, first_table, second_table)


def three_terms(x):
    high = x.astype(jnp.bfloat16)
    rest = x - high.astype(jnp.float32)
    middle = rest.astype(jnp.bfloat16)
    low = (rest - middle.astype(jnp.float32)).astype(jnp.bfloat16)
    return high, middle, low


def scorer(landing, chunks, staged, blocks_here, paired, *refs):
    node_count = len(landing)
    block_refs, refs = dict(zip(landing, refs[:node_count])), refs[node_count:]
    node_ref, ends_ref, pair_ref, weight_ref, bias_ref, out_weight_ref = refs[:6]
    refs = refs[8:] if staged else refs[6:]
    (
        score_ref,
        mine_ref,
        other_ref,
        first_table,
        second_table,
        terms,
        offsets_near,
        offsets,
        offsets_sems,
    ) = refs
    feature_width, hidden_width = weight_ref.shape[1:]
    block_rows = (block_refs[0].shape[0] - LABEL_ROWS) * LANES // feature_width
    edge_total = ends_ref.shape[1]
    parts = hidden_width // LANES
    row_total = node_count * block_rows

    ids = ends_ref[...]
    target = ids >> bits(block_rows)
    slot_of = (target >> bits(blocks_here)) ^ node_ref[0]
    delivered = jnp.full(ids.shape, -1, jnp.int32)
    for slot, ref in block_refs.items():
        label = ref[ref.shape[0] - LABEL_ROWS :, :].astype(jnp.float32)[:2].astype(jnp.int32)
        label = jnp.concatenate([label] * (edge_total // LANES), axis=1)
        delivered = jnp.where(slot_of == slot, label, delivered)
    row = (slot_of << bits(block_rows)) + (ids & (block_rows - 1))
    row = jnp.where(delivered == (target & (blocks_here - 1)), row, row_total)
    second_of_two = lax.broadcasted_iota(jnp.int32, ids.shape, 1) & 1
    offsets_near[...] = LEAD + (row - second_of_two) * parts
    offsets_copies = [
        pltpu.make_async_copy(
            offsets_near.at[end], offsets.at[pl.ds(end * edge_total, edge_total)], offsets_sems.at[end]
        )
        for end in range(2)
    ]
    for copy in offsets_copies:
        copy.start()

    if not staged:
        open_tables(bias_ref, first_table, second_table)
    for slots in chunks:
        project(slots, [block_refs[slot] for slot in slots], weight_ref, bias_ref, first_table, second_table)

    out_weight = out_weight_ref[...]
    early = lax.broadcasted_iota(jnp.int32, (8, LANES), 0) < parts
    for copy in offsets_copies:
        copy.wait()

    def two_rows(table, end, edge):
        at = end * edge_total + edge
        return jnp.where(early, table[pl.ds(offsets[at], 8), :], table[pl.ds(offsets[at + 1], 8), :])

    group_edges = 128

    def score_group(step, carry):
        for pair in range(group_edges // 2):
            edge = step * group_edges + 2 * pair
            x = two_rows(first_table, 0, edge) + two_rows(second_table, 1, edge)
            weighted = x * out_weight
            terms[pl.ds(pl.multiple_of(edge * parts, 8), 8), :] = weighted + weighted * jnp.tanh(
                x * (GELU_A + GELU_B * (x * x))
            )
        return carry

    lax.fori_loop(0, edge_total // group_edges, score_group, 0)

    sums = terms[pl.ds(0, edge_total, stride=parts), :]
    for part in range(1, parts):
        sums = sums + terms[pl.ds(part, edge_total, stride=parts), :]
    scores = lax.dot_general(
        jnp.ones((8, 3 * LANES), jnp.bfloat16),
        jnp.concatenate(three_terms(sums), axis=1),
        (((1,), (1,)), ((), ())),
        preferred_element_type=jnp.float32,
    )
    score_ref[...] = scores[0:1, :]

    pair = pair_ref[...] & (PAIRS_ROW - 1)
    pair_rows = PAIRS_ROW // LANES
    high = lax.broadcasted_iota(jnp.int32, (pair_rows, edge_total), 0) == (pair >> bits(LANES))
    low = lax.broadcasted_iota(jnp.int32, (LANES, edge_total), 0) == (pair & (LANES - 1))
    placed = jnp.concatenate(
        [term.astype(jnp.float32) for term in three_terms(jnp.where(high, scores[:pair_rows], 0.0))], axis=0
    )
    pooled = lax.dot_general(
        placed.astype(jnp.bfloat16),
        low.astype(jnp.float32).astype(jnp.bfloat16),
        (((1,), (1,)), ((), ())),
        preferred_element_type=jnp.float32,
    )
    pooled = pooled[:pair_rows] + pooled[pair_rows : 2 * pair_rows] + pooled[2 * pair_rows :]
    half = pair_rows // 2
    low_is_mine = True if not paired else lax.axis_index("edge") == 0
    mine_ref[...] = jnp.where(low_is_mine, pooled[:half], pooled[half:])
    other_ref[...] = jnp.where(low_is_mine, pooled[half:], pooled[:half])


def offsets_in_order(node_count):
    if node_count == 16:
        return [14, 2, 15, 1, 8, 5, 12, 4, 11, 3, 9, 7, 10, 6, 13]
    half = node_count // 2
    order = []
    for place in range(half):
        order.append(half + place)
        if place + 1 < half:
            order.append(place + 1)
    return order


def body(embedding, send_list, edge_ends, pair_index, w_first, b_first, w_second):
    node_count = lax.axis_size("node")
    node_self = lax.axis_index("node").astype(jnp.int32).reshape(1)
    blocks_here, block_rows, feature_width = embedding.shape
    hidden_width = w_first.shape[1]
    parts = hidden_width // LANES
    body_rows = feature_width // LANES * block_rows
    edge_total = edge_ends.shape[1]
    table_rows = LEAD + node_count * block_rows * parts + 2 * parts
    vmem = pl.BlockSpec(memory_space=pltpu.VMEM)
    smem = pl.BlockSpec(memory_space=pltpu.SMEM)
    block = jax.ShapeDtypeStruct((body_rows + LABEL_ROWS, LANES), jnp.bfloat16)
    table = jax.ShapeDtypeStruct((table_rows, LANES), jnp.float32)
    needed = (2 * table_rows + edge_total * parts) * LANES * 4 + 4 * feature_width * hidden_width
    needed += 2 * node_count * block.shape[0] * LANES
    params = pltpu.CompilerParams(vmem_limit_bytes=needed + 6 * 2**20)

    sent = pl.pallas_call(
        pick,
        out_shape=(block,) * node_count,
        in_specs=[smem, smem, vmem],
        out_specs=(vmem,) * node_count,
        compiler_params=params,
    )(node_self, send_list, embedding)

    weight = w_first.reshape(2, feature_width, hidden_width)
    bias = b_first.reshape(parts, LANES)
    out_weight = w_second.astype(jnp.float32).reshape(parts, LANES)
    ends = edge_ends
    pair = pair_index.reshape(1, edge_total)
    shared = [weight, bias, out_weight, ends, pair]
    twice = jax.ShapeDtypeStruct((2 * parts, LANES), jnp.float32)
    shared = pl.pallas_call(
        keep,
        out_shape=[weight, twice, twice, ends, pair],
        in_specs=[vmem] * 5,
        out_specs=[vmem] * 5,
        compiler_params=params,
    )(*shared)
    weight, bias, out_weight, ends, pair = shared

    def add_to_tables(slots, tables):
        blocks = [arrived[slot] for slot in slots]
        return pl.pallas_call(
            functools.partial(projector, slots, not tables),
            out_shape=[table, table],
            in_specs=[vmem] * (len(slots) + 2 + len(tables)),
            out_specs=[vmem] * 2,
            input_output_aliases={len(slots) + 2 + end: end for end in range(len(tables))},
            compiler_params=params,
        )(*blocks, weight, bias, *tables)

    staged = 4 * table_rows * LANES * 4 < 40 * 2**20
    tables = []
    order = offsets_in_order(node_count)
    landing = [0] + order
    arrived = {0: sent[0]}
    turn = node_self
    waiting = [0]
    for place, offset in enumerate(order):
        operand = sent[offset]
        if place >= IN_FLIGHT:
            landed = order[place - IN_FLIGHT]
            operand, arrived[landed], turn = lax.optimization_barrier((operand, arrived[landed], turn))
            waiting.append(landed)
        if place == IN_FLIGHT:
            operand, turn, weight, bias, out_weight, ends, pair = lax.optimization_barrier(
                (operand, turn, weight, bias, out_weight, ends, pair)
            )
        if staged and len(waiting) == CHUNK:
            tables = add_to_tables(waiting, tables)
            operand, turn, *tables = lax.optimization_barrier((operand, turn, *tables))
            waiting = []
        arrived[offset] = lax.ppermute(operand, "node", [(node, node ^ offset) for node in range(node_count)])

    done = [] if not staged else [slot for slot in landing if slot not in waiting + order[-IN_FLIGHT:]]
    last = [slot for slot in landing if slot not in done]
    chunks = [last[start : start + CHUNK] for start in range(0, len(last), CHUNK)]
    if staged:
        chunks[-1:] = [chunks[-1][:-2], chunks[-1][-2:]]
        for slots in chunks[:-1]:
            tables = add_to_tables(slots, tables)
        chunks = chunks[-1:]

    paired = lax.axis_size("edge") == 2
    half_pool = jax.ShapeDtypeStruct((PAIRS_ROW // LANES // 2, LANES), jnp.float32)
    scores, mine, other = pl.pallas_call(
        functools.partial(scorer, landing, chunks, staged, blocks_here, paired),
        out_shape=[jax.ShapeDtypeStruct((1, edge_total), jnp.float32), half_pool, half_pool] + [table] * len(tables),
        in_specs=[vmem] * node_count + [smem] + [vmem] * (5 + len(tables)),
        out_specs=[vmem] * (3 + len(tables)),
        input_output_aliases={node_count + 6 + end: 3 + end for end in range(len(tables))},
        scratch_shapes=([] if staged else [pltpu.VMEM(table.shape, table.dtype)] * 2)
        + [
            pltpu.VMEM((edge_total * parts, LANES), jnp.float32),
            pltpu.VMEM((2, edge_total), jnp.int32),
            pltpu.SMEM((2 * edge_total,), jnp.int32),
            pltpu.SemaphoreType.DMA((2,)),
        ],
        compiler_params=params,
    )(*[arrived[slot] for slot in landing], node_self, ends, pair, weight, bias, out_weight, *tables)[:3]
    edge_score = scores.reshape(edge_total)
    if paired:
        pair_cost = (mine + lax.ppermute(other, "edge", [(0, 1), (1, 0)])).reshape(PAIRS_ROW // 2)
    else:
        pooled = jnp.concatenate([mine, other]).reshape(PAIRS_ROW)
        pair_cost = lax.psum_scatter(pooled, "edge", scatter_dimension=0, tiled=True)
    return (edge_score, pair_cost)


def solution(mesh):
    return jax.shard_map(
        body,
        mesh=mesh,
        in_specs=(
            P("node", None, None),
            P("edge", "node", None),
            P(None, ("node", "edge")),
            P(("node", "edge")),
            P(),
            P(),
            P(),
        ),
        out_specs=(P(("node", "edge")), P(("node", "edge"))),
        check_vma=False,
    )
```

time: 112 us -> 64.5 us (0.58)
  waiting for transfers between devices: 42.5 us -> 20.6 us
  local copies, waits for them, and re-layouts: 26.2 us -> 5.19 us
  starting transfers between devices: 12.5 us -> 26.2 us
  matrix products: 11.7 us -> 0 us
  other arithmetic: 11.5 us -> 1.26 us
  Pallas kernels: 0 us -> 9.52 us
  blocking collectives: 4.65 us -> 0 us
    all_to_all x2 -> x0, waiting for transfers between devices: 42.5 us -> none  [the longest x1 41.9 us: body(): lax.all_to_all(picked, 'node', split_axis=0, concat_axis=0, tiled=True)]
    ppermute x0 -> x16, starting transfers between devices: none -> 26.2 us  [the longest x15 24.3 us: body(): lax.ppermute(operand, 'node', [(node, node ^ offset) for node in range(no...]
    gather x5 -> x0, local copies, waits for them, and re-layouts: 21 us -> none  [the longest x4 20.3 us: tile_step(): end_rows = jnp.take(flat_rows, rows_at, axis=0)]
    ppermute x0 -> x16, waiting for transfers between devices: none -> 20.6 us  [the longest x15 19.8 us: body(): lax.ppermute(operand, 'node', [(node, node ^ offset) for node in range(no...]
    all_to_all x2 -> x0, starting transfers between devices: 12.5 us -> none  [the longest x1 6.66 us: body(): lax.all_to_all(labels, 'node', split_axis=0, concat_axis=0, tiled=True)]
    dot_general x16 -> x0, matrix products: 11.7 us -> none  [the longest x4 3.93 us: tile_step(): scores = jnp.dot(hidden, w_out, precision=lax.Precision.HIGHEST)]
    pallas_call x0 -> x7, Pallas kernels: none -> 9.52 us  [the longest x1 5.96 us: body(): pl.pallas_call(functools.partial(scorer, landing, chunks, staged, blocks_...]
    select_n x8 -> x0, other arithmetic: 9.41 us -> none  [the longest x4 6.33 us: tile_step(): end_rows = jnp.where(present[..., None], end_rows, jnp.zeros_like(end_rows))]
  transfers between devices with their start and end apart: 2 -> 16, of which waited for: 2 -> 7; matrix products, arithmetic and copies ran while one was open for 7% -> 1% of each run, Pallas kernels for 0% -> 4%
where the time goes in v4:
time: 64.5 us; the launch traced here: 63.4 us
  starting transfers between devices  26.2 us (41%)
  waiting for transfers between devices  20.6 us (32%)
  Pallas kernels  9.52 us (15%)
  local copies, waits for them, and re-layouts  5.19 us (8%)
  other arithmetic  1.26 us (2%)
  between operations  0.73 us (1%)
    ppermute x15, starting transfers between devices, body(): lax.ppermute(operand, 'node', [(node, node ^ offset) for node in range(no...  24.3 us
    ppermute x15, waiting for transfers between devices, body(): lax.ppermute(operand, 'node', [(node, node ^ offset) for node in range(no...  19.8 us
    pallas_call x1, Pallas kernels, body(): pl.pallas_call(functools.partial(scorer, landing, chunks, staged, blocks_...  5.96 us
    unnamed x12, local copies, waits for them, and re-layouts  5.19 us
    pallas_call x4, Pallas kernels, add_to_tables(): pl.pallas_call(functools.partial(projector, slots, not tables), out_shape...  2.56 us
    ppermute x1, starting transfers between devices, body(): lax.ppermute(other, 'edge', [(0, 1), (1, 0)])  1.83 us
  transfers between devices with their start and end apart: 16, of which 7 were waited for; matrix products, arithmetic and copies ran while one was open for 1% of the time, Pallas kernels for 4%

profile of v4, /device:TPU:9, one launch (start us, length us, event | category | flops | bytes accessed | tf_op | source)
XLA Modules:
  0.0 63.4 jit_solution(6518844635854722469)
XLA Ops:
  0.6 0.0 copy-start
  0.6 1.2 %copy-done = bf16[8,128,512]{2,1,0:T(8,128)(2,1)S(1)} copy-done((bf16[8,128,512]{2,1,0:T(8,128)(2,1)S(1)}, bf16[8,128,512]{2,1,0:T(8,128)(2,1)}, u32[]{:S(2)}) %copy-start) | copy-done | bytes 1048600
  1.9 0.7 %copy-done.5 = s32[1,1,16]{2,1,0:T(1,128)S(1)} copy-done((s32[1,1,16]{2,1,0:T(1,128)S(1)}, s32[1,1,16]{2,1,0:T(1,128)}, u32[]{:S(2)}) %copy-start.5) | copy-done | bytes 88
  2.5 0.9 %shard_map.86 = (bf16[520,128]{1,0:T(8,128)(2,1)S(1)}, bf16[520,128]{1,0:T(8,128)(2,1)S(1)}, bf16[520,128]{1,0:T(8,128)(2,1)S(1)}, bf16[520,128]{1,0:T(8,128)(2,...) custom-call(s32[1]{0:T(128)} %bitcast.node_ref.refs_16_, ...), custom_call_target="tpu_custom_call" | custom-call | tf_op jit(solution)/shard_map/pallas_call | solution.py:225
  3.5 2.3 %collective-permute-start = (bf16[520,128]{1,0:T(8,128)(2,1)S(1)}, bf16[520,128]{1,0:T(8,128)(2,1)S(1)}, u32[]{:S(2)}, u32[]{:S(2)}) collective-permute-start(bf16[520,128]{1,0:T(8,128)(2,1)S(1)} %get-tuple-element.68), channel_id=1, source_target_pairs={{0,28},{2,30},{4,24},{6,26},{8,20},{10,22},{12,16},{14,18},{16,12}... | collective-permute-start | bytes 399368 | tf_op jit(solution)/shard_map/ppermute | solution.py:281
  5.8 0.2 collective-permute-start.1
  6.0 2.1 %collective-permute-start.2 = (bf16[520,128]{1,0:T(8,128)(2,1)S(1)}, bf16[520,128]{1,0:T(8,128)(2,1)S(1)}, u32[]{:S(2)}, u32[]{:S(2)}) collective-permute-start(bf16[520,128]{1,0:T(8,128)(2,1)S(1)} %get-tuple-element.74), channel_id=1, source_target_pairs={{0,30},{2,28},{4,26},{6,24},{8,22},{10,20},{12,18},{14,16},{16,14}... | collective-permute-start | bytes 399368 | tf_op jit(solution)/shard_map/ppermute | solution.py:281
  8.1 0.3 collective-permute-start.3
  8.3 4.1 %collective-permute-start.4 = (bf16[520,128]{1,0:T(8,128)(2,1)S(1)}, bf16[520,128]{1,0:T(8,128)(2,1)S(1)}, u32[]{:S(2)}, u32[]{:S(2)}) collective-permute-start(bf16[520,128]{1,0:T(8,128)(2,1)S(1)} %get-tuple-element.80), channel_id=1, source_target_pairs={{0,16},{2,18},{4,20},{6,22},{8,24},{10,26},{12,28},{14,30},{16,0},... | collective-permute-start | bytes 399368 | tf_op jit(solution)/shard_map/ppermute | solution.py:281
  12.4 0.7 %bitcast_convert_fusion.out_weight_ref = f32[4,128]{1,0:T(4,128)S(1)} fusion(bf16[512]{0:T(512)(128)(2,1)} %param.13), kind=kLoop, calls=%fused_computation.1 | loop fusion | flops 512 | bytes 3072 | tf_op jit(solution)/shard_map/reshape | solution.py:235
  13.1 1.2 %copy-done.1 = bf16[1024,512]{1,0:T(8,128)(2,1)S(1)} copy-done((bf16[1024,512]{1,0:T(8,128)(2,1)S(1)}, bf16[1024,512]{1,0:T(8,128)(2,1)}, u32[]{:S(2)}) %copy-start.1) | copy-done | bytes 1048600
  14.3 0.7 %copy-done.2 = s32[2,2048]{1,0:T(2,128)S(1)} copy-done((s32[2,2048]{1,0:T(2,128)S(1)}, s32[2,2048]{1,0:T(2,128)}, u32[]{:S(2)}) %copy-start.2) | copy-done | bytes 16408
  15.0 0.7 %copy-done.3 = s32[2048]{0:T(1024)S(1)} copy-done((s32[2048]{0:T(1024)S(1)}, s32[2048]{0:T(1024)}, u32[]{:S(2)}) %copy-start.3) | copy-done | bytes 8216
  15.7 0.7 %copy-done.4 = f32[512]{0:T(512)S(1)} copy-done((f32[512]{0:T(512)S(1)}, f32[512]{0:T(512)}, u32[]{:S(2)}) %copy-start.4) | copy-done | bytes 2072
  16.4 0.1 shard_map.87
  16.5 0.0 collective-permute-done.refs_1_
  16.5 0.1 collective-permute-start.5
  16.6 0.0 collective-permute-done.1.refs_2_
  16.6 1.2 %collective-permute-start.6 = (bf16[520,128]{1,0:T(8,128)(2,1)S(1)}, bf16[520,128]{1,0:T(8,128)(2,1)S(1)}, u32[]{:S(2)}, u32[]{:S(2)}) collective-permute-start(bf16[520,128]{1,0:T(8,128)(2,1)S(1)} %get-tuple-element.92), channel_id=1, source_target_pairs={{0,24},{2,26},{4,28},{6,30},{8,16},{10,18},{12,20},{14,22},{16,8},... | collective-permute-start | bytes 399368 | tf_op jit(solution)/shard_map/ppermute | solution.py:281
  17.8 4.2 %collective-permute-done.2.refs_3_ = bf16[520,128]{1,0:T(8,128)(2,1)S(1)} collective-permute-done((bf16[520,128]{1,0:T(8,128)(2,1)S(1)}, bf16[520,128]{1,0:T(8,128)(2,1)S(1)}, u32[]{:S(2)}, u32[]{:S(2)}) %collective-permute-start.2) | collective-permute-done | bytes 133152 | tf_op jit(solution)/shard_map/ppermute | solution.py:281
  22.0 0.0 collective-permute-done.3.refs_0_.refs_4_
  22.0 0.0 collective-permute-start.8
  22.0 0.7 %shard_map.88 = (f32[8208,128]{1,0:T(8,128)S(1)}, f32[8208,128]{1,0:T(8,128)S(1)}) custom-call(bf16[520,128]{1,0:T(8,128)(2,1)S(1)} %get-tuple-element.66.refs_0_, bf16[520,128]{1,0:T(8,128)(2,1)S(1)} %collective-permute-done.refs_1_, bf16[520,128]{1,0:T(8,128)(2,1)S(1)} %collective-permute-done.1.refs_2_, ...), custom_call_target="tpu_custom_call" | custom-call | tf_op jit(solution)/shard_map/pallas_call | solution.py:251
  22.7 3.6 %collective-permute-start.7 = (bf16[520,128]{1,0:T(8,128)(2,1)S(1)}, bf16[520,128]{1,0:T(8,128)(2,1)S(1)}, u32[]{:S(2)}, u32[]{:S(2)}) collective-permute-start(bf16[520,128]{1,0:T(8,128)(2,1)S(1)} %get-tuple-element.100), channel_id=1, source_target_pairs={{0,8},{2,10},{4,12},{6,14},{8,0},{10,2},{12,4},{14,6},{16,24},{18,... | collective-permute-start | bytes 399368 | tf_op jit(solution)/shard_map/ppermute | solution.py:281
  26.3 0.0 collective-permute-done.4.refs_1_.refs_5_
  26.3 0.2 collective-permute-start.9
  26.5 0.0 collective-permute-done.5.refs_2_.refs_6_
  26.5 2.4 %collective-permute-start.10 = (bf16[520,128]{1,0:T(8,128)(2,1)S(1)}, bf16[520,128]{1,0:T(8,128)(2,1)S(1)}, u32[]{:S(2)}, u32[]{:S(2)}) collective-permute-start(bf16[520,128]{1,0:T(8,128)(2,1)S(1)} %get-tuple-element.108), channel_id=1, source_target_pairs={{0,18},{2,16},{4,22},{6,20},{8,26},{10,24},{12,30},{14,28},{16,2},... | collective-permute-start | bytes 399368 | tf_op jit(solution)/shard_map/ppermute | solution.py:281
  28.9 2.1 %collective-permute-done.6.refs_3_.refs_7_ = bf16[520,128]{1,0:T(8,128)(2,1)S(1)} collective-permute-done((bf16[520,128]{1,0:T(8,128)(2,1)S(1)}, bf16[520,128]{1,0:T(8,128)(2,1)S(1)}, u32[]{:S(2)}, u32[]{:S(2)}) %collective-permute-start.6) | collective-permute-done | bytes 133152 | tf_op jit(solution)/shard_map/ppermute | solution.py:281
  31.0 6.5 %collective-permute-done.8.refs_1_.refs_9_ = bf16[520,128]{1,0:T(8,128)(2,1)S(1)} collective-permute-done((bf16[520,128]{1,0:T(8,128)(2,1)S(1)}, bf16[520,128]{1,0:T(8,128)(2,1)S(1)}, u32[]{:S(2)}, u32[]{:S(2)}) %collective-permute-start.8) | collective-permute-done | bytes 133152 | tf_op jit(solution)/shard_map/ppermute | solution.py:281
  37.4 3.4 %collective-permute-start.13 = (bf16[520,128]{1,0:T(8,128)(2,1)S(1)}, bf16[520,128]{1,0:T(8,128)(2,1)S(1)}, u32[]{:S(2)}, u32[]{:S(2)}) collective-permute-start(bf16[520,128]{1,0:T(8,128)(2,1)S(1)} %get-tuple-element.116), channel_id=1, source_target_pairs={{0,12},{2,14},{4,8},{6,10},{8,4},{10,6},{12,0},{14,2},{16,28},{18,... | collective-permute-start | bytes 399368 | tf_op jit(solution)/shard_map/ppermute | solution.py:281
  40.8 0.0 collective-permute-done.7.refs_0_.refs_8_
  40.8 0.7 %collective-permute-start.12 = (bf16[520,128]{1,0:T(8,128)(2,1)S(1)}, bf16[520,128]{1,0:T(8,128)(2,1)S(1)}, u32[]{:S(2)}, u32[]{:S(2)}) collective-permute-start(bf16[520,128]{1,0:T(8,128)(2,1)S(1)} %get-tuple-element.115), channel_id=1, source_target_pairs={{0,20},{2,22},{4,16},{6,18},{8,28},{10,30},{12,24},{14,26},{16,4},... | collective-permute-start | bytes 399368 | tf_op jit(solution)/shard_map/ppermute | solution.py:281
  41.5 0.7 %shard_map.89 = (f32[8208,128]{1,0:T(8,128)S(1)}, f32[8208,128]{1,0:T(8,128)S(1)}) custom-call(bf16[520,128]{1,0:T(8,128)(2,1)S(1)} %collective-permute-done.3.refs_0_.refs_4_, bf16[520,128]{1,0:T(8,128)(2,1)S(1)} %collective-permute-done.4.refs_1_.refs_5_, ...), custom_call_target="tpu_custom_call", output_to_operand_aliasing={{0}: (6, {}), {1}: (7, {})} | custom-call | tf_op jit(solution)/shard_map/pallas_call | solution.py:251
  42.2 3.2 %collective-permute-start.11 = (bf16[520,128]{1,0:T(8,128)(2,1)S(1)}, bf16[520,128]{1,0:T(8,128)(2,1)S(1)}, u32[]{:S(2)}, u32[]{:S(2)}) collective-permute-start(bf16[520,128]{1,0:T(8,128)(2,1)S(1)} %get-tuple-element.114), channel_id=1, source_target_pairs={{0,14},{2,12},{4,10},{6,8},{8,6},{10,4},{12,2},{14,0},{16,30},{18,... | collective-permute-start | bytes 399368 | tf_op jit(solution)/shard_map/ppermute | solution.py:281
  45.5 0.0 collective-permute-done.9.refs_2_.refs_10_
  45.5 0.6 collective-permute-start.14
  46.1 0.0 collective-permute-done.10.refs_3_.refs_11_
  46.1 0.7 %shard_map.90 = (f32[8208,128]{1,0:T(8,128)S(1)}, f32[8208,128]{1,0:T(8,128)S(1)}) custom-call(bf16[520,128]{1,0:T(8,128)(2,1)S(1)} %collective-permute-done.7.refs_0_.refs_8_, bf16[520,128]{1,0:T(8,128)(2,1)S(1)} %collective-permute-done.8.refs_1_.refs_9_, ...), custom_call_target="tpu_custom_call", output_to_operand_aliasing={{0}: (6, {}), {1}: (7, {})} | custom-call | tf_op jit(solution)/shard_map/pallas_call | solution.py:251
  46.8 1.2 %collective-permute-done.12.refs_1_.refs_13_ = bf16[520,128]{1,0:T(8,128)(2,1)S(1)} collective-permute-done((bf16[520,128]{1,0:T(8,128)(2,1)S(1)}, bf16[520,128]{1,0:T(8,128)(2,1)S(1)}, u32[]{:S(2)}, u32[]{:S(2)}) %collective-permute-start.12) | collective-permute-done | bytes 133152 | tf_op jit(solution)/shard_map/ppermute | solution.py:281
  48.0 2.8 %collective-permute-done.11.refs_0_.refs_12_ = bf16[520,128]{1,0:T(8,128)(2,1)S(1)} collective-permute-done((bf16[520,128]{1,0:T(8,128)(2,1)S(1)}, bf16[520,128]{1,0:T(8,128)(2,1)S(1)}, u32[]{:S(2)}, u32[]{:S(2)}) %collective-permute-start.11) | collective-permute-done | bytes 133152 | tf_op jit(solution)/shard_map/ppermute | solution.py:281
  50.8 0.4 shard_map.91
  51.2 0.0 collective-permute-done.13.refs_14_
  51.3 3.0 %collective-permute-done.14.refs_15_ = bf16[520,128]{1,0:T(8,128)(2,1)S(1)} collective-permute-done((bf16[520,128]{1,0:T(8,128)(2,1)S(1)}, bf16[520,128]{1,0:T(8,128)(2,1)S(1)}, u32[]{:S(2)}, u32[]{:S(2)}) %collective-permute-start.14) | collective-permute-done | bytes 133152 | tf_op jit(solution)/shard_map/ppermute | solution.py:281
  54.2 6.0 %shard_map.92 = (f32[1,2048]{1,0:T(1,128)}, f32[4,128]{1,0:T(4,128)S(1)}, f32[4,128]{1,0:T(4,128)S(1)}, f32[8208,128]{1,0:T(8,128)S(1)}, f32[8208,128]{1,0:T(8,128)S(1)}) custom-call(bf16[520,128]{1,0:T(8,128)(2,1)S(1)} %get-tuple-element.66.refs_0_, ...), custom_call_target="tpu_custom_call", output_to_operand_aliasing={{3}: (22, {}), {4}: (23, {})} | custom-call | tf_op jit(solution)/shard_map/pallas_call | solution.py:294
  60.2 1.8 %collective-permute-start.15 = (f32[4,128]{1,0:T(4,128)S(1)}, f32[4,128]{1,0:T(4,128)S(1)}, u32[]{:S(2)}, u32[]{:S(2)}) collective-permute-start(f32[4,128]{1,0:T(4,128)S(1)} %get-tuple-element.129), channel_id=1, source_target_pairs={{0,1},{1,0},{2,3},{3,2},{4,5},{5,4},{6,7},{7,6},{8,9},{9,8},{10,11... | collective-permute-start | bytes 6152 | tf_op jit(solution)/shard_map/ppermute | solution.py:311
  62.0 0.8 %collective-permute-done.15 = f32[4,128]{1,0:T(4,128)S(1)} collective-permute-done((f32[4,128]{1,0:T(4,128)S(1)}, f32[4,128]{1,0:T(4,128)S(1)}, u32[]{:S(2)}, u32[]{:S(2)}) %collective-permute-start.15) | collective-permute-done | bytes 2080 | tf_op jit(solution)/shard_map/ppermute | solution.py:311
  62.9 0.6 add_bitcast_fusion
  (5 shorter events, 0.0 us)
Async XLA Ops:
  0.6 1.2 %copy-start = (bf16[8,128,512]{2,1,0:T(8,128)(2,1)S(1)}, bf16[8,128,512]{2,1,0:T(8,128)(2,1)}, u32[]{:S(2)}) copy-start(bf16[8,128,512]{2,1,0:T(8,128)(2,1)} %embedding_ref.1) | copy-start | bytes 3145732
  1.9 0.7 %copy-start.5 = (s32[1,1,16]{2,1,0:T(1,128)S(1)}, s32[1,1,16]{2,1,0:T(1,128)}, u32[]{:S(2)}) copy-start(s32[1,1,16]{2,1,0:T(1,128)} %wanted_ref.1) | copy-start | bytes 196
  3.5 13.0 %collective-permute-start = (bf16[520,128]{1,0:T(8,128)(2,1)S(1)}, bf16[520,128]{1,0:T(8,128)(2,1)S(1)}, u32[]{:S(2)}, u32[]{:S(2)}) collective-permute-start(bf16[520,128]{1,0:T(8,128)(2,1)S(1)} %get-tuple-element.68), channel_id=1, source_target_pairs={{0,28},{2,30},{4,24},{6,26},{8,20},{10,22},{12,16},{14,18},{16,12}... | collective-permute-start | bytes 399368 | tf_op jit(solution)/shard_map/ppermute | solution.py:281
  5.8 10.8 %collective-permute-start.1 = (bf16[520,128]{1,0:T(8,128)(2,1)S(1)}, bf16[520,128]{1,0:T(8,128)(2,1)S(1)}, u32[]{:S(2)}, u32[]{:S(2)}) collective-permute-start(bf16[520,128]{1,0:T(8,128)(2,1)S(1)} %get-tuple-element.71), channel_id=1, source_target_pairs={{0,4},{2,6},{4,0},{6,2},{8,12},{10,14},{12,8},{14,10},{16,20},{18,... | collective-permute-start | bytes 399368 | tf_op jit(solution)/shard_map/ppermute | solution.py:281
  6.0 15.9 %collective-permute-start.2 = (bf16[520,128]{1,0:T(8,128)(2,1)S(1)}, bf16[520,128]{1,0:T(8,128)(2,1)S(1)}, u32[]{:S(2)}, u32[]{:S(2)}) collective-permute-start(bf16[520,128]{1,0:T(8,128)(2,1)S(1)} %get-tuple-element.74), channel_id=1, source_target_pairs={{0,30},{2,28},{4,26},{6,24},{8,22},{10,20},{12,18},{14,16},{16,14}... | collective-permute-start | bytes 399368 | tf_op jit(solution)/shard_map/ppermute | solution.py:281
  8.1 13.9 %collective-permute-start.3 = (bf16[520,128]{1,0:T(8,128)(2,1)S(1)}, bf16[520,128]{1,0:T(8,128)(2,1)S(1)}, u32[]{:S(2)}, u32[]{:S(2)}) collective-permute-start(bf16[520,128]{1,0:T(8,128)(2,1)S(1)} %get-tuple-element.77), channel_id=1, source_target_pairs={{0,2},{2,0},{4,6},{6,4},{8,10},{10,8},{12,14},{14,12},{16,18},{18,... | collective-permute-start | bytes 399368 | tf_op jit(solution)/shard_map/ppermute | solution.py:281
  8.3 18.0 %collective-permute-start.4 = (bf16[520,128]{1,0:T(8,128)(2,1)S(1)}, bf16[520,128]{1,0:T(8,128)(2,1)S(1)}, u32[]{:S(2)}, u32[]{:S(2)}) collective-permute-start(bf16[520,128]{1,0:T(8,128)(2,1)S(1)} %get-tuple-element.80), channel_id=1, source_target_pairs={{0,16},{2,18},{4,20},{6,22},{8,24},{10,26},{12,28},{14,30},{16,0},... | collective-permute-start | bytes 399368 | tf_op jit(solution)/shard_map/ppermute | solution.py:281
  13.1 1.2 %copy-start.1 = (bf16[1024,512]{1,0:T(8,128)(2,1)S(1)}, bf16[1024,512]{1,0:T(8,128)(2,1)}, u32[]{:S(2)}) copy-start(bf16[1024,512]{1,0:T(8,128)(2,1)} %param.11) | copy-start | bytes 3145732
  14.3 0.7 %copy-start.2 = (s32[2,2048]{1,0:T(2,128)S(1)}, s32[2,2048]{1,0:T(2,128)}, u32[]{:S(2)}) copy-start(s32[2,2048]{1,0:T(2,128)} %ends_ref.1) | copy-start | bytes 49156
  15.0 0.7 %copy-start.3 = (s32[2048]{0:T(1024)S(1)}, s32[2048]{0:T(1024)}, u32[]{:S(2)}) copy-start(s32[2048]{0:T(1024)} %param.10) | copy-start | bytes 24580
  15.7 0.7 %copy-start.4 = (f32[512]{0:T(512)S(1)}, f32[512]{0:T(512)}, u32[]{:S(2)}) copy-start(f32[512]{0:T(512)} %param.12) | copy-start | bytes 6148
  16.5 10.0 %collective-permute-start.5 = (bf16[520,128]{1,0:T(8,128)(2,1)S(1)}, bf16[520,128]{1,0:T(8,128)(2,1)S(1)}, u32[]{:S(2)}, u32[]{:S(2)}) collective-permute-start(bf16[520,128]{1,0:T(8,128)(2,1)S(1)} %get-tuple-element.89), channel_id=1, source_target_pairs={{0,10},{2,8},{4,14},{6,12},{8,2},{10,0},{12,6},{14,4},{16,26},{18,... | collective-permute-start | bytes 399368 | tf_op jit(solution)/shard_map/ppermute | solution.py:281
  16.6 14.4 %collective-permute-start.6 = (bf16[520,128]{1,0:T(8,128)(2,1)S(1)}, bf16[520,128]{1,0:T(8,128)(2,1)S(1)}, u32[]{:S(2)}, u32[]{:S(2)}) collective-permute-start(bf16[520,128]{1,0:T(8,128)(2,1)S(1)} %get-tuple-element.92), channel_id=1, source_target_pairs={{0,24},{2,26},{4,28},{6,30},{8,16},{10,18},{12,20},{14,22},{16,8},... | collective-permute-start | bytes 399368 | tf_op jit(solution)/shard_map/ppermute | solution.py:281
  22.0 15.5 %collective-permute-start.8 = (bf16[520,128]{1,0:T(8,128)(2,1)S(1)}, bf16[520,128]{1,0:T(8,128)(2,1)S(1)}, u32[]{:S(2)}, u32[]{:S(2)}) collective-permute-start(bf16[520,128]{1,0:T(8,128)(2,1)S(1)} %get-tuple-element.103), channel_id=1, source_target_pairs={{0,22},{2,20},{4,18},{6,16},{8,30},{10,28},{12,26},{14,24},{16,6},... | collective-permute-start | bytes 399368 | tf_op jit(solution)/shard_map/ppermute | solution.py:281
  22.7 18.2 %collective-permute-start.7 = (bf16[520,128]{1,0:T(8,128)(2,1)S(1)}, bf16[520,128]{1,0:T(8,128)(2,1)S(1)}, u32[]{:S(2)}, u32[]{:S(2)}) collective-permute-start(bf16[520,128]{1,0:T(8,128)(2,1)S(1)} %get-tuple-element.100), channel_id=1, source_target_pairs={{0,8},{2,10},{4,12},{6,14},{8,0},{10,2},{12,4},{14,6},{16,24},{18,... | collective-permute-start | bytes 399368 | tf_op jit(solution)/shard_map/ppermute | solution.py:281
  26.3 19.2 %collective-permute-start.9 = (bf16[520,128]{1,0:T(8,128)(2,1)S(1)}, bf16[520,128]{1,0:T(8,128)(2,1)S(1)}, u32[]{:S(2)}, u32[]{:S(2)}) collective-permute-start(bf16[520,128]{1,0:T(8,128)(2,1)S(1)} %get-tuple-element.106), channel_id=1, source_target_pairs={{0,6},{2,4},{4,2},{6,0},{8,14},{10,12},{12,10},{14,8},{16,22},{18,... | collective-permute-start | bytes 399368 | tf_op jit(solution)/shard_map/ppermute | solution.py:281
  26.5 19.5 %collective-permute-start.10 = (bf16[520,128]{1,0:T(8,128)(2,1)S(1)}, bf16[520,128]{1,0:T(8,128)(2,1)S(1)}, u32[]{:S(2)}, u32[]{:S(2)}) collective-permute-start(bf16[520,128]{1,0:T(8,128)(2,1)S(1)} %get-tuple-element.108), channel_id=1, source_target_pairs={{0,18},{2,16},{4,22},{6,20},{8,26},{10,24},{12,30},{14,28},{16,2},... | collective-permute-start | bytes 399368 | tf_op jit(solution)/shard_map/ppermute | solution.py:281
  37.4 13.8 %collective-permute-start.13 = (bf16[520,128]{1,0:T(8,128)(2,1)S(1)}, bf16[520,128]{1,0:T(8,128)(2,1)S(1)}, u32[]{:S(2)}, u32[]{:S(2)}) collective-permute-start(bf16[520,128]{1,0:T(8,128)(2,1)S(1)} %get-tuple-element.116), channel_id=1, source_target_pairs={{0,12},{2,14},{4,8},{6,10},{8,4},{10,6},{12,0},{14,2},{16,28},{18,... | collective-permute-start | bytes 399368 | tf_op jit(solution)/shard_map/ppermute | solution.py:281
  40.8 7.1 %collective-permute-start.12 = (bf16[520,128]{1,0:T(8,128)(2,1)S(1)}, bf16[520,128]{1,0:T(8,128)(2,1)S(1)}, u32[]{:S(2)}, u32[]{:S(2)}) collective-permute-start(bf16[520,128]{1,0:T(8,128)(2,1)S(1)} %get-tuple-element.115), channel_id=1, source_target_pairs={{0,20},{2,22},{4,16},{6,18},{8,28},{10,30},{12,24},{14,26},{16,4},... | collective-permute-start | bytes 399368 | tf_op jit(solution)/shard_map/ppermute | solution.py:281
  42.2 8.6 %collective-permute-start.11 = (bf16[520,128]{1,0:T(8,128)(2,1)S(1)}, bf16[520,128]{1,0:T(8,128)(2,1)S(1)}, u32[]{:S(2)}, u32[]{:S(2)}) collective-permute-start(bf16[520,128]{1,0:T(8,128)(2,1)S(1)} %get-tuple-element.114), channel_id=1, source_target_pairs={{0,14},{2,12},{4,10},{6,8},{8,6},{10,4},{12,2},{14,0},{16,30},{18,... | collective-permute-start | bytes 399368 | tf_op jit(solution)/shard_map/ppermute | solution.py:281
  45.5 8.8 %collective-permute-start.14 = (bf16[520,128]{1,0:T(8,128)(2,1)S(1)}, bf16[520,128]{1,0:T(8,128)(2,1)S(1)}, u32[]{:S(2)}, u32[]{:S(2)}) collective-permute-start(bf16[520,128]{1,0:T(8,128)(2,1)S(1)} %get-tuple-element.117), channel_id=1, source_target_pairs={{0,26},{2,24},{4,30},{6,28},{8,18},{10,16},{12,22},{14,20},{16,10}... | collective-permute-start | bytes 399368 | tf_op jit(solution)/shard_map/ppermute | solution.py:281
  60.2 2.6 %collective-permute-start.15 = (f32[4,128]{1,0:T(4,128)S(1)}, f32[4,128]{1,0:T(4,128)S(1)}, u32[]{:S(2)}, u32[]{:S(2)}) collective-permute-start(f32[4,128]{1,0:T(4,128)S(1)} %get-tuple-element.129), channel_id=1, source_target_pairs={{0,1},{1,0},{2,3},{3,2},{4,5},{5,4},{6,7},{7,6},{8,9},{9,8},{10,11... | collective-permute-start | bytes 6152 | tf_op jit(solution)/shard_map/ppermute | solution.py:311

commit v5 on v4

v5 whole, which is shorter than its diff:
```python
import functools

import jax
import jax.numpy as jnp
from jax import lax
from jax.experimental import pallas as pl
from jax.experimental.pallas import tpu as pltpu
from jax.sharding import PartitionSpec as P

PAIRS_ROW = 1024
LANES = 128
LEAD = 8
LABEL_ROWS = 8
IN_FLIGHT = 5
SORT_AT = 6
LATE = 6
CHUNK = 4
GELU_A = 0.7978845608028654
GELU_B = GELU_A * 0.044715


def bits(power_of_two):
    return power_of_two.bit_length() - 1


def pick(node_ref, wanted_ref, embedding_ref, *sent_refs):
    blocks_here, block_rows, feature_width = embedding_ref.shape
    groups = feature_width // LANES
    for offset, sent_ref in enumerate(sent_refs):
        wanted = wanted_ref[0, 0, node_ref[0] ^ offset]
        block = jnp.clip(wanted, 0, blocks_here - 1)
        for group in range(groups):
            sent_ref[group * block_rows : (group + 1) * block_rows, :] = embedding_ref[
                block, :, group * LANES : (group + 1) * LANES
            ]
        label = jnp.full((LABEL_ROWS, LANES), wanted.astype(jnp.float32))
        sent_ref[groups * block_rows :, :] = label.astype(jnp.bfloat16)


def project(slots, block_refs, weight_ref, first_table, second_table):
    feature_width, hidden_width = weight_ref.shape[1:]
    groups = feature_width // LANES
    block_rows = (block_refs[0].shape[0] - LABEL_ROWS) // groups
    parts = hidden_width // LANES
    rows = jnp.concatenate(
        [
            jnp.concatenate([ref[group * block_rows : (group + 1) * block_rows, :] for group in range(groups)], axis=1)
            for ref in block_refs
        ],
        axis=0,
    )
    for end, table in enumerate((first_table, second_table)):
        shares = jnp.dot(rows, weight_ref[end], preferred_element_type=jnp.float32)
        for part in range(parts):
            share = shares[:, part * LANES : (part + 1) * LANES]
            for place, slot in enumerate(slots):
                at = pl.ds(LEAD + slot * block_rows * parts + part, block_rows, stride=parts)
                table[at, :] = share[place * block_rows : (place + 1) * block_rows]


def open_tables(parts, *tables):
    for table in tables:
        table[table.shape[0] - 2 * parts :, :] = jnp.zeros((2 * parts, LANES), jnp.float32)


def keep_weight(weight_ref, weight):
    weight[...] = weight_ref[...]


def projector(slots, opening, *refs):
    count = len(slots)
    first_table, second_table = refs[-2:]
    if opening:
        open_tables(refs[count].shape[2] // LANES, first_table, second_table)
    project(slots, refs[:count], refs[count], first_table, second_table)


def three_terms(x):
    high = x.astype(jnp.bfloat16)
    rest = x - high.astype(jnp.float32)
    middle = rest.astype(jnp.bfloat16)
    low = (rest - middle.astype(jnp.float32)).astype(jnp.bfloat16)
    return high, middle, low


def one_hot(count, places):
    return lax.broadcasted_iota(jnp.int32, (count, places.shape[1]), 0) == places


def summed_by(rows, columns, row_count):
    def sums(values):
        kept = [jnp.where(one_hot(row_count, rows), value, 0.0) for value in values]
        return lax.dot_general(
            jnp.concatenate(kept, axis=0).astype(jnp.bfloat16),
            one_hot(LANES, columns).astype(jnp.float32).astype(jnp.bfloat16),
            (((1,), (1,)), ((), ())),
            preferred_element_type=jnp.float32,
        )

    return sums


def sorter(late_slots, block_rows, blocks_here, node_ref, edges_ref, ends_out, pair_out, edge_out, late_out):
    edge_total = edges_ref.shape[1]
    groups = edge_total // LANES

    def as_rows(line):
        return jnp.concatenate([line[:, group * LANES : (group + 1) * LANES] for group in range(groups)], axis=0)

    def as_line(rows):
        return jnp.concatenate([rows[group : group + 1] for group in range(groups)], axis=1)

    ids = edges_ref[0:2, :]
    slot_of = (ids >> bits(block_rows * blocks_here)) ^ node_ref[0]
    late = jnp.zeros(ids.shape, jnp.float32)
    for slot in late_slots:
        late = jnp.where(slot_of == slot, 1.0, late)
    flags = as_rows(jnp.maximum(late[0:1], late[1:2]))

    def matrix(rows, columns, keep):
        at = [lax.broadcasted_iota(jnp.int32, (rows, columns), axis) for axis in range(2)]
        return jnp.where(keep(*at), 1.0, 0.0).astype(jnp.bfloat16)

    def product(left, right):
        return jnp.dot(left, right, preferred_element_type=jnp.float32)

    in_row = product(flags.astype(jnp.bfloat16), matrix(LANES, LANES, lambda i, j: i < j))
    of_row = product(flags.astype(jnp.bfloat16), matrix(LANES, LANES, lambda i, j: i >= 0)).astype(jnp.bfloat16)
    rows_before = product(matrix(groups, groups, lambda i, j: j < i), of_row)
    late_total = product(matrix(groups, groups, lambda i, j: i >= 0), of_row)
    late_out[...] = late_total[:8]

    index = lax.broadcasted_iota(jnp.int32, flags.shape, 0) * LANES + lax.broadcasted_iota(jnp.int32, flags.shape, 1)
    before = in_row + rows_before
    place = jnp.where(flags > 0.0, edge_total - late_total + before, index.astype(jnp.float32) - before)
    place = as_line(place.astype(jnp.int32))

    pair = edges_ref[2:3, :] & (PAIRS_ROW - 1)
    edge = lax.broadcasted_iota(jnp.int32, pair.shape, 1)
    pieces = []
    for line in (ids[0:1], ids[1:2], pair, edge):
        pieces += [(line >> 8).astype(jnp.float32), (line & 255).astype(jnp.float32)]
    moved = summed_by(place >> bits(LANES), place & (LANES - 1), groups)(pieces).astype(jnp.int32)
    moved = [moved[piece * groups : (piece + 1) * groups] for piece in range(len(pieces))]
    ends_out[:groups, :] = (moved[0] << 8) + moved[1]
    ends_out[groups:, :] = (moved[2] << 8) + moved[3]
    pair_out[...] = as_line((moved[4] << 8) + moved[5])
    edge_out[...] = as_line((moved[6] << 8) + moved[7])


class Gather:
    def __init__(self, block_refs, block_rows, blocks_here, row_total, parts, node_ref, ends_ref, late_ref, scratch):
        self.offsets_near, self.offsets, self.sems = scratch
        self.parts = parts
        self.groups = ends_ref.shape[0] // 2
        late_total = jnp.max(late_ref[...]).astype(jnp.int32)
        self.early_groups = (self.groups * LANES - late_total) >> bits(LANES)
        ids = ends_ref[...]
        target = ids >> bits(block_rows)
        slot_of = (target >> bits(blocks_here)) ^ node_ref[0]
        delivered = jnp.full(ids.shape, -1, jnp.int32)
        for slot, ref in block_refs.items():
            label = ref[ref.shape[0] - LABEL_ROWS :, :].astype(jnp.float32).astype(jnp.int32)
            label = jnp.concatenate([label] * (ids.shape[0] // LABEL_ROWS), axis=0)
            delivered = jnp.where(slot_of == slot, label, delivered)
        row = (slot_of << bits(block_rows)) + (ids & (block_rows - 1))
        row = jnp.where(delivered == (target & (blocks_here - 1)), row, row_total)
        second_of_two = lax.broadcasted_iota(jnp.int32, ids.shape, 1) & 1
        self.offsets_near[...] = LEAD + (row - second_of_two) * parts

    def copies(self, group):
        return [
            pltpu.make_async_copy(
                self.offsets_near.at[end * self.groups + group],
                self.offsets.at[pl.ds((end * self.groups + group) * LANES, LANES)],
                self.sems.at[end, group],
            )
            for end in range(2)
        ]

    def start(self, first, behind):
        def step(group, carry):
            for copy in self.copies(group):
                copy.start()
            return carry

        lax.fori_loop(first, behind, step, 0)

    def score(self, first, behind, tables, hidden_ref, terms):
        bias = hidden_ref[: 2 * self.parts, :]
        out_weight = hidden_ref[2 * self.parts :, :]
        early = lax.broadcasted_iota(jnp.int32, (8, LANES), 0) < self.parts

        def two_rows(end, edge):
            at = end * self.groups * LANES + edge
            table, offsets = tables[end], self.offsets
            return jnp.where(early, table[pl.ds(offsets[at], 8), :], table[pl.ds(offsets[at + 1], 8), :])

        def step(group, carry):
            for copy in self.copies(group):
                copy.wait()
            for pair in range(LANES // 2):
                edge = group * LANES + 2 * pair
                x = two_rows(0, edge) + two_rows(1, edge) + bias
                weighted = x * out_weight
                terms[pl.ds(pl.multiple_of(edge * self.parts, 8), 8), :] = weighted + weighted * jnp.tanh(
                    x * (GELU_A + GELU_B * (x * x))
                )
            return carry

        lax.fori_loop(first, behind, step, 0)


def early_scorer(slots, node_count, blocks_here, *refs):
    block_refs = dict(zip(slots, refs[: len(slots)]))
    node_ref, ends_ref, late_ref, hidden_ref = refs[len(slots) : len(slots) + 4]
    first_table, second_table, terms = refs[len(slots) + 6 : len(slots) + 9]
    parts = hidden_ref.shape[0] // 4
    block_rows = (first_table.shape[0] - LEAD - 2 * parts) // (node_count * parts)
    gather = Gather(
        block_refs, block_rows, blocks_here, node_count * block_rows, parts, node_ref, ends_ref, late_ref, refs[-3:]
    )
    gather.start(0, gather.early_groups)
    gather.score(0, gather.early_groups, (first_table, second_table), hidden_ref, terms)


def scorer(landing, chunks, staged, blocks_here, paired, *refs):
    node_count = len(landing)
    block_refs, refs = dict(zip(landing, refs[:node_count])), refs[node_count:]
    node_ref, ends_ref, pair_ref, edge_ref, late_ref, weight_ref, hidden_ref = refs[:7]
    refs = refs[10:] if staged else refs[7:]
    score_ref, mine_ref, other_ref, first_table, second_table, terms = refs[:6]
    feature_width, hidden_width = weight_ref.shape[1:]
    block_rows = (block_refs[0].shape[0] - LABEL_ROWS) * LANES // feature_width
    parts = hidden_width // LANES
    groups = ends_ref.shape[0] // 2
    edge_total = groups * LANES

    gather = Gather(
        block_refs, block_rows, blocks_here, node_count * block_rows, parts, node_ref, ends_ref, late_ref, refs[6:]
    )
    gather.start(gather.early_groups, groups)
    if not staged:
        open_tables(parts, first_table, second_table)
    for slots in chunks:
        project(slots, [block_refs[slot] for slot in slots], weight_ref, first_table, second_table)
    gather.score(gather.early_groups, groups, (first_table, second_table), hidden_ref, terms)

    sums = terms[pl.ds(0, edge_total, stride=parts), :]
    for part in range(1, parts):
        sums = sums + terms[pl.ds(part, edge_total, stride=parts), :]
    scores = lax.dot_general(
        jnp.full((8, 3 * LANES), 0.5, jnp.bfloat16),
        jnp.concatenate(three_terms(sums), axis=1),
        (((1,), (1,)), ((), ())),
        preferred_element_type=jnp.float32,
    )
    scores = [term.astype(jnp.float32) for term in three_terms(scores[0:1])]

    def place(rows, columns, row_count):
        sums = summed_by(rows, columns, row_count)(scores)
        return sums[:row_count] + sums[row_count : 2 * row_count] + sums[2 * row_count :]

    edge = edge_ref[...]
    score_ref[...] = place(edge >> bits(LANES), edge & (LANES - 1), groups)
    pair = pair_ref[...]
    pooled = place(pair >> bits(LANES), pair & (LANES - 1), PAIRS_ROW // LANES)
    half = PAIRS_ROW // LANES // 2
    low_is_mine = True if not paired else lax.axis_index("edge") == 0
    mine_ref[...] = jnp.where(low_is_mine, pooled[:half], pooled[half:])
    other_ref[...] = jnp.where(low_is_mine, pooled[half:], pooled[:half])


def offsets_in_order(node_count):
    if node_count == 16:
        return [2, 14, 1, 15, 5, 8, 4, 12, 3, 11, 7, 9, 6, 10, 13]
    half = node_count // 2
    order = []
    for place in range(half):
        order.append(half + place)
        if place + 1 < half:
            order.append(place + 1)
    return order


def nothing(*refs):
    pass


def after(array, others, params):
    vmem = pl.BlockSpec(memory_space=pltpu.VMEM)
    return pl.pallas_call(
        nothing,
        out_shape=jax.ShapeDtypeStruct(array.shape, array.dtype),
        in_specs=[vmem] * (1 + len(others)),
        out_specs=vmem,
        input_output_aliases={0: 0},
        compiler_params=params,
    )(array, *others)


def body(embedding, send_list, edge_ends, pair_index, w_first, b_first, w_second):
    node_count = lax.axis_size("node")
    node_self = lax.axis_index("node").astype(jnp.int32).reshape(1)
    blocks_here, block_rows, feature_width = embedding.shape
    hidden_width = w_first.shape[1]
    parts = hidden_width // LANES
    body_rows = feature_width // LANES * block_rows
    edge_total = edge_ends.shape[1]
    table_rows = LEAD + node_count * block_rows * parts + 2 * parts
    vmem = pl.BlockSpec(memory_space=pltpu.VMEM)
    smem = pl.BlockSpec(memory_space=pltpu.SMEM)
    block = jax.ShapeDtypeStruct((body_rows + LABEL_ROWS, LANES), jnp.bfloat16)
    table = jax.ShapeDtypeStruct((table_rows, LANES), jnp.float32)
    needed = (2 * table_rows + edge_total * parts) * LANES * 4 + 4 * feature_width * hidden_width
    needed += 2 * node_count * block.shape[0] * LANES
    params = pltpu.CompilerParams(vmem_limit_bytes=needed + 6 * 2**20)

    sent = pl.pallas_call(
        pick,
        out_shape=(block,) * node_count,
        in_specs=[smem, smem, vmem],
        out_specs=(vmem,) * node_count,
        compiler_params=params,
    )(node_self, send_list, embedding)

    weight = w_first.reshape(2, feature_width, hidden_width)
    bias = b_first.reshape(parts, LANES)
    out_weight = w_second.astype(jnp.float32).reshape(parts, LANES)
    hidden = jnp.concatenate([bias, bias, out_weight, out_weight])
    edges = jnp.concatenate([edge_ends, pair_index.reshape(1, edge_total)])
    weight = pl.pallas_call(
        keep_weight, out_shape=weight, in_specs=[vmem], out_specs=vmem, compiler_params=params
    )(weight)
    def add_to_tables(slots, tables):
        blocks = [arrived[slot] for slot in slots]
        return pl.pallas_call(
            functools.partial(projector, slots, not tables),
            out_shape=[table, table],
            in_specs=[vmem] * (len(slots) + 1 + len(tables)),
            out_specs=[vmem] * 2,
            input_output_aliases={len(slots) + 1 + end: end for end in range(len(tables))},
            compiler_params=params,
        )(*blocks, weight, *tables)

    staged = 4 * table_rows * LANES * 4 < 40 * 2**20
    order = offsets_in_order(node_count)
    landing = [0] + order
    early_slots = landing[:-LATE] if staged else []
    late_slots = landing[-LATE:] if staged else landing

    groups = edge_total // LANES
    sorted_edges = pl.pallas_call(
        functools.partial(sorter, late_slots, block_rows, blocks_here),
        out_shape=[
            jax.ShapeDtypeStruct((2 * groups, LANES), jnp.int32),
            jax.ShapeDtypeStruct((1, edge_total), jnp.int32),
            jax.ShapeDtypeStruct((1, edge_total), jnp.int32),
            jax.ShapeDtypeStruct((8, LANES), jnp.float32),
        ],
        in_specs=[smem, vmem],
        out_specs=[vmem] * 4,
        compiler_params=params,
    )(node_self, edges)
    ends, pair, edge, late = sorted_edges
    gather_scratch = [
        pltpu.VMEM((2 * groups, LANES), jnp.int32),
        pltpu.SMEM((2 * edge_total,), jnp.int32),
        pltpu.SemaphoreType.DMA((2, groups)),
    ]
    terms_shape = jax.ShapeDtypeStruct((edge_total * parts, LANES), jnp.float32)

    def score_early(tables):
        count = len(early_slots)
        return pl.pallas_call(
            functools.partial(early_scorer, early_slots, node_count, blocks_here),
            out_shape=[table, table, terms_shape],
            in_specs=[vmem] * count + [smem] + [vmem] * 5,
            out_specs=[vmem] * 3,
            input_output_aliases={count + 4 + end: end for end in range(2)},
            scratch_shapes=gather_scratch,
            compiler_params=params,
        )(*[arrived[slot] for slot in early_slots], node_self, ends, late, hidden, *tables)

    arrived = {0: sent[0]}
    waiting = [0]
    behind = []
    tables = []
    terms = []
    for place, offset in enumerate(order):
        operand = sent[offset]
        if place >= IN_FLIGHT:
            landed = order[place - IN_FLIGHT]
            behind = behind + [arrived[landed]]
            if place == IN_FLIGHT:
                behind = behind + [weight]
            if place == SORT_AT:
                behind = behind + [ends]
            if staged and (len(waiting) == CHUNK or waiting[-1:] == early_slots[-1:]):
                tables = add_to_tables(waiting, tables)
                if waiting[-1] == early_slots[-1]:
                    *tables, scored = score_early(tables)
                    terms = [scored]
                    behind = behind + [scored]
                behind = behind + [tables[0]]
                waiting = []
            operand = after(operand, behind, params)
            behind = [operand]
            waiting.append(landed)
        arrived[offset] = lax.ppermute(operand, "node", [(node, node ^ offset) for node in range(node_count)])

    last = (waiting + order[-IN_FLIGHT:]) if staged else landing
    chunks = [last[start : start + CHUNK] for start in range(0, len(last), CHUNK)]
    if staged:
        chunks = [last[:-2], last[-2:]]
        for slots in chunks[:-1]:
            tables = add_to_tables(slots, tables)
        chunks = chunks[-1:]

    paired = lax.axis_size("edge") == 2
    half_pool = jax.ShapeDtypeStruct((PAIRS_ROW // LANES // 2, LANES), jnp.float32)
    passed = [*tables, *terms]
    scores, mine, other = pl.pallas_call(
        functools.partial(scorer, landing, chunks, staged, blocks_here, paired),
        out_shape=[jax.ShapeDtypeStruct((groups, LANES), jnp.float32), half_pool, half_pool]
        + [jax.ShapeDtypeStruct(array.shape, array.dtype) for array in passed],
        in_specs=[vmem] * node_count + [smem] + [vmem] * (6 + len(passed)),
        out_specs=[vmem] * (3 + len(passed)),
        input_output_aliases={node_count + 7 + item: 3 + item for item in range(len(passed))},
        scratch_shapes=([] if staged else [pltpu.VMEM(kind.shape, kind.dtype) for kind in (table, table, terms_shape)])
        + gather_scratch,
        compiler_params=params,
    )(
        *[arrived[slot] for slot in landing],
        node_self,
        ends,
        pair,
        edge,
        late,
        weight,
        hidden,
        *passed,
    )[:3]
    edge_score = scores.reshape(edge_total)
    if paired:
        pair_cost = (mine + lax.ppermute(other, "edge", [(0, 1), (1, 0)])).reshape(PAIRS_ROW // 2)
    else:
        pooled = jnp.concatenate([mine, other]).reshape(PAIRS_ROW)
        pair_cost = lax.psum_scatter(pooled, "edge", scatter_dimension=0, tiled=True)
    return (edge_score, pair_cost)


def solution(mesh):
    return jax.shard_map(
        body,
        mesh=mesh,
        in_specs=(
            P("node", None, None),
            P("edge", "node", None),
            P(None, ("node", "edge")),
            P(("node", "edge")),
            P(),
            P(),
            P(),
        ),
        out_specs=(P(("node", "edge")), P(("node", "edge"))),
        check_vma=False,
    )
```

time: 64.5 us -> 61.1 us (0.947)
  starting transfers between devices: 26.2 us -> 20.7 us
  waiting for transfers between devices: 20.6 us -> 23 us
  local copies, waits for them, and re-layouts: 5.19 us -> 3.11 us
  Pallas kernels: 9.52 us -> 11.3 us
    ppermute x15, starting transfers between devices: 24.3 us -> 19 us  [body(): lax.ppermute(operand, 'node', [(node, node ^ offset) for node in range(no...]
    pallas_call x1 -> x13, Pallas kernels: 0.07 us -> 3.77 us  [the longest x1 3.09 us: score_early(): pl.pallas_call(functools.partial(early_scorer, early_slots, node_count, b...]
    ppermute x15, waiting for transfers between devices: 19.8 us -> 22.1 us  [body(): lax.ppermute(operand, 'node', [(node, node ^ offset) for node in range(no...]
    unnamed x12 -> x10, local copies, waits for them, and re-layouts: 5.19 us -> 3.11 us
    pallas_call x1, Pallas kernels: 5.96 us -> 4.08 us  [body(): pl.pallas_call(functools.partial(scorer, landing, chunks, staged, blocks_...]
    concatenate x0 -> x2, other arithmetic: none -> 0.76 us  [the longest x1 0.75 us: body(): edges = jnp.concatenate([edge_ends, pair_index.reshape(1, edge_total)])]
    reshape x1, other arithmetic: 0.68 us -> 0.01 us  [body(): out_weight = w_second.astype(jnp.float32).reshape(parts, LANES)]
  transfers between devices with their start and end apart: 16 -> 16, of which waited for: 7 -> 8; matrix products, arithmetic and copies ran while one was open for 1% -> 1% of each run, Pallas kernels for 4% -> 10%
where the time goes in v5:
time: 61.1 us; the launch traced here: 60.3 us
  waiting for transfers between devices  23 us (38%)
  starting transfers between devices  20.7 us (34%)
  Pallas kernels  11.3 us (18%)
  local copies, waits for them, and re-layouts  3.11 us (5%)
  other arithmetic  1.34 us (2%)
  between operations  0.79 us (1%)
    ppermute x15, waiting for transfers between devices, body(): lax.ppermute(operand, 'node', [(node, node ^ offset) for node in range(no...  22.1 us
    ppermute x15, starting transfers between devices, body(): lax.ppermute(operand, 'node', [(node, node ^ offset) for node in range(no...  19 us
    pallas_call x1, Pallas kernels, body(): pl.pallas_call(functools.partial(scorer, landing, chunks, staged, blocks_...  4.08 us
    unnamed x10, local copies, waits for them, and re-layouts  3.11 us
    pallas_call x1, Pallas kernels, score_early(): pl.pallas_call(functools.partial(early_scorer, early_slots, node_count, b...  3.09 us
    pallas_call x4, Pallas kernels, add_to_tables(): pl.pallas_call(functools.partial(projector, slots, not tables), out_shape...  2.55 us
    ppermute x1, starting transfers between devices, body(): lax.ppermute(other, 'edge', [(0, 1), (1, 0)])  1.76 us
  transfers between devices with their start and end apart: 16, of which 8 were waited for; matrix products, arithmetic and copies ran while one was open for 1% of the time, Pallas kernels for 10%

profile of v5, /device:TPU:9, one launch (start us, length us, event | category | flops | bytes accessed | tf_op | source)
XLA Modules:
  0.0 60.3 jit_solution(15897475322367999487)
XLA Ops:
  0.6 1.2 %copy-done = bf16[8,128,512]{2,1,0:T(8,128)(2,1)S(1)} copy-done((bf16[8,128,512]{2,1,0:T(8,128)(2,1)S(1)}, bf16[8,128,512]{2,1,0:T(8,128)(2,1)}, u32[]{:S(2)}) %copy-start) | copy-done | bytes 1048600
  1.9 0.7 %copy-done.2 = s32[1,1,16]{2,1,0:T(1,128)S(1)} copy-done((s32[1,1,16]{2,1,0:T(1,128)S(1)}, s32[1,1,16]{2,1,0:T(1,128)}, u32[]{:S(2)}) %copy-start.2) | copy-done | bytes 88
  2.5 0.9 %shard_map.86 = (bf16[520,128]{1,0:T(8,128)(2,1)S(1)}, bf16[520,128]{1,0:T(8,128)(2,1)S(1)}, bf16[520,128]{1,0:T(8,128)(2,1)S(1)}, bf16[520,128]{1,0:T(8,128)(2,...) custom-call(s32[1]{0:T(128)} %bitcast.node_ref.refs_10_.refs_16_, ...), custom_call_target="tpu_custom_call" | custom-call | tf_op jit(solution)/shard_map/pallas_call | solution.py:319
  3.5 1.3 %collective-permute-start = (bf16[520,128]{1,0:T(8,128)(2,1)S(1)}, bf16[520,128]{1,0:T(8,128)(2,1)S(1)}, u32[]{:S(2)}, u32[]{:S(2)}) collective-permute-start(bf16[520,128]{1,0:T(8,128)(2,1)S(1)} %get-tuple-element.37), channel_id=1, source_target_pairs={{0,4},{2,6},{4,0},{6,2},{8,12},{10,14},{12,8},{14,10},{16,20},{18,... | collective-permute-start | bytes 399368 | tf_op jit(solution)/shard_map/ppermute | solution.py:410
  4.8 1.2 %collective-permute-start.1 = (bf16[520,128]{1,0:T(8,128)(2,1)S(1)}, bf16[520,128]{1,0:T(8,128)(2,1)S(1)}, u32[]{:S(2)}, u32[]{:S(2)}) collective-permute-start(bf16[520,128]{1,0:T(8,128)(2,1)S(1)} %get-tuple-element.38), channel_id=1, source_target_pairs={{0,28},{2,30},{4,24},{6,26},{8,20},{10,22},{12,16},{14,18},{16,12}... | collective-permute-start | bytes 399368 | tf_op jit(solution)/shard_map/ppermute | solution.py:410
  6.0 1.2 %collective-permute-start.2 = (bf16[520,128]{1,0:T(8,128)(2,1)S(1)}, bf16[520,128]{1,0:T(8,128)(2,1)S(1)}, u32[]{:S(2)}, u32[]{:S(2)}) collective-permute-start(bf16[520,128]{1,0:T(8,128)(2,1)S(1)} %get-tuple-element.39), channel_id=1, source_target_pairs={{0,2},{2,0},{4,6},{6,4},{8,10},{10,8},{12,14},{14,12},{16,18},{18,... | collective-permute-start | bytes 399368 | tf_op jit(solution)/shard_map/ppermute | solution.py:410
  7.2 1.1 %collective-permute-start.3 = (bf16[520,128]{1,0:T(8,128)(2,1)S(1)}, bf16[520,128]{1,0:T(8,128)(2,1)S(1)}, u32[]{:S(2)}, u32[]{:S(2)}) collective-permute-start(bf16[520,128]{1,0:T(8,128)(2,1)S(1)} %get-tuple-element.40), channel_id=1, source_target_pairs={{0,30},{2,28},{4,26},{6,24},{8,22},{10,20},{12,18},{14,16},{16,14}... | collective-permute-start | bytes 399368 | tf_op jit(solution)/shard_map/ppermute | solution.py:410
  8.3 2.9 %collective-permute-start.4 = (bf16[520,128]{1,0:T(8,128)(2,1)S(1)}, bf16[520,128]{1,0:T(8,128)(2,1)S(1)}, u32[]{:S(2)}, u32[]{:S(2)}) collective-permute-start(bf16[520,128]{1,0:T(8,128)(2,1)S(1)} %get-tuple-element.41), channel_id=1, source_target_pairs={{0,10},{2,8},{4,14},{6,12},{8,2},{10,0},{12,6},{14,4},{16,26},{18,... | collective-permute-start | bytes 399368 | tf_op jit(solution)/shard_map/ppermute | solution.py:410
  11.2 0.8 %pad_add_fusion.edges_ref = s32[3,2048]{1,0:T(4,128)S(1)} fusion(s32[1,2048]{1,0:T(1,128)} %bitcast.11, s32[2,2048]{1,0:T(2,128)} %param.9), kind=kLoop, calls=%fused_computation | loop fusion | flops 6144 | bytes 49152 | tf_op jit(solution)/shard_map/concatenate | solution.py:331
  12.0 0.6 shard_map.89
  12.6 0.0 copy-start.1
  12.6 1.2 %copy-done.1 = bf16[1024,512]{1,0:T(8,128)(2,1)S(1)} copy-done((bf16[1024,512]{1,0:T(8,128)(2,1)S(1)}, bf16[1024,512]{1,0:T(8,128)(2,1)}, u32[]{:S(2)}) %copy-start.1) | copy-done | bytes 1048600
  13.8 0.1 shard_map.87.refs_2_.refs_4_.refs_21_
  13.9 0.0 collective-permute-done.refs_1_
  13.9 0.0 copy-start.4
  13.9 0.0 copy-start.3
  13.9 1.3 %collective-permute-start.5 = (bf16[520,128]{1,0:T(8,128)(2,1)S(1)}, bf16[520,128]{1,0:T(8,128)(2,1)S(1)}, u32[]{:S(2)}, u32[]{:S(2)}) collective-permute-start(bf16[520,128]{1,0:T(8,128)(2,1)S(1)} %shard_map.88.refs_1_), channel_id=1, source_target_pairs={{0,16},{2,18},{4,20},{6,22},{8,24},{10,26},{12,28},{14,30},{16,0},... | collective-permute-start | bytes 399368 | tf_op jit(solution)/shard_map/ppermute | solution.py:410
  15.2 0.0 collective-permute-done.1.refs_2_
  15.2 2.4 %collective-permute-start.6 = (bf16[520,128]{1,0:T(8,128)(2,1)S(1)}, bf16[520,128]{1,0:T(8,128)(2,1)S(1)}, u32[]{:S(2)}, u32[]{:S(2)}) collective-permute-start(bf16[520,128]{1,0:T(8,128)(2,1)S(1)} %shard_map.90.refs_1_), channel_id=1, source_target_pairs={{0,8},{2,10},{4,12},{6,14},{8,0},{10,2},{12,4},{14,6},{16,24},{18,... | collective-permute-start | bytes 399368 | tf_op jit(solution)/shard_map/ppermute | solution.py:410
  17.6 0.0 collective-permute-done.2.refs_2_.refs_3_
  17.6 0.0 collective-permute-start.7
  17.6 0.7 %shard_map.92 = (f32[8208,128]{1,0:T(8,128)S(1)}, f32[8208,128]{1,0:T(8,128)S(1)}) custom-call(bf16[520,128]{1,0:T(8,128)(2,1)S(1)} %get-tuple-element.36.refs_0_, bf16[520,128]{1,0:T(8,128)(2,1)S(1)} %collective-permute-done.refs_1_, bf16[520,128]{1,0:T(8,128)(2,1)S(1)} %collective-permute-done.1.refs_2_, ...), custom_call_target="tpu_custom_call" | custom-call | tf_op jit(solution)/shard_map/pallas_call | solution.py:337
  18.3 2.9 %collective-permute-done.3.refs_2_.refs_0_.refs_4_ = bf16[520,128]{1,0:T(8,128)(2,1)S(1)} collective-permute-done((bf16[520,128]{1,0:T(8,128)(2,1)S(1)}, bf16[520,128]{1,0:T(8,128)(2,1)S(1)}, u32[]{:S(2)}, u32[]{:S(2)}) %collective-permute-start.3) | collective-permute-done | bytes 133152 | tf_op jit(solution)/shard_map/ppermute | solution.py:410
  21.2 0.0 collective-permute-start.8
  21.2 0.0 collective-permute-done.4.refs_2_.refs_1_.refs_5_
  21.2 1.4 %collective-permute-start.9 = (bf16[520,128]{1,0:T(8,128)(2,1)S(1)}, bf16[520,128]{1,0:T(8,128)(2,1)S(1)}, u32[]{:S(2)}, u32[]{:S(2)}) collective-permute-start(bf16[520,128]{1,0:T(8,128)(2,1)S(1)} %shard_map.94.refs_1_), channel_id=1, source_target_pairs={{0,22},{2,20},{4,18},{6,16},{8,30},{10,28},{12,26},{14,24},{16,6},... | collective-permute-start | bytes 399368 | tf_op jit(solution)/shard_map/ppermute | solution.py:410
  22.6 1.3 %collective-permute-done.5.refs_2_.refs_6_ = bf16[520,128]{1,0:T(8,128)(2,1)S(1)} collective-permute-done((bf16[520,128]{1,0:T(8,128)(2,1)S(1)}, bf16[520,128]{1,0:T(8,128)(2,1)S(1)}, u32[]{:S(2)}, u32[]{:S(2)}) %collective-permute-start.5) | collective-permute-done | bytes 133152 | tf_op jit(solution)/shard_map/ppermute | solution.py:410
  24.0 4.1 %collective-permute-start.10 = (bf16[520,128]{1,0:T(8,128)(2,1)S(1)}, bf16[520,128]{1,0:T(8,128)(2,1)S(1)}, u32[]{:S(2)}, u32[]{:S(2)}) collective-permute-start(bf16[520,128]{1,0:T(8,128)(2,1)S(1)} %shard_map.95.refs_1_), channel_id=1, source_target_pairs={{0,14},{2,12},{4,10},{6,8},{8,6},{10,4},{12,2},{14,0},{16,30},{18,... | collective-permute-start | bytes 399368 | tf_op jit(solution)/shard_map/ppermute | solution.py:410
  28.0 0.0 collective-permute-done.6.refs_2_.refs_3_.refs_7_
  28.1 0.7 %collective-permute-start.11 = (bf16[520,128]{1,0:T(8,128)(2,1)S(1)}, bf16[520,128]{1,0:T(8,128)(2,1)S(1)}, u32[]{:S(2)}, u32[]{:S(2)}) collective-permute-start(bf16[520,128]{1,0:T(8,128)(2,1)S(1)} %shard_map.96.refs_1_), channel_id=1, source_target_pairs={{0,18},{2,16},{4,22},{6,20},{8,26},{10,24},{12,30},{14,28},{16,2},... | collective-permute-start | bytes 399368 | tf_op jit(solution)/shard_map/ppermute | solution.py:410
  28.8 0.7 %shard_map.97 = (f32[8208,128]{1,0:T(8,128)S(1)}, f32[8208,128]{1,0:T(8,128)S(1)}) custom-call(bf16[520,128]{1,0:T(8,128)(2,1)S(1)} %collective-permute-done.3.refs_2_.refs_0_.refs_4_, bf16[520,128]{1,0:T(8,128)(2,1)S(1)} %collective-permute-done.4.refs_2_.refs_1_.refs_5_, ...), custom_call_target="tpu_custom_call", output_to_operand_aliasing={{0}: (5, {}), {1}: (6, {})} | custom-call | tf_op jit(solution)/shard_map/pallas_call | solution.py:337
  29.5 4.3 %collective-permute-done.7.refs_2_.refs_0_.refs_8_ = bf16[520,128]{1,0:T(8,128)(2,1)S(1)} collective-permute-done((bf16[520,128]{1,0:T(8,128)(2,1)S(1)}, bf16[520,128]{1,0:T(8,128)(2,1)S(1)}, u32[]{:S(2)}, u32[]{:S(2)}) %collective-permute-start.7) | collective-permute-done | bytes 133152 | tf_op jit(solution)/shard_map/ppermute | solution.py:410
  33.8 0.0 collective-permute-start.12
  33.8 0.0 collective-permute-done.8.refs_2_.refs_1_.refs_9_
  33.8 0.3 collective-permute-start.13
  34.2 0.4 shard_map.100
  34.6 3.1 %shard_map.101 = (f32[8208,128]{1,0:T(8,128)S(1)}, f32[8208,128]{1,0:T(8,128)S(1)}, f32[8192,128]{1,0:T(8,128)S(1)}) custom-call(bf16[520,128]{1,0:T(8,128)(2,1)S(1)} %get-tuple-element.36.refs_0_, bf16[520,128]{1,0:T(8,128)(2,1)S(1)} %collective-permute-done.refs_1_, ...), custom_call_target="tpu_custom_call", output_to_operand_aliasing={{0}: (14, {}), {1}: (15, {})} | custom-call | tf_op jit(solution)/shard_map/pallas_call | solution.py:375
  37.7 1.0 %collective-permute-start.14 = (bf16[520,128]{1,0:T(8,128)(2,1)S(1)}, bf16[520,128]{1,0:T(8,128)(2,1)S(1)}, u32[]{:S(2)}, u32[]{:S(2)}) collective-permute-start(bf16[520,128]{1,0:T(8,128)(2,1)S(1)} %shard_map.102), channel_id=1, source_target_pairs={{0,26},{2,24},{4,30},{6,28},{8,18},{10,16},{12,22},{14,20},{16,10}... | collective-permute-start | bytes 399368 | tf_op jit(solution)/shard_map/ppermute | solution.py:410
  38.7 1.4 %collective-permute-done.12.refs_3_.refs_13_ = bf16[520,128]{1,0:T(8,128)(2,1)S(1)} collective-permute-done((bf16[520,128]{1,0:T(8,128)(2,1)S(1)}, bf16[520,128]{1,0:T(8,128)(2,1)S(1)}, u32[]{:S(2)}, u32[]{:S(2)}) %collective-permute-start.12) | collective-permute-done | bytes 133152 | tf_op jit(solution)/shard_map/ppermute | solution.py:410
  40.1 1.1 %collective-permute-done.11.refs_2_.refs_12_ = bf16[520,128]{1,0:T(8,128)(2,1)S(1)} collective-permute-done((bf16[520,128]{1,0:T(8,128)(2,1)S(1)}, bf16[520,128]{1,0:T(8,128)(2,1)S(1)}, u32[]{:S(2)}, u32[]{:S(2)}) %collective-permute-start.11) | collective-permute-done | bytes 133152 | tf_op jit(solution)/shard_map/ppermute | solution.py:410
  41.2 0.0 collective-permute-done.10.refs_1_.refs_11_
  41.2 0.7 %shard_map.103 = (f32[8208,128]{1,0:T(8,128)S(1)}, f32[8208,128]{1,0:T(8,128)S(1)}) custom-call(bf16[520,128]{1,0:T(8,128)(2,1)S(1)} %collective-permute-done.9.refs_2_.refs_0_.refs_10_, bf16[520,128]{1,0:T(8,128)(2,1)S(1)} %collective-permute-done.10.refs_1_.refs_11_, ...), custom_call_target="tpu_custom_call", output_to_operand_aliasing={{0}: (5, {}), {1}: (6, {})} | custom-call | tf_op jit(solution)/shard_map/pallas_call | solution.py:337
  41.9 5.1 %collective-permute-done.13.refs_14_ = bf16[520,128]{1,0:T(8,128)(2,1)S(1)} collective-permute-done((bf16[520,128]{1,0:T(8,128)(2,1)S(1)}, bf16[520,128]{1,0:T(8,128)(2,1)S(1)}, u32[]{:S(2)}, u32[]{:S(2)}) %collective-permute-start.13) | collective-permute-done | bytes 133152 | tf_op jit(solution)/shard_map/ppermute | solution.py:410
  47.1 6.0 %collective-permute-done.14.refs_15_ = bf16[520,128]{1,0:T(8,128)(2,1)S(1)} collective-permute-done((bf16[520,128]{1,0:T(8,128)(2,1)S(1)}, bf16[520,128]{1,0:T(8,128)(2,1)S(1)}, u32[]{:S(2)}, u32[]{:S(2)}) %collective-permute-start.14) | collective-permute-done | bytes 133152 | tf_op jit(solution)/shard_map/ppermute | solution.py:410
  53.0 4.1 %shard_map.104 = (f32[16,128]{1,0:T(8,128)}, f32[4,128]{1,0:T(4,128)S(1)}, f32[4,128]{1,0:T(4,128)S(1)}, f32[8208,128]{1,0:T(8,128)S(1)}, f32[8208,128]{1,0:T(8,128)S(1)}, /*index=5*/f32[8192,128]{1,0:T(8,128)S(1)}) custom-call(bf16[520,128]{1,0:T(8,128)(2,1)S(1)} %get-tuple-element.36.refs_0_, ...), custom_call_target="tpu_custom_call", output_to_operand_aliasing={{3}: (23, {}), {4}: (24, {}), {5}: (25, {})} | custom-call | tf_op jit(solution)/shard_map/pallas_call | solution.py:423
  57.1 1.8 %collective-permute-start.15 = (f32[4,128]{1,0:T(4,128)S(1)}, f32[4,128]{1,0:T(4,128)S(1)}, u32[]{:S(2)}, u32[]{:S(2)}) collective-permute-start(f32[4,128]{1,0:T(4,128)S(1)} %get-tuple-element.69), channel_id=1, source_target_pairs={{0,1},{1,0},{2,3},{3,2},{4,5},{5,4},{6,7},{7,6},{8,9},{9,8},{10,11... | collective-permute-start | bytes 6152 | tf_op jit(solution)/shard_map/ppermute | solution.py:446
  58.9 0.8 %collective-permute-done.15 = f32[4,128]{1,0:T(4,128)S(1)} collective-permute-done((f32[4,128]{1,0:T(4,128)S(1)}, f32[4,128]{1,0:T(4,128)S(1)}, u32[]{:S(2)}, u32[]{:S(2)}) %collective-permute-start.15) | collective-permute-done | bytes 2080 | tf_op jit(solution)/shard_map/ppermute | solution.py:446
  59.7 0.6 add_bitcast_fusion
  (17 shorter events, 0.0 us)
Async XLA Ops:
  0.6 1.2 %copy-start = (bf16[8,128,512]{2,1,0:T(8,128)(2,1)S(1)}, bf16[8,128,512]{2,1,0:T(8,128)(2,1)}, u32[]{:S(2)}) copy-start(bf16[8,128,512]{2,1,0:T(8,128)(2,1)} %embedding_ref.1) | copy-start | bytes 3145732
  1.9 0.7 %copy-start.2 = (s32[1,1,16]{2,1,0:T(1,128)S(1)}, s32[1,1,16]{2,1,0:T(1,128)}, u32[]{:S(2)}) copy-start(s32[1,1,16]{2,1,0:T(1,128)} %wanted_ref.1) | copy-start | bytes 196
  3.5 10.4 %collective-permute-start = (bf16[520,128]{1,0:T(8,128)(2,1)S(1)}, bf16[520,128]{1,0:T(8,128)(2,1)S(1)}, u32[]{:S(2)}, u32[]{:S(2)}) collective-permute-start(bf16[520,128]{1,0:T(8,128)(2,1)S(1)} %get-tuple-element.37), channel_id=1, source_target_pairs={{0,4},{2,6},{4,0},{6,2},{8,12},{10,14},{12,8},{14,10},{16,20},{18,... | collective-permute-start | bytes 399368 | tf_op jit(solution)/shard_map/ppermute | solution.py:410
  4.8 10.4 %collective-permute-start.1 = (bf16[520,128]{1,0:T(8,128)(2,1)S(1)}, bf16[520,128]{1,0:T(8,128)(2,1)S(1)}, u32[]{:S(2)}, u32[]{:S(2)}) collective-permute-start(bf16[520,128]{1,0:T(8,128)(2,1)S(1)} %get-tuple-element.38), channel_id=1, source_target_pairs={{0,28},{2,30},{4,24},{6,26},{8,20},{10,22},{12,16},{14,18},{16,12}... | collective-permute-start | bytes 399368 | tf_op jit(solution)/shard_map/ppermute | solution.py:410
  6.0 11.6 %collective-permute-start.2 = (bf16[520,128]{1,0:T(8,128)(2,1)S(1)}, bf16[520,128]{1,0:T(8,128)(2,1)S(1)}, u32[]{:S(2)}, u32[]{:S(2)}) collective-permute-start(bf16[520,128]{1,0:T(8,128)(2,1)S(1)} %get-tuple-element.39), channel_id=1, source_target_pairs={{0,2},{2,0},{4,6},{6,4},{8,10},{10,8},{12,14},{14,12},{16,18},{18,... | collective-permute-start | bytes 399368 | tf_op jit(solution)/shard_map/ppermute | solution.py:410
  7.2 14.0 %collective-permute-start.3 = (bf16[520,128]{1,0:T(8,128)(2,1)S(1)}, bf16[520,128]{1,0:T(8,128)(2,1)S(1)}, u32[]{:S(2)}, u32[]{:S(2)}) collective-permute-start(bf16[520,128]{1,0:T(8,128)(2,1)S(1)} %get-tuple-element.40), channel_id=1, source_target_pairs={{0,30},{2,28},{4,26},{6,24},{8,22},{10,20},{12,18},{14,16},{16,14}... | collective-permute-start | bytes 399368 | tf_op jit(solution)/shard_map/ppermute | solution.py:410
  8.3 12.9 %collective-permute-start.4 = (bf16[520,128]{1,0:T(8,128)(2,1)S(1)}, bf16[520,128]{1,0:T(8,128)(2,1)S(1)}, u32[]{:S(2)}, u32[]{:S(2)}) collective-permute-start(bf16[520,128]{1,0:T(8,128)(2,1)S(1)} %get-tuple-element.41), channel_id=1, source_target_pairs={{0,10},{2,8},{4,14},{6,12},{8,2},{10,0},{12,6},{14,4},{16,26},{18,... | collective-permute-start | bytes 399368 | tf_op jit(solution)/shard_map/ppermute | solution.py:410
  12.6 1.2 %copy-start.1 = (bf16[1024,512]{1,0:T(8,128)(2,1)S(1)}, bf16[1024,512]{1,0:T(8,128)(2,1)}, u32[]{:S(2)}) copy-start(bf16[1024,512]{1,0:T(8,128)(2,1)} %param.11) | copy-start | bytes 3145732
  13.9 8.7 %copy-start.4 = (bf16[512]{0:T(512)(128)(2,1)S(1)}, bf16[512]{0:T(512)(128)(2,1)}, u32[]{:S(2)}) copy-start(bf16[512]{0:T(512)(128)(2,1)} %param.13) | copy-start | bytes 3076
  13.9 8.7 %copy-start.3 = (f32[512]{0:T(512)S(1)}, f32[512]{0:T(512)}, u32[]{:S(2)}) copy-start(f32[512]{0:T(512)} %param.12) | copy-start | bytes 6148
  13.9 10.1 %collective-permute-start.5 = (bf16[520,128]{1,0:T(8,128)(2,1)S(1)}, bf16[520,128]{1,0:T(8,128)(2,1)S(1)}, u32[]{:S(2)}, u32[]{:S(2)}) collective-permute-start(bf16[520,128]{1,0:T(8,128)(2,1)S(1)} %shard_map.88.refs_1_), channel_id=1, source_target_pairs={{0,16},{2,18},{4,20},{6,22},{8,24},{10,26},{12,28},{14,30},{16,0},... | collective-permute-start | bytes 399368 | tf_op jit(solution)/shard_map/ppermute | solution.py:410
  15.2 12.9 %collective-permute-start.6 = (bf16[520,128]{1,0:T(8,128)(2,1)S(1)}, bf16[520,128]{1,0:T(8,128)(2,1)S(1)}, u32[]{:S(2)}, u32[]{:S(2)}) collective-permute-start(bf16[520,128]{1,0:T(8,128)(2,1)S(1)} %shard_map.90.refs_1_), channel_id=1, source_target_pairs={{0,8},{2,10},{4,12},{6,14},{8,0},{10,2},{12,4},{14,6},{16,24},{18,... | collective-permute-start | bytes 399368 | tf_op jit(solution)/shard_map/ppermute | solution.py:410
  17.6 16.2 %collective-permute-start.7 = (bf16[520,128]{1,0:T(8,128)(2,1)S(1)}, bf16[520,128]{1,0:T(8,128)(2,1)S(1)}, u32[]{:S(2)}, u32[]{:S(2)}) collective-permute-start(bf16[520,128]{1,0:T(8,128)(2,1)S(1)} %shard_map.91.refs_1_), channel_id=1, source_target_pairs={{0,24},{2,26},{4,28},{6,30},{8,16},{10,18},{12,20},{14,22},{16,8},... | collective-permute-start | bytes 399368 | tf_op jit(solution)/shard_map/ppermute | solution.py:410
  21.2 12.6 %collective-permute-start.8 = (bf16[520,128]{1,0:T(8,128)(2,1)S(1)}, bf16[520,128]{1,0:T(8,128)(2,1)S(1)}, u32[]{:S(2)}, u32[]{:S(2)}) collective-permute-start(bf16[520,128]{1,0:T(8,128)(2,1)S(1)} %shard_map.93.refs_1_), channel_id=1, source_target_pairs={{0,6},{2,4},{4,2},{6,0},{8,14},{10,12},{12,10},{14,8},{16,22},{18,... | collective-permute-start | bytes 399368 | tf_op jit(solution)/shard_map/ppermute | solution.py:410
  21.2 16.5 %collective-permute-start.9 = (bf16[520,128]{1,0:T(8,128)(2,1)S(1)}, bf16[520,128]{1,0:T(8,128)(2,1)S(1)}, u32[]{:S(2)}, u32[]{:S(2)}) collective-permute-start(bf16[520,128]{1,0:T(8,128)(2,1)S(1)} %shard_map.94.refs_1_), channel_id=1, source_target_pairs={{0,22},{2,20},{4,18},{6,16},{8,30},{10,28},{12,26},{14,24},{16,6},... | collective-permute-start | bytes 399368 | tf_op jit(solution)/shard_map/ppermute | solution.py:410
  24.0 17.2 %collective-permute-start.10 = (bf16[520,128]{1,0:T(8,128)(2,1)S(1)}, bf16[520,128]{1,0:T(8,128)(2,1)S(1)}, u32[]{:S(2)}, u32[]{:S(2)}) collective-permute-start(bf16[520,128]{1,0:T(8,128)(2,1)S(1)} %shard_map.95.refs_1_), channel_id=1, source_target_pairs={{0,14},{2,12},{4,10},{6,8},{8,6},{10,4},{12,2},{14,0},{16,30},{18,... | collective-permute-start | bytes 399368 | tf_op jit(solution)/shard_map/ppermute | solution.py:410
  28.1 13.2 %collective-permute-start.11 = (bf16[520,128]{1,0:T(8,128)(2,1)S(1)}, bf16[520,128]{1,0:T(8,128)(2,1)S(1)}, u32[]{:S(2)}, u32[]{:S(2)}) collective-permute-start(bf16[520,128]{1,0:T(8,128)(2,1)S(1)} %shard_map.96.refs_1_), channel_id=1, source_target_pairs={{0,18},{2,16},{4,22},{6,20},{8,26},{10,24},{12,30},{14,28},{16,2},... | collective-permute-start | bytes 399368 | tf_op jit(solution)/shard_map/ppermute | solution.py:410
  33.8 6.3 %collective-permute-start.12 = (bf16[520,128]{1,0:T(8,128)(2,1)S(1)}, bf16[520,128]{1,0:T(8,128)(2,1)S(1)}, u32[]{:S(2)}, u32[]{:S(2)}) collective-permute-start(bf16[520,128]{1,0:T(8,128)(2,1)S(1)} %shard_map.98.refs_1_), channel_id=1, source_target_pairs={{0,12},{2,14},{4,8},{6,10},{8,4},{10,6},{12,0},{14,2},{16,28},{18,... | collective-permute-start | bytes 399368 | tf_op jit(solution)/shard_map/ppermute | solution.py:410
  33.8 13.2 %collective-permute-start.13 = (bf16[520,128]{1,0:T(8,128)(2,1)S(1)}, bf16[520,128]{1,0:T(8,128)(2,1)S(1)}, u32[]{:S(2)}, u32[]{:S(2)}) collective-permute-start(bf16[520,128]{1,0:T(8,128)(2,1)S(1)} %shard_map.99.refs_1_), channel_id=1, source_target_pairs={{0,20},{2,22},{4,16},{6,18},{8,28},{10,30},{12,24},{14,26},{16,4},... | collective-permute-start | bytes 399368 | tf_op jit(solution)/shard_map/ppermute | solution.py:410
  37.7 15.3 %collective-permute-start.14 = (bf16[520,128]{1,0:T(8,128)(2,1)S(1)}, bf16[520,128]{1,0:T(8,128)(2,1)S(1)}, u32[]{:S(2)}, u32[]{:S(2)}) collective-permute-start(bf16[520,128]{1,0:T(8,128)(2,1)S(1)} %shard_map.102), channel_id=1, source_target_pairs={{0,26},{2,24},{4,30},{6,28},{8,18},{10,16},{12,22},{14,20},{16,10}... | collective-permute-start | bytes 399368 | tf_op jit(solution)/shard_map/ppermute | solution.py:410
  57.1 2.6 %collective-permute-start.15 = (f32[4,128]{1,0:T(4,128)S(1)}, f32[4,128]{1,0:T(4,128)S(1)}, u32[]{:S(2)}, u32[]{:S(2)}) collective-permute-start(f32[4,128]{1,0:T(4,128)S(1)} %get-tuple-element.69), channel_id=1, source_target_pairs={{0,1},{1,0},{2,3},{3,2},{4,5},{5,4},{6,7},{7,6},{8,9},{9,8},{10,11... | collective-permute-start | bytes 6152 | tf_op jit(solution)/shard_map/ppermute | solution.py:446

commit v6 on v5

--- a/solution.py
+++ b/solution.py
@@ -13,7 +13,7 @@
 LABEL_ROWS = 8
 IN_FLIGHT = 5
 SORT_AT = 6
-LATE = 6
+LATE = (6, 2)
 CHUNK = 4
 GELU_A = 0.7978845608028654
 GELU_B = GELU_A * 0.044715
@@ -100,7 +100,7 @@
     return sums
 
 
-def sorter(late_slots, block_rows, blocks_here, node_ref, edges_ref, ends_out, pair_out, edge_out, late_out):
+def sorter(late_stages, block_rows, blocks_here, node_ref, edges_ref, ends_out, pair_out, edge_out, late_out):
     edge_total = edges_ref.shape[1]
     groups = edge_total // LANES
 
@@ -112,11 +112,6 @@
 
     ids = edges_ref[0:2, :]
     slot_of = (ids >> bits(block_rows * blocks_here)) ^ node_ref[0]
-    late = jnp.zeros(ids.shape, jnp.float32)
-    for slot in late_slots:
-        late = jnp.where(slot_of == slot, 1.0, late)
-    flags = as_rows(jnp.maximum(late[0:1], late[1:2]))
-
     def matrix(rows, columns, keep):
         at = [lax.broadcasted_iota(jnp.int32, (rows, columns), axis) for axis in range(2)]
         return jnp.where(keep(*at), 1.0, 0.0).astype(jnp.bfloat16)
@@ -124,15 +119,28 @@
     def product(left, right):
         return jnp.dot(left, right, preferred_element_type=jnp.float32)
 
-    in_row = product(flags.astype(jnp.bfloat16), matrix(LANES, LANES, lambda i, j: i < j))
-    of_row = product(flags.astype(jnp.bfloat16), matrix(LANES, LANES, lambda i, j: i >= 0)).astype(jnp.bfloat16)
-    rows_before = product(matrix(groups, groups, lambda i, j: j < i), of_row)
-    late_total = product(matrix(groups, groups, lambda i, j: i >= 0), of_row)
-    late_out[...] = late_total[:8]
-
-    index = lax.broadcasted_iota(jnp.int32, flags.shape, 0) * LANES + lax.broadcasted_iota(jnp.int32, flags.shape, 1)
-    before = in_row + rows_before
-    place = jnp.where(flags > 0.0, edge_total - late_total + before, index.astype(jnp.float32) - before)
+    index = lax.broadcasted_iota(jnp.int32, (groups, LANES), 0) * LANES
+    index = index + lax.broadcasted_iota(jnp.int32, (groups, LANES), 1)
+    flags = [jnp.ones((groups, LANES), jnp.float32)]
+    before = [index.astype(jnp.float32)]
+    total = [jnp.full((groups, LANES), float(edge_total), jnp.float32)]
+    for stage, late_slots in enumerate(late_stages):
+        late = jnp.zeros(ids.shape, jnp.float32)
+        for slot in late_slots:
+            late = jnp.where(slot_of == slot, 1.0, late)
+        late = as_rows(jnp.maximum(late[0:1], late[1:2]))
+        in_row = product(late.astype(jnp.bfloat16), matrix(LANES, LANES, lambda i, j: i < j))
+        of_row = product(late.astype(jnp.bfloat16), matrix(LANES, LANES, lambda i, j: i >= 0)).astype(jnp.bfloat16)
+        flags.append(late)
+        before.append(in_row + product(matrix(groups, groups, lambda i, j: j < i), of_row))
+        total.append(product(matrix(groups, groups, lambda i, j: i >= 0), of_row))
+        late_out[8 * stage : 8 * stage + 8, :] = total[-1][:8]
+    flags.append(jnp.zeros((groups, LANES), jnp.float32))
+    before.append(flags[-1])
+    place = jnp.zeros((groups, LANES), jnp.float32)
+    for stage in range(len(late_stages) + 1):
+        here = edge_total - total[stage] + before[stage] - before[stage + 1]
+        place = place + (flags[stage] - flags[stage + 1]) * here
     place = as_line(place.astype(jnp.int32))
 
     pair = edges_ref[2:3, :] & (PAIRS_ROW - 1)
@@ -153,8 +161,7 @@
         self.offsets_near, self.offsets, self.sems = scratch
         self.parts = parts
         self.groups = ends_ref.shape[0] // 2
-        late_total = jnp.max(late_ref[...]).astype(jnp.int32)
-        self.early_groups = (self.groups * LANES - late_total) >> bits(LANES)
+        self.late_ref = late_ref
         ids = ends_ref[...]
         target = ids >> bits(block_rows)
         slot_of = (target >> bits(blocks_here)) ^ node_ref[0]
@@ -168,6 +175,10 @@
         second_of_two = lax.broadcasted_iota(jnp.int32, ids.shape, 1) & 1
         self.offsets_near[...] = LEAD + (row - second_of_two) * parts
 
+    def bound(self, stage):
+        late_total = jnp.max(self.late_ref[8 * stage : 8 * stage + 8, :]).astype(jnp.int32)
+        return (self.groups * LANES - late_total) >> bits(LANES)
+
     def copies(self, group):
         return [
             pltpu.make_async_copy(
@@ -211,17 +222,19 @@
         lax.fori_loop(first, behind, step, 0)
 
 
-def early_scorer(slots, node_count, blocks_here, *refs):
+def early_scorer(stage, slots, chunk, node_count, blocks_here, *refs):
     block_refs = dict(zip(slots, refs[: len(slots)]))
-    node_ref, ends_ref, late_ref, hidden_ref = refs[len(slots) : len(slots) + 4]
-    first_table, second_table, terms = refs[len(slots) + 6 : len(slots) + 9]
+    node_ref, ends_ref, late_ref, weight_ref, hidden_ref = refs[len(slots) : len(slots) + 5]
+    first_table, second_table, terms = refs[-6:-3]
     parts = hidden_ref.shape[0] // 4
     block_rows = (first_table.shape[0] - LEAD - 2 * parts) // (node_count * parts)
     gather = Gather(
         block_refs, block_rows, blocks_here, node_count * block_rows, parts, node_ref, ends_ref, late_ref, refs[-3:]
     )
-    gather.start(0, gather.early_groups)
-    gather.score(0, gather.early_groups, (first_table, second_table), hidden_ref, terms)
+    first, behind = gather.bound(stage - 1) if stage > 0 else 0, gather.bound(stage)
+    gather.start(first, behind)
+    project(chunk, [block_refs[slot] for slot in chunk], weight_ref, first_table, second_table)
+    gather.score(first, behind, (first_table, second_table), hidden_ref, terms)
 
 
 def scorer(landing, chunks, staged, blocks_here, paired, *refs):
@@ -230,6 +243,7 @@
     node_ref, ends_ref, pair_ref, edge_ref, late_ref, weight_ref, hidden_ref = refs[:7]
     refs = refs[10:] if staged else refs[7:]
     score_ref, mine_ref, other_ref, first_table, second_table, terms = refs[:6]
+    *gather_scratch, sorted_scores = refs[6:]
     feature_width, hidden_width = weight_ref.shape[1:]
     block_rows = (block_refs[0].shape[0] - LABEL_ROWS) * LANES // feature_width
     parts = hidden_width // LANES
@@ -237,25 +251,40 @@
     edge_total = groups * LANES
 
     gather = Gather(
-        block_refs, block_rows, blocks_here, node_count * block_rows, parts, node_ref, ends_ref, late_ref, refs[6:]
+        block_refs, block_rows, blocks_here, node_count * block_rows, parts, node_ref, ends_ref, late_ref, gather_scratch
     )
-    gather.start(gather.early_groups, groups)
+    first = gather.bound(late_ref.shape[0] // 8 - 1)
+    gather.start(first, groups)
     if not staged:
         open_tables(parts, first_table, second_table)
     for slots in chunks:
         project(slots, [block_refs[slot] for slot in slots], weight_ref, first_table, second_table)
-    gather.score(gather.early_groups, groups, (first_table, second_table), hidden_ref, terms)
-
-    sums = terms[pl.ds(0, edge_total, stride=parts), :]
-    for part in range(1, parts):
-        sums = sums + terms[pl.ds(part, edge_total, stride=parts), :]
-    scores = lax.dot_general(
-        jnp.full((8, 3 * LANES), 0.5, jnp.bfloat16),
-        jnp.concatenate(three_terms(sums), axis=1),
-        (((1,), (1,)), ((), ())),
-        preferred_element_type=jnp.float32,
-    )
-    scores = [term.astype(jnp.float32) for term in three_terms(scores[0:1])]
+
+    def add_up(begin, end):
+        edges = end - begin
+        sums = terms[pl.ds(begin * parts, edges, stride=parts), :]
+        for part in range(1, parts):
+            sums = sums + terms[pl.ds(begin * parts + part, edges, stride=parts), :]
+        scores = lax.dot_general(
+            jnp.full((8, 3 * LANES), 0.5, jnp.bfloat16),
+            jnp.concatenate(three_terms(sums), axis=1),
+            (((1,), (1,)), ((), ())),
+            preferred_element_type=jnp.float32,
+        )
+        sorted_scores[:, begin:end] = scores[0:1]
+
+    half = edge_total // 2
+    if staged:
+        add_up(0, half)
+    gather.score(first, groups, (first_table, second_table), hidden_ref, terms)
+
+    @pl.when(first < groups // 2)
+    def _():
+        add_up(0, half)
+
+    add_up(half, edge_total)
+    scores = sorted_scores[...]
+    scores = [term.astype(jnp.float32) for term in three_terms(scores)]
 
     def place(rows, columns, row_count):
         sums = summed_by(rows, columns, row_count)(scores)
@@ -271,9 +300,13 @@
     other_ref[...] = jnp.where(low_is_mine, pooled[half:], pooled[:half])
 
 
+def emit(array_ref, out_ref):
+    out_ref[...] = array_ref[...]
+
+
 def offsets_in_order(node_count):
     if node_count == 16:
-        return [2, 14, 1, 15, 5, 8, 4, 12, 3, 11, 7, 9, 6, 10, 13]
+        return [15, 14, 1, 2, 5, 8, 4, 12, 3, 11, 9, 7, 6, 10, 13]
     half = node_count // 2
     order = []
     for place in range(half):
@@ -346,17 +379,16 @@
     staged = 4 * table_rows * LANES * 4 < 40 * 2**20
     order = offsets_in_order(node_count)
     landing = [0] + order
-    early_slots = landing[:-LATE] if staged else []
-    late_slots = landing[-LATE:] if staged else landing
+    late_stages = [landing[-count:] for count in LATE] if staged else [landing]
 
     groups = edge_total // LANES
     sorted_edges = pl.pallas_call(
-        functools.partial(sorter, late_slots, block_rows, blocks_here),
+        functools.partial(sorter, late_stages, block_rows, blocks_here),
         out_shape=[
             jax.ShapeDtypeStruct((2 * groups, LANES), jnp.int32),
             jax.ShapeDtypeStruct((1, edge_total), jnp.int32),
             jax.ShapeDtypeStruct((1, edge_total), jnp.int32),
-            jax.ShapeDtypeStruct((8, LANES), jnp.float32),
+            jax.ShapeDtypeStruct((8 * len(late_stages), LANES), jnp.float32),
         ],
         in_specs=[smem, vmem],
         out_specs=[vmem] * 4,
@@ -370,23 +402,24 @@
     ]
     terms_shape = jax.ShapeDtypeStruct((edge_total * parts, LANES), jnp.float32)
 
-    def score_early(tables):
-        count = len(early_slots)
+    def score_early(stage, chunk, passed):
+        slots = [slot for slot in landing if slot not in late_stages[stage]]
+        count = len(slots)
         return pl.pallas_call(
-            functools.partial(early_scorer, early_slots, node_count, blocks_here),
+            functools.partial(early_scorer, stage, slots, chunk, node_count, blocks_here),
             out_shape=[table, table, terms_shape],
-            in_specs=[vmem] * count + [smem] + [vmem] * 5,
+            in_specs=[vmem] * count + [smem] + [vmem] * (4 + len(passed)),
             out_specs=[vmem] * 3,
-            input_output_aliases={count + 4 + end: end for end in range(2)},
+            input_output_aliases={count + 5 + item: item for item in range(len(passed))},
             scratch_shapes=gather_scratch,
             compiler_params=params,
-        )(*[arrived[slot] for slot in early_slots], node_self, ends, late, hidden, *tables)
+        )(*[arrived[slot] for slot in slots], node_self, ends, late, weight, hidden, *passed)
 
     arrived = {0: sent[0]}
     waiting = [0]
     behind = []
-    tables = []
-    terms = []
+    passed = []
+    stage = 0
     for place, offset in enumerate(order):
         operand = sent[offset]
         if place >= IN_FLIGHT:
@@ -396,13 +429,14 @@
                 behind = behind + [weight]
             if place == SORT_AT:
                 behind = behind + [ends]
-            if staged and (len(waiting) == CHUNK or waiting[-1:] == early_slots[-1:]):
-                tables = add_to_tables(waiting, tables)
-                if waiting[-1] == early_slots[-1]:
-                    *tables, scored = score_early(tables)
-                    terms = [scored]
-                    behind = behind + [scored]
-                behind = behind + [tables[0]]
+            if staged and stage < len(late_stages) and waiting and waiting[-1] == landing[-LATE[stage] - 1]:
+                passed = score_early(stage, waiting, passed)
+                behind = behind + [passed[2]]
+                stage += 1
+                waiting = []
+            elif staged and len(waiting) == CHUNK:
+                passed = add_to_tables(waiting, passed)
+                behind = behind + [passed[0]]
                 waiting = []
             operand = after(operand, behind, params)
             behind = [operand]
@@ -412,14 +446,14 @@
     last = (waiting + order[-IN_FLIGHT:]) if staged else landing
     chunks = [last[start : start + CHUNK] for start in range(0, len(last), CHUNK)]
     if staged:
-        chunks = [last[:-2], last[-2:]]
-        for slots in chunks[:-1]:
-            tables = add_to_tables(slots, tables)
-        chunks = chunks[-1:]
+        chunks = [last[-2:]]
+        if stage < len(late_stages):
+            passed = score_early(stage, last[:-2], passed)
+        else:
+            passed = [*add_to_tables(last[:-2], passed[:2]), passed[2]]
 
     paired = lax.axis_size("edge") == 2
     half_pool = jax.ShapeDtypeStruct((PAIRS_ROW // LANES // 2, LANES), jnp.float32)
-    passed = [*tables, *terms]
     scores, mine, other = pl.pallas_call(
         functools.partial(scorer, landing, chunks, staged, blocks_here, paired),
         out_shape=[jax.ShapeDtypeStruct((groups, LANES), jnp.float32), half_pool, half_pool]
@@ -428,7 +462,8 @@
         out_specs=[vmem] * (3 + len(passed)),
         input_output_aliases={node_count + 7 + item: 3 + item for item in range(len(passed))},
         scratch_shapes=([] if staged else [pltpu.VMEM(kind.shape, kind.dtype) for kind in (table, table, terms_shape)])
-        + gather_scratch,
+        + gather_scratch
+        + [pltpu.VMEM((1, edge_total), jnp.float32)],
         compiler_params=params,
     )(
         *[arrived[slot] for slot in landing],
@@ -441,6 +476,7 @@
         hidden,
         *passed,
     )[:3]
+    scores = pl.pallas_call(emit, out_shape=scores, in_specs=[vmem], out_specs=vmem, compiler_params=params)(scores)
     edge_score = scores.reshape(edge_total)
     if paired:
         pair_cost = (mine + lax.ppermute(other, "edge", [(0, 1), (1, 0)])).reshape(PAIRS_ROW // 2)

time: 61.1 us -> 58.6 us (0.959)
  waiting for transfers between devices: 23 us -> 16.8 us
  starting transfers between devices: 20.7 us -> 24.8 us
    ppermute x15, waiting for transfers between devices: 22.1 us -> 16.6 us  [body(): lax.ppermute(operand, 'node', [(node, node ^ offset) for node in range(no...]
    ppermute x15, starting transfers between devices: 19 us -> 22.3 us  [body(): lax.ppermute(operand, 'node', [(node, node ^ offset) for node in range(no...]
    pallas_call x2 -> x4, Pallas kernels: 3.69 us -> 6.55 us  [the longest x2 5.2 us: score_early(): pl.pallas_call(functools.partial(early_scorer, stage, slots, chunk, node_...]
    pallas_call x1, Pallas kernels: 4.08 us -> 2.43 us  [body(): pl.pallas_call(functools.partial(scorer, landing, chunks, staged, blocks_...]
    pallas_call x4 -> x2, Pallas kernels: 2.55 us -> 1.4 us  [add_to_tables(): pl.pallas_call(functools.partial(projector, slots, not tables), out_shape...]
    ppermute x1, starting transfers between devices: 1.76 us -> 2.46 us  [body(): lax.ppermute(other, 'edge', [(0, 1), (1, 0)])]
  transfers between devices with their start and end apart: 16 -> 16, of which waited for: 8 -> 6; matrix products, arithmetic and copies ran while one was open for 1% -> 1% of each run, Pallas kernels for 10% -> 14%
where the time goes in v6:
time: 58.6 us; the launch traced here: 58.3 us
  starting transfers between devices  24.8 us (42%)
  waiting for transfers between devices  16.8 us (29%)
  Pallas kernels  11.4 us (19%)
  local copies, waits for them, and re-layouts  3.11 us (5%)
  other arithmetic  1.34 us (2%)
  between operations  0.84 us (1%)
    ppermute x15, starting transfers between devices, body(): lax.ppermute(operand, 'node', [(node, node ^ offset) for node in range(no...  22.3 us
    ppermute x15, waiting for transfers between devices, body(): lax.ppermute(operand, 'node', [(node, node ^ offset) for node in range(no...  16.6 us
    pallas_call x2, Pallas kernels, score_early(): pl.pallas_call(functools.partial(early_scorer, stage, slots, chunk, node_...  5.2 us
    unnamed x10, local copies, waits for them, and re-layouts  3.11 us
    ppermute x1, starting transfers between devices, body(): lax.ppermute(other, 'edge', [(0, 1), (1, 0)])  2.46 us
    pallas_call x1, Pallas kernels, body(): pl.pallas_call(functools.partial(scorer, landing, chunks, staged, blocks_...  2.43 us
    pallas_call x2, Pallas kernels, add_to_tables(): pl.pallas_call(functools.partial(projector, slots, not tables), out_shape...  1.4 us
  transfers between devices with their start and end apart: 16, of which 6 were waited for; matrix products, arithmetic and copies ran while one was open for 1% of the time, Pallas kernels for 14%

profile of v6, /device:TPU:9, one launch (start us, length us, event | category | flops | bytes accessed | tf_op | source)
XLA Modules:
  0.0 58.3 jit_solution(9097999133515765489)
XLA Ops:
  0.6 1.2 %copy-done = bf16[8,128,512]{2,1,0:T(8,128)(2,1)S(1)} copy-done((bf16[8,128,512]{2,1,0:T(8,128)(2,1)S(1)}, bf16[8,128,512]{2,1,0:T(8,128)(2,1)}, u32[]{:S(2)}) %copy-start) | copy-done | bytes 1048600
  1.9 0.7 %copy-done.2 = s32[1,1,16]{2,1,0:T(1,128)S(1)} copy-done((s32[1,1,16]{2,1,0:T(1,128)S(1)}, s32[1,1,16]{2,1,0:T(1,128)}, u32[]{:S(2)}) %copy-start.2) | copy-done | bytes 88
  2.5 0.9 %shard_map.86 = (bf16[520,128]{1,0:T(8,128)(2,1)S(1)}, bf16[520,128]{1,0:T(8,128)(2,1)S(1)}, bf16[520,128]{1,0:T(8,128)(2,1)S(1)}, bf16[520,128]{1,0:T(8,128)(2,...) custom-call(s32[1]{0:T(128)} %bitcast.node_ref.refs_10_.refs_14_.ref, ...), custom_call_target="tpu_custom_call" | custom-call | tf_op jit(solution)/shard_map/pallas_call | solution.py:352
  3.5 3.2 %collective-permute-start = (bf16[520,128]{1,0:T(8,128)(2,1)S(1)}, bf16[520,128]{1,0:T(8,128)(2,1)S(1)}, u32[]{:S(2)}, u32[]{:S(2)}) collective-permute-start(bf16[520,128]{1,0:T(8,128)(2,1)S(1)} %get-tuple-element.36), channel_id=1, source_target_pairs={{0,30},{2,28},{4,26},{6,24},{8,22},{10,20},{12,18},{14,16},{16,14}... | collective-permute-start | bytes 399368 | tf_op jit(solution)/shard_map/ppermute | solution.py:444
  6.7 0.1 collective-permute-start.1
  6.8 0.3 collective-permute-start.2
  7.1 1.2 %collective-permute-start.3 = (bf16[520,128]{1,0:T(8,128)(2,1)S(1)}, bf16[520,128]{1,0:T(8,128)(2,1)S(1)}, u32[]{:S(2)}, u32[]{:S(2)}) collective-permute-start(bf16[520,128]{1,0:T(8,128)(2,1)S(1)} %get-tuple-element.39), channel_id=1, source_target_pairs={{0,4},{2,6},{4,0},{6,2},{8,12},{10,14},{12,8},{14,10},{16,20},{18,... | collective-permute-start | bytes 399368 | tf_op jit(solution)/shard_map/ppermute | solution.py:444
  8.3 2.9 %collective-permute-start.4 = (bf16[520,128]{1,0:T(8,128)(2,1)S(1)}, bf16[520,128]{1,0:T(8,128)(2,1)S(1)}, u32[]{:S(2)}, u32[]{:S(2)}) collective-permute-start(bf16[520,128]{1,0:T(8,128)(2,1)S(1)} %get-tuple-element.40), channel_id=1, source_target_pairs={{0,10},{2,8},{4,14},{6,12},{8,2},{10,0},{12,6},{14,4},{16,26},{18,... | collective-permute-start | bytes 399368 | tf_op jit(solution)/shard_map/ppermute | solution.py:444
  11.2 0.8 %pad_add_fusion.edges_ref = s32[3,2048]{1,0:T(4,128)S(1)} fusion(s32[1,2048]{1,0:T(1,128)} %bitcast.11, s32[2,2048]{1,0:T(2,128)} %param.9), kind=kLoop, calls=%fused_computation | loop fusion | flops 6144 | bytes 49152 | tf_op jit(solution)/shard_map/concatenate | solution.py:364
  12.0 0.8 %shard_map.89 = (s32[32,128]{1,0:T(8,128)S(1)}, s32[1,2048]{1,0:T(1,128)S(1)}, s32[1,2048]{1,0:T(1,128)S(1)}, f32[16,128]{1,0:T(8,128)S(1)}) custom-call(s32[1]{0:T(128)} %bitcast.node_ref.refs_10_.refs_14_.refs_16_, s32[3,2048]{1,0:T(4,128)S(1)} %pad_add_fusion.edges_ref), custom_call_target="tpu_custom_call" | custom-call | tf_op jit(solution)/shard_map/pallas_call | solution.py:385
  12.7 0.0 copy-start.1
  12.7 1.2 %copy-done.1 = bf16[1024,512]{1,0:T(8,128)(2,1)S(1)} copy-done((bf16[1024,512]{1,0:T(8,128)(2,1)S(1)}, bf16[1024,512]{1,0:T(8,128)(2,1)}, u32[]{:S(2)}) %copy-start.1) | copy-done | bytes 1048600
  13.9 0.1 shard_map.87.refs_2_.refs_4_.refs_13_.refs_17_.refs_21_
  14.0 0.0 collective-permute-done.refs_1_
  14.0 0.0 copy-start.4
  14.0 0.0 copy-start.3
  14.1 1.3 %collective-permute-start.5 = (bf16[520,128]{1,0:T(8,128)(2,1)S(1)}, bf16[520,128]{1,0:T(8,128)(2,1)S(1)}, u32[]{:S(2)}, u32[]{:S(2)}) collective-permute-start(bf16[520,128]{1,0:T(8,128)(2,1)S(1)} %shard_map.88.refs_1_), channel_id=1, source_target_pairs={{0,16},{2,18},{4,20},{6,22},{8,24},{10,26},{12,28},{14,30},{16,0},... | collective-permute-start | bytes 399368 | tf_op jit(solution)/shard_map/ppermute | solution.py:444
  15.3 3.3 %collective-permute-done.1.refs_2_ = bf16[520,128]{1,0:T(8,128)(2,1)S(1)} collective-permute-done((bf16[520,128]{1,0:T(8,128)(2,1)S(1)}, bf16[520,128]{1,0:T(8,128)(2,1)S(1)}, u32[]{:S(2)}, u32[]{:S(2)}) %collective-permute-start.1) | collective-permute-done | bytes 133152 | tf_op jit(solution)/shard_map/ppermute | solution.py:444
  18.6 0.0 collective-permute-start.6
  18.6 0.0 collective-permute-done.2.refs_2_.refs_3_
  18.6 1.1 %collective-permute-start.7 = (bf16[520,128]{1,0:T(8,128)(2,1)S(1)}, bf16[520,128]{1,0:T(8,128)(2,1)S(1)}, u32[]{:S(2)}, u32[]{:S(2)}) collective-permute-start(bf16[520,128]{1,0:T(8,128)(2,1)S(1)} %shard_map.91.refs_1_), channel_id=1, source_target_pairs={{0,24},{2,26},{4,28},{6,30},{8,16},{10,18},{12,20},{14,22},{16,8},... | collective-permute-start | bytes 399368 | tf_op jit(solution)/shard_map/ppermute | solution.py:444
  19.7 0.7 %shard_map.92 = (f32[8208,128]{1,0:T(8,128)S(1)}, f32[8208,128]{1,0:T(8,128)S(1)}) custom-call(bf16[520,128]{1,0:T(8,128)(2,1)S(1)} %get-tuple-element.35.refs_0_, bf16[520,128]{1,0:T(8,128)(2,1)S(1)} %collective-permute-done.refs_1_, bf16[520,128]{1,0:T(8,128)(2,1)S(1)} %collective-permute-done.1.refs_2_, ...), custom_call_target="tpu_custom_call" | custom-call | tf_op jit(solution)/shard_map/pallas_call | solution.py:370
  20.4 0.0 collective-permute-done.3.refs_2_.refs_0_.refs_4_
  20.4 1.7 %collective-permute-start.8 = (bf16[520,128]{1,0:T(8,128)(2,1)S(1)}, bf16[520,128]{1,0:T(8,128)(2,1)S(1)}, u32[]{:S(2)}, u32[]{:S(2)}) collective-permute-start(bf16[520,128]{1,0:T(8,128)(2,1)S(1)} %shard_map.93.refs_1_), channel_id=1, source_target_pairs={{0,6},{2,4},{4,2},{6,0},{8,14},{10,12},{12,10},{14,8},{16,22},{18,... | collective-permute-start | bytes 399368 | tf_op jit(solution)/shard_map/ppermute | solution.py:444
  22.1 0.0 collective-permute-done.4.refs_2_.refs_1_.refs_5_
  22.1 3.3 %collective-permute-start.9 = (bf16[520,128]{1,0:T(8,128)(2,1)S(1)}, bf16[520,128]{1,0:T(8,128)(2,1)S(1)}, u32[]{:S(2)}, u32[]{:S(2)}) collective-permute-start(bf16[520,128]{1,0:T(8,128)(2,1)S(1)} %shard_map.94.refs_1_), channel_id=1, source_target_pairs={{0,22},{2,20},{4,18},{6,16},{8,30},{10,28},{12,26},{14,24},{16,6},... | collective-permute-start | bytes 399368 | tf_op jit(solution)/shard_map/ppermute | solution.py:444
  25.4 1.2 %collective-permute-start.10 = (bf16[520,128]{1,0:T(8,128)(2,1)S(1)}, bf16[520,128]{1,0:T(8,128)(2,1)S(1)}, u32[]{:S(2)}, u32[]{:S(2)}) collective-permute-start(bf16[520,128]{1,0:T(8,128)(2,1)S(1)} %shard_map.95.refs_1_), channel_id=1, source_target_pairs={{0,18},{2,16},{4,22},{6,20},{8,26},{10,24},{12,30},{14,28},{16,2},... | collective-permute-start | bytes 399368 | tf_op jit(solution)/shard_map/ppermute | solution.py:444
  26.6 0.0 collective-permute-done.6.refs_2_.refs_3_.refs_7_
  26.6 2.6 %collective-permute-start.11 = (bf16[520,128]{1,0:T(8,128)(2,1)S(1)}, bf16[520,128]{1,0:T(8,128)(2,1)S(1)}, u32[]{:S(2)}, u32[]{:S(2)}) collective-permute-start(bf16[520,128]{1,0:T(8,128)(2,1)S(1)} %shard_map.96.refs_1_), channel_id=1, source_target_pairs={{0,14},{2,12},{4,10},{6,8},{8,6},{10,4},{12,2},{14,0},{16,30},{18,... | collective-permute-start | bytes 399368 | tf_op jit(solution)/shard_map/ppermute | solution.py:444
  29.2 0.7 %shard_map.97 = (f32[8208,128]{1,0:T(8,128)S(1)}, f32[8208,128]{1,0:T(8,128)S(1)}) custom-call(bf16[520,128]{1,0:T(8,128)(2,1)S(1)} %collective-permute-done.3.refs_2_.refs_0_.refs_4_, bf16[520,128]{1,0:T(8,128)(2,1)S(1)} %collective-permute-done.4.refs_2_.refs_1_.refs_5_, ...), custom_call_target="tpu_custom_call", output_to_operand_aliasing={{0}: (5, {}), {1}: (6, {})} | custom-call | tf_op jit(solution)/shard_map/pallas_call | solution.py:370
  29.9 4.1 %collective-permute-done.7.refs_2_.refs_8_ = bf16[520,128]{1,0:T(8,128)(2,1)S(1)} collective-permute-done((bf16[520,128]{1,0:T(8,128)(2,1)S(1)}, bf16[520,128]{1,0:T(8,128)(2,1)S(1)}, u32[]{:S(2)}, u32[]{:S(2)}) %collective-permute-start.7) | collective-permute-done | bytes 133152 | tf_op jit(solution)/shard_map/ppermute | solution.py:444
  34.0 0.0 collective-permute-start.12
  34.0 0.0 collective-permute-done.8.refs_2_.refs_9_
  34.0 3.4 %collective-permute-start.13 = (bf16[520,128]{1,0:T(8,128)(2,1)S(1)}, bf16[520,128]{1,0:T(8,128)(2,1)S(1)}, u32[]{:S(2)}, u32[]{:S(2)}) collective-permute-start(bf16[520,128]{1,0:T(8,128)(2,1)S(1)} %shard_map.99.refs_1_), channel_id=1, source_target_pairs={{0,20},{2,22},{4,16},{6,18},{8,28},{10,30},{12,24},{14,26},{16,4},... | collective-permute-start | bytes 399368 | tf_op jit(solution)/shard_map/ppermute | solution.py:444
  37.5 2.8 %shard_map.100 = (f32[8208,128]{1,0:T(8,128)S(1)}, f32[8208,128]{1,0:T(8,128)S(1)}, f32[8192,128]{1,0:T(8,128)S(1)}) custom-call(bf16[520,128]{1,0:T(8,128)(2,1)S(1)} %get-tuple-element.35.refs_0_, bf16[520,128]{1,0:T(8,128)(2,1)S(1)} %collective-permute-done.refs_1_, ...), custom_call_target="tpu_custom_call", output_to_operand_aliasing={{0}: (15, {}), {1}: (16, {})} | custom-call | tf_op jit(solution)/shard_map/pallas_call | solution.py:408
  40.3 0.0 collective-permute-done.9.refs_2_.refs_10_
  40.3 0.1 collective-permute-start.14
  40.4 0.0 collective-permute-done.12.refs_13_
  40.4 0.0 collective-permute-done.11.refs_12_
  40.4 2.6 %collective-permute-done.10.refs_11_ = bf16[520,128]{1,0:T(8,128)(2,1)S(1)} collective-permute-done((bf16[520,128]{1,0:T(8,128)(2,1)S(1)}, bf16[520,128]{1,0:T(8,128)(2,1)S(1)}, u32[]{:S(2)}, u32[]{:S(2)}) %collective-permute-start.10) | collective-permute-done | bytes 133152 | tf_op jit(solution)/shard_map/ppermute | solution.py:444
  43.0 2.4 %shard_map.102 = (f32[8208,128]{1,0:T(8,128)S(1)}, f32[8208,128]{1,0:T(8,128)S(1)}, f32[8192,128]{1,0:T(8,128)S(1)}) custom-call(bf16[520,128]{1,0:T(8,128)(2,1)S(1)} %get-tuple-element.35.refs_0_, bf16[520,128]{1,0:T(8,128)(2,1)S(1)} %collective-permute-done.refs_1_, ...), custom_call_target="tpu_custom_call", output_to_operand_aliasing={{0}: (19, {}), {1}: (20, {}), {2}: (21, {})} | custom-call | tf_op jit(solution)/shard_map/pallas_call | solution.py:408
  45.4 3.3 %collective-permute-done.13.refs_14_ = bf16[520,128]{1,0:T(8,128)(2,1)S(1)} collective-permute-done((bf16[520,128]{1,0:T(8,128)(2,1)S(1)}, bf16[520,128]{1,0:T(8,128)(2,1)S(1)}, u32[]{:S(2)}, u32[]{:S(2)}) %collective-permute-start.13) | collective-permute-done | bytes 133152 | tf_op jit(solution)/shard_map/ppermute | solution.py:444
  48.7 3.3 %collective-permute-done.14.refs_15_ = bf16[520,128]{1,0:T(8,128)(2,1)S(1)} collective-permute-done((bf16[520,128]{1,0:T(8,128)(2,1)S(1)}, bf16[520,128]{1,0:T(8,128)(2,1)S(1)}, u32[]{:S(2)}, u32[]{:S(2)}) %collective-permute-start.14) | collective-permute-done | bytes 133152 | tf_op jit(solution)/shard_map/ppermute | solution.py:444
  52.0 2.4 %shard_map.103 = (f32[16,128]{1,0:T(8,128)S(1)}, f32[4,128]{1,0:T(4,128)S(1)}, f32[4,128]{1,0:T(4,128)S(1)}, f32[8208,128]{1,0:T(8,128)S(1)}, f32[8208,128]{1,0:T(8,128)S(1)}, /*index=5*/f32[8192,128]{1,0:T(8,128)S(1)}) custom-call(bf16[520,128]{1,0:T(8,128)(2,1)S(1)} %get-tuple-element.35.refs_0_, ...), custom_call_target="tpu_custom_call", output_to_operand_aliasing={{3}: (23, {}), {4}: (24, {}), {5}: (25, {})} | custom-call | tf_op jit(solution)/shard_map/pallas_call | solution.py:457
  54.4 2.5 %collective-permute-start.15 = (f32[4,128]{1,0:T(4,128)S(1)}, f32[4,128]{1,0:T(4,128)S(1)}, u32[]{:S(2)}, u32[]{:S(2)}) collective-permute-start(f32[4,128]{1,0:T(4,128)S(1)} %get-tuple-element.67), channel_id=1, source_target_pairs={{0,1},{1,0},{2,3},{3,2},{4,5},{5,4},{6,7},{7,6},{8,9},{9,8},{10,11... | collective-permute-start | bytes 6152 | tf_op jit(solution)/shard_map/ppermute | solution.py:482
  56.9 0.6 %shard_map.104 = f32[16,128]{1,0:T(8,128)} custom-call(f32[16,128]{1,0:T(8,128)S(1)} %get-tuple-element.65.array_ref), custom_call_target="tpu_custom_call" | custom-call | tf_op jit(solution)/shard_map/pallas_call | solution.py:479
  57.5 0.2 collective-permute-done.15
  57.7 0.6 add_bitcast_fusion
  (17 shorter events, 0.0 us)
Async XLA Ops:
  0.6 1.2 %copy-start = (bf16[8,128,512]{2,1,0:T(8,128)(2,1)S(1)}, bf16[8,128,512]{2,1,0:T(8,128)(2,1)}, u32[]{:S(2)}) copy-start(bf16[8,128,512]{2,1,0:T(8,128)(2,1)} %embedding_ref.1) | copy-start | bytes 3145732
  1.9 0.7 %copy-start.2 = (s32[1,1,16]{2,1,0:T(1,128)S(1)}, s32[1,1,16]{2,1,0:T(1,128)}, u32[]{:S(2)}) copy-start(s32[1,1,16]{2,1,0:T(1,128)} %wanted_ref.1) | copy-start | bytes 196
  3.5 10.6 %collective-permute-start = (bf16[520,128]{1,0:T(8,128)(2,1)S(1)}, bf16[520,128]{1,0:T(8,128)(2,1)S(1)}, u32[]{:S(2)}, u32[]{:S(2)}) collective-permute-start(bf16[520,128]{1,0:T(8,128)(2,1)S(1)} %get-tuple-element.36), channel_id=1, source_target_pairs={{0,30},{2,28},{4,26},{6,24},{8,22},{10,20},{12,18},{14,16},{16,14}... | collective-permute-start | bytes 399368 | tf_op jit(solution)/shard_map/ppermute | solution.py:444
  6.7 11.9 %collective-permute-start.1 = (bf16[520,128]{1,0:T(8,128)(2,1)S(1)}, bf16[520,128]{1,0:T(8,128)(2,1)S(1)}, u32[]{:S(2)}, u32[]{:S(2)}) collective-permute-start(bf16[520,128]{1,0:T(8,128)(2,1)S(1)} %get-tuple-element.37), channel_id=1, source_target_pairs={{0,28},{2,30},{4,24},{6,26},{8,20},{10,22},{12,16},{14,18},{16,12}... | collective-permute-start | bytes 399368 | tf_op jit(solution)/shard_map/ppermute | solution.py:444
  6.8 11.8 %collective-permute-start.2 = (bf16[520,128]{1,0:T(8,128)(2,1)S(1)}, bf16[520,128]{1,0:T(8,128)(2,1)S(1)}, u32[]{:S(2)}, u32[]{:S(2)}) collective-permute-start(bf16[520,128]{1,0:T(8,128)(2,1)S(1)} %get-tuple-element.38), channel_id=1, source_target_pairs={{0,2},{2,0},{4,6},{6,4},{8,10},{10,8},{12,14},{14,12},{16,18},{18,... | collective-permute-start | bytes 399368 | tf_op jit(solution)/shard_map/ppermute | solution.py:444
  7.1 13.3 %collective-permute-start.3 = (bf16[520,128]{1,0:T(8,128)(2,1)S(1)}, bf16[520,128]{1,0:T(8,128)(2,1)S(1)}, u32[]{:S(2)}, u32[]{:S(2)}) collective-permute-start(bf16[520,128]{1,0:T(8,128)(2,1)S(1)} %get-tuple-element.39), channel_id=1, source_target_pairs={{0,4},{2,6},{4,0},{6,2},{8,12},{10,14},{12,8},{14,10},{16,20},{18,... | collective-permute-start | bytes 399368 | tf_op jit(solution)/shard_map/ppermute | solution.py:444
  8.3 13.8 %collective-permute-start.4 = (bf16[520,128]{1,0:T(8,128)(2,1)S(1)}, bf16[520,128]{1,0:T(8,128)(2,1)S(1)}, u32[]{:S(2)}, u32[]{:S(2)}) collective-permute-start(bf16[520,128]{1,0:T(8,128)(2,1)S(1)} %get-tuple-element.40), channel_id=1, source_target_pairs={{0,10},{2,8},{4,14},{6,12},{8,2},{10,0},{12,6},{14,4},{16,26},{18,... | collective-permute-start | bytes 399368 | tf_op jit(solution)/shard_map/ppermute | solution.py:444
  12.7 1.2 %copy-start.1 = (bf16[1024,512]{1,0:T(8,128)(2,1)S(1)}, bf16[1024,512]{1,0:T(8,128)(2,1)}, u32[]{:S(2)}) copy-start(bf16[1024,512]{1,0:T(8,128)(2,1)} %param.11) | copy-start | bytes 3145732
  14.0 11.3 %copy-start.4 = (bf16[512]{0:T(512)(128)(2,1)S(1)}, bf16[512]{0:T(512)(128)(2,1)}, u32[]{:S(2)}) copy-start(bf16[512]{0:T(512)(128)(2,1)} %param.13) | copy-start | bytes 3076
  14.0 11.3 %copy-start.3 = (f32[512]{0:T(512)S(1)}, f32[512]{0:T(512)}, u32[]{:S(2)}) copy-start(f32[512]{0:T(512)} %param.12) | copy-start | bytes 6148
  14.1 11.3 %collective-permute-start.5 = (bf16[520,128]{1,0:T(8,128)(2,1)S(1)}, bf16[520,128]{1,0:T(8,128)(2,1)S(1)}, u32[]{:S(2)}, u32[]{:S(2)}) collective-permute-start(bf16[520,128]{1,0:T(8,128)(2,1)S(1)} %shard_map.88.refs_1_), channel_id=1, source_target_pairs={{0,16},{2,18},{4,20},{6,22},{8,24},{10,26},{12,28},{14,30},{16,0},... | collective-permute-start | bytes 399368 | tf_op jit(solution)/shard_map/ppermute | solution.py:444
  18.6 8.0 %collective-permute-start.6 = (bf16[520,128]{1,0:T(8,128)(2,1)S(1)}, bf16[520,128]{1,0:T(8,128)(2,1)S(1)}, u32[]{:S(2)}, u32[]{:S(2)}) collective-permute-start(bf16[520,128]{1,0:T(8,128)(2,1)S(1)} %shard_map.90.refs_1_), channel_id=1, source_target_pairs={{0,8},{2,10},{4,12},{6,14},{8,0},{10,2},{12,4},{14,6},{16,24},{18,... | collective-permute-start | bytes 399368 | tf_op jit(solution)/shard_map/ppermute | solution.py:444
  18.6 15.4 %collective-permute-start.7 = (bf16[520,128]{1,0:T(8,128)(2,1)S(1)}, bf16[520,128]{1,0:T(8,128)(2,1)S(1)}, u32[]{:S(2)}, u32[]{:S(2)}) collective-permute-start(bf16[520,128]{1,0:T(8,128)(2,1)S(1)} %shard_map.91.refs_1_), channel_id=1, source_target_pairs={{0,24},{2,26},{4,28},{6,30},{8,16},{10,18},{12,20},{14,22},{16,8},... | collective-permute-start | bytes 399368 | tf_op jit(solution)/shard_map/ppermute | solution.py:444
  20.4 13.6 %collective-permute-start.8 = (bf16[520,128]{1,0:T(8,128)(2,1)S(1)}, bf16[520,128]{1,0:T(8,128)(2,1)S(1)}, u32[]{:S(2)}, u32[]{:S(2)}) collective-permute-start(bf16[520,128]{1,0:T(8,128)(2,1)S(1)} %shard_map.93.refs_1_), channel_id=1, source_target_pairs={{0,6},{2,4},{4,2},{6,0},{8,14},{10,12},{12,10},{14,8},{16,22},{18,... | collective-permute-start | bytes 399368 | tf_op jit(solution)/shard_map/ppermute | solution.py:444
  22.1 18.2 %collective-permute-start.9 = (bf16[520,128]{1,0:T(8,128)(2,1)S(1)}, bf16[520,128]{1,0:T(8,128)(2,1)S(1)}, u32[]{:S(2)}, u32[]{:S(2)}) collective-permute-start(bf16[520,128]{1,0:T(8,128)(2,1)S(1)} %shard_map.94.refs_1_), channel_id=1, source_target_pairs={{0,22},{2,20},{4,18},{6,16},{8,30},{10,28},{12,26},{14,24},{16,6},... | collective-permute-start | bytes 399368 | tf_op jit(solution)/shard_map/ppermute | solution.py:444
  25.4 17.6 %collective-permute-start.10 = (bf16[520,128]{1,0:T(8,128)(2,1)S(1)}, bf16[520,128]{1,0:T(8,128)(2,1)S(1)}, u32[]{:S(2)}, u32[]{:S(2)}) collective-permute-start(bf16[520,128]{1,0:T(8,128)(2,1)S(1)} %shard_map.95.refs_1_), channel_id=1, source_target_pairs={{0,18},{2,16},{4,22},{6,20},{8,26},{10,24},{12,30},{14,28},{16,2},... | collective-permute-start | bytes 399368 | tf_op jit(solution)/shard_map/ppermute | solution.py:444
  26.6 13.8 %collective-permute-start.11 = (bf16[520,128]{1,0:T(8,128)(2,1)S(1)}, bf16[520,128]{1,0:T(8,128)(2,1)S(1)}, u32[]{:S(2)}, u32[]{:S(2)}) collective-permute-start(bf16[520,128]{1,0:T(8,128)(2,1)S(1)} %shard_map.96.refs_1_), channel_id=1, source_target_pairs={{0,14},{2,12},{4,10},{6,8},{8,6},{10,4},{12,2},{14,0},{16,30},{18,... | collective-permute-start | bytes 399368 | tf_op jit(solution)/shard_map/ppermute | solution.py:444
  34.0 6.4 %collective-permute-start.12 = (bf16[520,128]{1,0:T(8,128)(2,1)S(1)}, bf16[520,128]{1,0:T(8,128)(2,1)S(1)}, u32[]{:S(2)}, u32[]{:S(2)}) collective-permute-start(bf16[520,128]{1,0:T(8,128)(2,1)S(1)} %shard_map.98.refs_1_), channel_id=1, source_target_pairs={{0,12},{2,14},{4,8},{6,10},{8,4},{10,6},{12,0},{14,2},{16,28},{18,... | collective-permute-start | bytes 399368 | tf_op jit(solution)/shard_map/ppermute | solution.py:444
  34.0 14.7 %collective-permute-start.13 = (bf16[520,128]{1,0:T(8,128)(2,1)S(1)}, bf16[520,128]{1,0:T(8,128)(2,1)S(1)}, u32[]{:S(2)}, u32[]{:S(2)}) collective-permute-start(bf16[520,128]{1,0:T(8,128)(2,1)S(1)} %shard_map.99.refs_1_), channel_id=1, source_target_pairs={{0,20},{2,22},{4,16},{6,18},{8,28},{10,30},{12,24},{14,26},{16,4},... | collective-permute-start | bytes 399368 | tf_op jit(solution)/shard_map/ppermute | solution.py:444
  40.3 11.6 %collective-permute-start.14 = (bf16[520,128]{1,0:T(8,128)(2,1)S(1)}, bf16[520,128]{1,0:T(8,128)(2,1)S(1)}, u32[]{:S(2)}, u32[]{:S(2)}) collective-permute-start(bf16[520,128]{1,0:T(8,128)(2,1)S(1)} %shard_map.101), channel_id=1, source_target_pairs={{0,26},{2,24},{4,30},{6,28},{8,18},{10,16},{12,22},{14,20},{16,10}... | collective-permute-start | bytes 399368 | tf_op jit(solution)/shard_map/ppermute | solution.py:444
  54.4 3.3 %collective-permute-start.15 = (f32[4,128]{1,0:T(4,128)S(1)}, f32[4,128]{1,0:T(4,128)S(1)}, u32[]{:S(2)}, u32[]{:S(2)}) collective-permute-start(f32[4,128]{1,0:T(4,128)S(1)} %get-tuple-element.67), channel_id=1, source_target_pairs={{0,1},{1,0},{2,3},{3,2},{4,5},{5,4},{6,7},{7,6},{8,9},{9,8},{10,11... | collective-permute-start | bytes 6152 | tf_op jit(solution)/shard_map/ppermute | solution.py:482

commit v7 on v6

--- a/solution.py
+++ b/solution.py
@@ -13,7 +13,7 @@
 LABEL_ROWS = 8
 IN_FLIGHT = 5
 SORT_AT = 6
-LATE = (6, 2)
+LATE = (6, 2, 1)
 CHUNK = 4
 GELU_A = 0.7978845608028654
 GELU_B = GELU_A * 0.044715
@@ -306,7 +306,7 @@
 
 def offsets_in_order(node_count):
     if node_count == 16:
-        return [15, 14, 1, 2, 5, 8, 4, 12, 3, 11, 9, 7, 6, 10, 13]
+        return [14, 15, 1, 2, 5, 8, 4, 12, 3, 11, 9, 7, 6, 10, 13]
     half = node_count // 2
     order = []
     for place in range(half):
@@ -355,7 +355,7 @@
         in_specs=[smem, smem, vmem],
         out_specs=(vmem,) * node_count,
         compiler_params=params,
-    )(node_self, send_list, embedding)
+    )(node_self, jnp.maximum(send_list, -1), embedding)
 
     weight = w_first.reshape(2, feature_width, hidden_width)
     bias = b_first.reshape(parts, LANES)
@@ -425,7 +425,7 @@
         if place >= IN_FLIGHT:
             landed = order[place - IN_FLIGHT]
             behind = behind + [arrived[landed]]
-            if place == IN_FLIGHT:
+            if place == IN_FLIGHT + 1:
                 behind = behind + [weight]
             if place == SORT_AT:
                 behind = behind + [ends]
@@ -446,11 +446,12 @@
     last = (waiting + order[-IN_FLIGHT:]) if staged else landing
     chunks = [last[start : start + CHUNK] for start in range(0, len(last), CHUNK)]
     if staged:
-        chunks = [last[-2:]]
-        if stage < len(late_stages):
-            passed = score_early(stage, last[:-2], passed)
-        else:
-            passed = [*add_to_tables(last[:-2], passed[:2]), passed[2]]
+        while stage < len(late_stages):
+            chunk = [slot for slot in last if slot not in late_stages[stage]]
+            last = late_stages[stage]
+            passed = score_early(stage, chunk, passed)
+            stage += 1
+        chunks = [last]
 
     paired = lax.axis_size("edge") == 2
     half_pool = jax.ShapeDtypeStruct((PAIRS_ROW // LANES // 2, LANES), jnp.float32)

time: 58.6 us -> 58.5 us (level)
  waiting for transfers between devices: 16.8 us -> 13.9 us
  starting transfers between devices: 24.8 us -> 26.3 us
  Pallas kernels: 11.4 us -> 12.2 us
  other arithmetic: 1.34 us -> 2 us
  local copies, waits for them, and re-layouts: 3.11 us -> 2.45 us
    ppermute x15, waiting for transfers between devices: 16.6 us -> 13.7 us  [body(): lax.ppermute(operand, 'node', [(node, node ^ offset) for node in range(no...]
    ppermute x15, starting transfers between devices: 22.3 us -> 24.7 us  [body(): lax.ppermute(operand, 'node', [(node, node ^ offset) for node in range(no...]
    pallas_call x2 -> x3, Pallas kernels: 5.2 us -> 6.41 us  [score_early(): pl.pallas_call(functools.partial(early_scorer, stage, slots, chunk, node_...]
    ppermute x1, starting transfers between devices: 2.46 us -> 1.6 us  [body(): lax.ppermute(other, 'edge', [(0, 1), (1, 0)])]
    max x0 -> x1, other arithmetic: none -> 0.66 us  [body(): jnp.maximum(send_list, -1)]
    unnamed x10 -> x8, local copies, waits for them, and re-layouts: 3.11 us -> 2.45 us
  transfers between devices with their start and end apart: 16 -> 16, of which waited for: 6 -> 5; matrix products, arithmetic and copies ran while one was open for 1% -> 1% of each run, Pallas kernels for 14% -> 16%
where the time goes in v7:
time: 58.5 us; the launch traced here: 57.7 us
  starting transfers between devices  26.3 us (45%)
  waiting for transfers between devices  13.9 us (24%)
  Pallas kernels  12.2 us (21%)
  local copies, waits for them, and re-layouts  2.45 us (4%)
  other arithmetic  2 us (3%)
  between operations  0.87 us (1%)
    ppermute x15, starting transfers between devices, body(): lax.ppermute(operand, 'node', [(node, node ^ offset) for node in range(no...  24.7 us
    ppermute x15, waiting for transfers between devices, body(): lax.ppermute(operand, 'node', [(node, node ^ offset) for node in range(no...  13.7 us
    pallas_call x3, Pallas kernels, score_early(): pl.pallas_call(functools.partial(early_scorer, stage, slots, chunk, node_...  6.41 us
    unnamed x8, local copies, waits for them, and re-layouts  2.45 us
    pallas_call x1, Pallas kernels, body(): pl.pallas_call(functools.partial(scorer, landing, chunks, staged, blocks_...  1.87 us
    ppermute x1, starting transfers between devices, body(): lax.ppermute(other, 'edge', [(0, 1), (1, 0)])  1.6 us
    pallas_call x2, Pallas kernels, add_to_tables(): pl.pallas_call(functools.partial(projector, slots, not tables), out_shape...  1.41 us
  transfers between devices with their start and end apart: 16, of which 5 were waited for; matrix products, arithmetic and copies ran while one was open for 1% of the time, Pallas kernels for 16%

profile of v7, /device:TPU:9, one launch (start us, length us, event | category | flops | bytes accessed | tf_op | source)
XLA Modules:
  0.0 57.7 jit_solution(12622181461305237090)
XLA Ops:
  0.6 0.7 %broadcast_maximum_fusion.wanted_ref = s32[1,1,16]{2,1,0:T(1,128)S(1)} fusion(s32[1,1,16]{2,1,0:T(1,128)} %param.8), kind=kLoop, calls=%fused_computation.4 | loop fusion | flops 16 | bytes 128 | tf_op jit(solution)/shard_map/max | solution.py:358
  1.3 1.2 %copy-done = bf16[8,128,512]{2,1,0:T(8,128)(2,1)S(1)} copy-done((bf16[8,128,512]{2,1,0:T(8,128)(2,1)S(1)}, bf16[8,128,512]{2,1,0:T(8,128)(2,1)}, u32[]{:S(2)}) %copy-start) | copy-done | bytes 1048600
  2.5 0.9 %shard_map.86 = (bf16[520,128]{1,0:T(8,128)(2,1)S(1)}, bf16[520,128]{1,0:T(8,128)(2,1)S(1)}, bf16[520,128]{1,0:T(8,128)(2,1)S(1)}, bf16[520,128]{1,0:T(8,128)(2,...) custom-call(s32[1]{0:T(128)} %bitcast.node_ref.refs_10_.refs_14_.ref, ...), custom_call_target="tpu_custom_call" | custom-call | tf_op jit(solution)/shard_map/pallas_call | solution.py:352
  3.5 2.3 %collective-permute-start = (bf16[520,128]{1,0:T(8,128)(2,1)S(1)}, bf16[520,128]{1,0:T(8,128)(2,1)S(1)}, u32[]{:S(2)}, u32[]{:S(2)}) collective-permute-start(bf16[520,128]{1,0:T(8,128)(2,1)S(1)} %get-tuple-element.39), channel_id=1, source_target_pairs={{0,28},{2,30},{4,24},{6,26},{8,20},{10,22},{12,16},{14,18},{16,12}... | collective-permute-start | bytes 399368 | tf_op jit(solution)/shard_map/ppermute | solution.py:444
  5.8 1.0 %collective-permute-start.1 = (bf16[520,128]{1,0:T(8,128)(2,1)S(1)}, bf16[520,128]{1,0:T(8,128)(2,1)S(1)}, u32[]{:S(2)}, u32[]{:S(2)}) collective-permute-start(bf16[520,128]{1,0:T(8,128)(2,1)S(1)} %get-tuple-element.40), channel_id=1, source_target_pairs={{0,30},{2,28},{4,26},{6,24},{8,22},{10,20},{12,18},{14,16},{16,14}... | collective-permute-start | bytes 399368 | tf_op jit(solution)/shard_map/ppermute | solution.py:444
  6.8 0.3 collective-permute-start.2
  7.1 1.2 %collective-permute-start.3 = (bf16[520,128]{1,0:T(8,128)(2,1)S(1)}, bf16[520,128]{1,0:T(8,128)(2,1)S(1)}, u32[]{:S(2)}, u32[]{:S(2)}) collective-permute-start(bf16[520,128]{1,0:T(8,128)(2,1)S(1)} %get-tuple-element.42), channel_id=1, source_target_pairs={{0,4},{2,6},{4,0},{6,2},{8,12},{10,14},{12,8},{14,10},{16,20},{18,... | collective-permute-start | bytes 399368 | tf_op jit(solution)/shard_map/ppermute | solution.py:444
  8.3 2.9 %collective-permute-start.4 = (bf16[520,128]{1,0:T(8,128)(2,1)S(1)}, bf16[520,128]{1,0:T(8,128)(2,1)S(1)}, u32[]{:S(2)}, u32[]{:S(2)}) collective-permute-start(bf16[520,128]{1,0:T(8,128)(2,1)S(1)} %get-tuple-element.43), channel_id=1, source_target_pairs={{0,10},{2,8},{4,14},{6,12},{8,2},{10,0},{12,6},{14,4},{16,26},{18,... | collective-permute-start | bytes 399368 | tf_op jit(solution)/shard_map/ppermute | solution.py:444
  11.2 0.8 %pad_add_fusion.edges_ref = s32[3,2048]{1,0:T(4,128)S(1)} fusion(s32[1,2048]{1,0:T(1,128)} %bitcast.11, s32[2,2048]{1,0:T(2,128)} %param.9), kind=kLoop, calls=%fused_computation | loop fusion | flops 6144 | bytes 49152 | tf_op jit(solution)/shard_map/concatenate | solution.py:364
  12.0 0.9 %shard_map.89 = (s32[32,128]{1,0:T(8,128)S(1)}, s32[1,2048]{1,0:T(1,128)S(1)}, s32[1,2048]{1,0:T(1,128)S(1)}, f32[24,128]{1,0:T(8,128)S(1)}) custom-call(s32[1]{0:T(128)} %bitcast.node_ref.refs_10_.refs_14_.refs_15_.refs_16_, s32[3,2048]{1,0:T(4,128)S(1)} %pad_add_fusion.edges_ref), custom_call_target="tpu_custom_call" | custom-call | tf_op jit(solution)/shard_map/pallas_call | solution.py:385
  12.9 0.0 copy-start.1
  12.9 1.2 %copy-done.1 = bf16[1024,512]{1,0:T(8,128)(2,1)S(1)} copy-done((bf16[1024,512]{1,0:T(8,128)(2,1)S(1)}, bf16[1024,512]{1,0:T(8,128)(2,1)}, u32[]{:S(2)}) %copy-start.1) | copy-done | bytes 1048600
  14.1 0.1 shard_map.88.refs_3_.refs_4_.refs_13_.refs_17_.refs_18_.refs_21_
  14.2 0.0 collective-permute-done.refs_1_
  14.2 1.3 %collective-permute-start.5 = (bf16[520,128]{1,0:T(8,128)(2,1)S(1)}, bf16[520,128]{1,0:T(8,128)(2,1)S(1)}, u32[]{:S(2)}, u32[]{:S(2)}) collective-permute-start(bf16[520,128]{1,0:T(8,128)(2,1)S(1)} %shard_map.87.refs_1_), channel_id=1, source_target_pairs={{0,16},{2,18},{4,20},{6,22},{8,24},{10,26},{12,28},{14,30},{16,0},... | collective-permute-start | bytes 399368 | tf_op jit(solution)/shard_map/ppermute | solution.py:444
  15.5 3.7 %collective-permute-done.1.refs_2_ = bf16[520,128]{1,0:T(8,128)(2,1)S(1)} collective-permute-done((bf16[520,128]{1,0:T(8,128)(2,1)S(1)}, bf16[520,128]{1,0:T(8,128)(2,1)S(1)}, u32[]{:S(2)}, u32[]{:S(2)}) %collective-permute-start.1) | collective-permute-done | bytes 133152 | tf_op jit(solution)/shard_map/ppermute | solution.py:444
  19.1 0.0 collective-permute-start.6
  19.1 0.0 collective-permute-done.2.refs_2_.refs_3_
  19.2 0.9 %collective-permute-start.7 = (bf16[520,128]{1,0:T(8,128)(2,1)S(1)}, bf16[520,128]{1,0:T(8,128)(2,1)S(1)}, u32[]{:S(2)}, u32[]{:S(2)}) collective-permute-start(bf16[520,128]{1,0:T(8,128)(2,1)S(1)} %shard_map.91.refs_1_), channel_id=1, source_target_pairs={{0,24},{2,26},{4,28},{6,30},{8,16},{10,18},{12,20},{14,22},{16,8},... | collective-permute-start | bytes 399368 | tf_op jit(solution)/shard_map/ppermute | solution.py:444
  20.1 0.7 %shard_map.92 = (f32[8208,128]{1,0:T(8,128)S(1)}, f32[8208,128]{1,0:T(8,128)S(1)}) custom-call(bf16[520,128]{1,0:T(8,128)(2,1)S(1)} %get-tuple-element.38.refs_0_, bf16[520,128]{1,0:T(8,128)(2,1)S(1)} %collective-permute-done.refs_1_, bf16[520,128]{1,0:T(8,128)(2,1)S(1)} %collective-permute-done.1.refs_2_, ...), custom_call_target="tpu_custom_call" | custom-call | tf_op jit(solution)/shard_map/pallas_call | solution.py:370
  20.8 0.0 collective-permute-done.3.refs_2_.refs_0_.refs_4_
  20.8 1.2 %collective-permute-start.8 = (bf16[520,128]{1,0:T(8,128)(2,1)S(1)}, bf16[520,128]{1,0:T(8,128)(2,1)S(1)}, u32[]{:S(2)}, u32[]{:S(2)}) collective-permute-start(bf16[520,128]{1,0:T(8,128)(2,1)S(1)} %shard_map.93.refs_1_), channel_id=1, source_target_pairs={{0,6},{2,4},{4,2},{6,0},{8,14},{10,12},{12,10},{14,8},{16,22},{18,... | collective-permute-start | bytes 399368 | tf_op jit(solution)/shard_map/ppermute | solution.py:444
  22.0 0.0 collective-permute-done.4.refs_2_.refs_1_.refs_5_
  22.0 3.5 %collective-permute-start.9 = (bf16[520,128]{1,0:T(8,128)(2,1)S(1)}, bf16[520,128]{1,0:T(8,128)(2,1)S(1)}, u32[]{:S(2)}, u32[]{:S(2)}) collective-permute-start(bf16[520,128]{1,0:T(8,128)(2,1)S(1)} %shard_map.94.refs_1_), channel_id=1, source_target_pairs={{0,22},{2,20},{4,18},{6,16},{8,30},{10,28},{12,26},{14,24},{16,6},... | collective-permute-start | bytes 399368 | tf_op jit(solution)/shard_map/ppermute | solution.py:444
  25.6 0.0 collective-permute-done.5.refs_2_.refs_6_
  25.6 1.0 %collective-permute-start.10 = (bf16[520,128]{1,0:T(8,128)(2,1)S(1)}, bf16[520,128]{1,0:T(8,128)(2,1)S(1)}, u32[]{:S(2)}, u32[]{:S(2)}) collective-permute-start(bf16[520,128]{1,0:T(8,128)(2,1)S(1)} %shard_map.95.refs_1_), channel_id=1, source_target_pairs={{0,18},{2,16},{4,22},{6,20},{8,26},{10,24},{12,30},{14,28},{16,2},... | collective-permute-start | bytes 399368 | tf_op jit(solution)/shard_map/ppermute | solution.py:444
  26.6 0.0 collective-permute-done.6.refs_2_.refs_3_.refs_7_
  26.6 2.8 %collective-permute-start.11 = (bf16[520,128]{1,0:T(8,128)(2,1)S(1)}, bf16[520,128]{1,0:T(8,128)(2,1)S(1)}, u32[]{:S(2)}, u32[]{:S(2)}) collective-permute-start(bf16[520,128]{1,0:T(8,128)(2,1)S(1)} %shard_map.96.refs_1_), channel_id=1, source_target_pairs={{0,14},{2,12},{4,10},{6,8},{8,6},{10,4},{12,2},{14,0},{16,30},{18,... | collective-permute-start | bytes 399368 | tf_op jit(solution)/shard_map/ppermute | solution.py:444
  29.4 0.7 %shard_map.97 = (f32[8208,128]{1,0:T(8,128)S(1)}, f32[8208,128]{1,0:T(8,128)S(1)}) custom-call(bf16[520,128]{1,0:T(8,128)(2,1)S(1)} %collective-permute-done.3.refs_2_.refs_0_.refs_4_, bf16[520,128]{1,0:T(8,128)(2,1)S(1)} %collective-permute-done.4.refs_2_.refs_1_.refs_5_, ...), custom_call_target="tpu_custom_call", output_to_operand_aliasing={{0}: (5, {}), {1}: (6, {})} | custom-call | tf_op jit(solution)/shard_map/pallas_call | solution.py:370
  30.1 0.0 collective-permute-done.7.refs_2_.refs_8_
  30.1 0.1 collective-permute-start.12
  30.2 0.0 collective-permute-done.8.refs_2_.refs_9_
  30.2 6.1 %collective-permute-start.13 = (bf16[520,128]{1,0:T(8,128)(2,1)S(1)}, bf16[520,128]{1,0:T(8,128)(2,1)S(1)}, u32[]{:S(2)}, u32[]{:S(2)}) collective-permute-start(bf16[520,128]{1,0:T(8,128)(2,1)S(1)} %shard_map.99.refs_1_), channel_id=1, source_target_pairs={{0,20},{2,22},{4,16},{6,18},{8,28},{10,30},{12,24},{14,26},{16,4},... | collective-permute-start | bytes 399368 | tf_op jit(solution)/shard_map/ppermute | solution.py:444
  36.3 4.3 %shard_map.100 = (f32[8208,128]{1,0:T(8,128)S(1)}, f32[8208,128]{1,0:T(8,128)S(1)}, f32[8192,128]{1,0:T(8,128)S(1)}) custom-call(bf16[520,128]{1,0:T(8,128)(2,1)S(1)} %get-tuple-element.38.refs_0_, bf16[520,128]{1,0:T(8,128)(2,1)S(1)} %collective-permute-done.refs_1_, ...), custom_call_target="tpu_custom_call", output_to_operand_aliasing={{0}: (15, {}), {1}: (16, {})} | custom-call | tf_op jit(solution)/shard_map/pallas_call | solution.py:408
  40.6 0.0 collective-permute-done.9.refs_2_.refs_10_
  40.6 0.1 collective-permute-start.14
  40.7 0.0 collective-permute-done.12.refs_13_
  40.7 0.0 collective-permute-done.11.refs_12_
  40.7 0.1 collective-permute-done.10.refs_11_
  40.9 1.4 %shard_map.102 = (f32[8208,128]{1,0:T(8,128)S(1)}, f32[8208,128]{1,0:T(8,128)S(1)}, f32[8192,128]{1,0:T(8,128)S(1)}) custom-call(bf16[520,128]{1,0:T(8,128)(2,1)S(1)} %get-tuple-element.38.refs_0_, bf16[520,128]{1,0:T(8,128)(2,1)S(1)} %collective-permute-done.refs_1_, ...), custom_call_target="tpu_custom_call", output_to_operand_aliasing={{0}: (19, {}), {1}: (20, {}), {2}: (21, {})} | custom-call | tf_op jit(solution)/shard_map/pallas_call | solution.py:408
  42.2 5.6 %collective-permute-done.13.refs_14_ = bf16[520,128]{1,0:T(8,128)(2,1)S(1)} collective-permute-done((bf16[520,128]{1,0:T(8,128)(2,1)S(1)}, bf16[520,128]{1,0:T(8,128)(2,1)S(1)}, u32[]{:S(2)}, u32[]{:S(2)}) %collective-permute-start.13) | collective-permute-done | bytes 133152 | tf_op jit(solution)/shard_map/ppermute | solution.py:444
  47.9 0.7 %shard_map.103 = (f32[8208,128]{1,0:T(8,128)S(1)}, f32[8208,128]{1,0:T(8,128)S(1)}, f32[8192,128]{1,0:T(8,128)S(1)}) custom-call(bf16[520,128]{1,0:T(8,128)(2,1)S(1)} %get-tuple-element.38.refs_0_, bf16[520,128]{1,0:T(8,128)(2,1)S(1)} %collective-permute-done.refs_1_, ...), custom_call_target="tpu_custom_call", output_to_operand_aliasing={{0}: (20, {}), {1}: (21, {}), {2}: (22, {})} | custom-call | tf_op jit(solution)/shard_map/pallas_call | solution.py:408
  48.6 4.3 %collective-permute-done.14.refs_15_ = bf16[520,128]{1,0:T(8,128)(2,1)S(1)} collective-permute-done((bf16[520,128]{1,0:T(8,128)(2,1)S(1)}, bf16[520,128]{1,0:T(8,128)(2,1)S(1)}, u32[]{:S(2)}, u32[]{:S(2)}) %collective-permute-start.14) | collective-permute-done | bytes 133152 | tf_op jit(solution)/shard_map/ppermute | solution.py:444
  52.9 1.9 %shard_map.104 = (f32[16,128]{1,0:T(8,128)S(1)}, f32[4,128]{1,0:T(4,128)S(1)}, f32[4,128]{1,0:T(4,128)S(1)}, f32[8208,128]{1,0:T(8,128)S(1)}, f32[8208,128]{1,0:T(8,128)S(1)}, /*index=5*/f32[8192,128]{1,0:T(8,128)S(1)}) custom-call(bf16[520,128]{1,0:T(8,128)(2,1)S(1)} %get-tuple-element.38.refs_0_, ...), custom_call_target="tpu_custom_call", output_to_operand_aliasing={{3}: (23, {}), {4}: (24, {}), {5}: (25, {})} | custom-call | tf_op jit(solution)/shard_map/pallas_call | solution.py:458
  54.7 1.6 %collective-permute-start.15 = (f32[4,128]{1,0:T(4,128)S(1)}, f32[4,128]{1,0:T(4,128)S(1)}, u32[]{:S(2)}, u32[]{:S(2)}) collective-permute-start(f32[4,128]{1,0:T(4,128)S(1)} %get-tuple-element.73), channel_id=1, source_target_pairs={{0,1},{1,0},{2,3},{3,2},{4,5},{5,4},{6,7},{7,6},{8,9},{9,8},{10,11... | collective-permute-start | bytes 6152 | tf_op jit(solution)/shard_map/ppermute | solution.py:483
  56.3 0.6 %shard_map.105 = f32[16,128]{1,0:T(8,128)} custom-call(f32[16,128]{1,0:T(8,128)S(1)} %get-tuple-element.71.array_ref), custom_call_target="tpu_custom_call" | custom-call | tf_op jit(solution)/shard_map/pallas_call | solution.py:480
  56.9 0.2 collective-permute-done.15
  57.2 0.6 %add_bitcast_fusion = f32[512]{0:T(512)} fusion(f32[4,128]{1,0:T(4,128)S(1)} %get-tuple-element.72, f32[4,128]{1,0:T(4,128)S(1)} %collective-permute-done.15), kind=kLoop, calls=%fused_computation.2 | loop fusion | flops 512 | bytes 6144 | tf_op jit(solution)/shard_map/reshape | solution.py:483
  (17 shorter events, 0.0 us)
Async XLA Ops:
  1.3 1.2 %copy-start = (bf16[8,128,512]{2,1,0:T(8,128)(2,1)S(1)}, bf16[8,128,512]{2,1,0:T(8,128)(2,1)}, u32[]{:S(2)}) copy-start(bf16[8,128,512]{2,1,0:T(8,128)(2,1)} %embedding_ref.1) | copy-start | bytes 3145732
  3.5 10.7 %collective-permute-start = (bf16[520,128]{1,0:T(8,128)(2,1)S(1)}, bf16[520,128]{1,0:T(8,128)(2,1)S(1)}, u32[]{:S(2)}, u32[]{:S(2)}) collective-permute-start(bf16[520,128]{1,0:T(8,128)(2,1)S(1)} %get-tuple-element.39), channel_id=1, source_target_pairs={{0,28},{2,30},{4,24},{6,26},{8,20},{10,22},{12,16},{14,18},{16,12}... | collective-permute-start | bytes 399368 | tf_op jit(solution)/shard_map/ppermute | solution.py:444
  5.8 13.3 %collective-permute-start.1 = (bf16[520,128]{1,0:T(8,128)(2,1)S(1)}, bf16[520,128]{1,0:T(8,128)(2,1)S(1)}, u32[]{:S(2)}, u32[]{:S(2)}) collective-permute-start(bf16[520,128]{1,0:T(8,128)(2,1)S(1)} %get-tuple-element.40), channel_id=1, source_target_pairs={{0,30},{2,28},{4,26},{6,24},{8,22},{10,20},{12,18},{14,16},{16,14}... | collective-permute-start | bytes 399368 | tf_op jit(solution)/shard_map/ppermute | solution.py:444
  6.8 12.3 %collective-permute-start.2 = (bf16[520,128]{1,0:T(8,128)(2,1)S(1)}, bf16[520,128]{1,0:T(8,128)(2,1)S(1)}, u32[]{:S(2)}, u32[]{:S(2)}) collective-permute-start(bf16[520,128]{1,0:T(8,128)(2,1)S(1)} %get-tuple-element.41), channel_id=1, source_target_pairs={{0,2},{2,0},{4,6},{6,4},{8,10},{10,8},{12,14},{14,12},{16,18},{18,... | collective-permute-start | bytes 399368 | tf_op jit(solution)/shard_map/ppermute | solution.py:444
  7.1 13.7 %collective-permute-start.3 = (bf16[520,128]{1,0:T(8,128)(2,1)S(1)}, bf16[520,128]{1,0:T(8,128)(2,1)S(1)}, u32[]{:S(2)}, u32[]{:S(2)}) collective-permute-start(bf16[520,128]{1,0:T(8,128)(2,1)S(1)} %get-tuple-element.42), channel_id=1, source_target_pairs={{0,4},{2,6},{4,0},{6,2},{8,12},{10,14},{12,8},{14,10},{16,20},{18,... | collective-permute-start | bytes 399368 | tf_op jit(solution)/shard_map/ppermute | solution.py:444
  8.3 13.7 %collective-permute-start.4 = (bf16[520,128]{1,0:T(8,128)(2,1)S(1)}, bf16[520,128]{1,0:T(8,128)(2,1)S(1)}, u32[]{:S(2)}, u32[]{:S(2)}) collective-permute-start(bf16[520,128]{1,0:T(8,128)(2,1)S(1)} %get-tuple-element.43), channel_id=1, source_target_pairs={{0,10},{2,8},{4,14},{6,12},{8,2},{10,0},{12,6},{14,4},{16,26},{18,... | collective-permute-start | bytes 399368 | tf_op jit(solution)/shard_map/ppermute | solution.py:444
  12.9 1.2 %copy-start.1 = (bf16[1024,512]{1,0:T(8,128)(2,1)S(1)}, bf16[1024,512]{1,0:T(8,128)(2,1)}, u32[]{:S(2)}) copy-start(bf16[1024,512]{1,0:T(8,128)(2,1)} %param.11) | copy-start | bytes 3145732
  14.2 11.4 %collective-permute-start.5 = (bf16[520,128]{1,0:T(8,128)(2,1)S(1)}, bf16[520,128]{1,0:T(8,128)(2,1)S(1)}, u32[]{:S(2)}, u32[]{:S(2)}) collective-permute-start(bf16[520,128]{1,0:T(8,128)(2,1)S(1)} %shard_map.87.refs_1_), channel_id=1, source_target_pairs={{0,16},{2,18},{4,20},{6,22},{8,24},{10,26},{12,28},{14,30},{16,0},... | collective-permute-start | bytes 399368 | tf_op jit(solution)/shard_map/ppermute | solution.py:444
  19.1 6.4 %copy-start.3 = (bf16[512]{0:T(512)(128)(2,1)S(1)}, bf16[512]{0:T(512)(128)(2,1)}, u32[]{:S(2)}) copy-start(bf16[512]{0:T(512)(128)(2,1)} %param.13) | copy-start | bytes 3076
  19.1 6.4 %copy-start.2 = (f32[512]{0:T(512)S(1)}, f32[512]{0:T(512)}, u32[]{:S(2)}) copy-start(f32[512]{0:T(512)} %param.12) | copy-start | bytes 6148
  19.1 7.5 %collective-permute-start.6 = (bf16[520,128]{1,0:T(8,128)(2,1)S(1)}, bf16[520,128]{1,0:T(8,128)(2,1)S(1)}, u32[]{:S(2)}, u32[]{:S(2)}) collective-permute-start(bf16[520,128]{1,0:T(8,128)(2,1)S(1)} %shard_map.90.refs_1_), channel_id=1, source_target_pairs={{0,8},{2,10},{4,12},{6,14},{8,0},{10,2},{12,4},{14,6},{16,24},{18,... | collective-permute-start | bytes 399368 | tf_op jit(solution)/shard_map/ppermute | solution.py:444
  19.2 11.0 %collective-permute-start.7 = (bf16[520,128]{1,0:T(8,128)(2,1)S(1)}, bf16[520,128]{1,0:T(8,128)(2,1)S(1)}, u32[]{:S(2)}, u32[]{:S(2)}) collective-permute-start(bf16[520,128]{1,0:T(8,128)(2,1)S(1)} %shard_map.91.refs_1_), channel_id=1, source_target_pairs={{0,24},{2,26},{4,28},{6,30},{8,16},{10,18},{12,20},{14,22},{16,8},... | collective-permute-start | bytes 399368 | tf_op jit(solution)/shard_map/ppermute | solution.py:444
  20.8 9.4 %collective-permute-start.8 = (bf16[520,128]{1,0:T(8,128)(2,1)S(1)}, bf16[520,128]{1,0:T(8,128)(2,1)S(1)}, u32[]{:S(2)}, u32[]{:S(2)}) collective-permute-start(bf16[520,128]{1,0:T(8,128)(2,1)S(1)} %shard_map.93.refs_1_), channel_id=1, source_target_pairs={{0,6},{2,4},{4,2},{6,0},{8,14},{10,12},{12,10},{14,8},{16,22},{18,... | collective-permute-start | bytes 399368 | tf_op jit(solution)/shard_map/ppermute | solution.py:444
  22.0 18.6 %collective-permute-start.9 = (bf16[520,128]{1,0:T(8,128)(2,1)S(1)}, bf16[520,128]{1,0:T(8,128)(2,1)S(1)}, u32[]{:S(2)}, u32[]{:S(2)}) collective-permute-start(bf16[520,128]{1,0:T(8,128)(2,1)S(1)} %shard_map.94.refs_1_), channel_id=1, source_target_pairs={{0,22},{2,20},{4,18},{6,16},{8,30},{10,28},{12,26},{14,24},{16,6},... | collective-permute-start | bytes 399368 | tf_op jit(solution)/shard_map/ppermute | solution.py:444
  25.6 15.3 %collective-permute-start.10 = (bf16[520,128]{1,0:T(8,128)(2,1)S(1)}, bf16[520,128]{1,0:T(8,128)(2,1)S(1)}, u32[]{:S(2)}, u32[]{:S(2)}) collective-permute-start(bf16[520,128]{1,0:T(8,128)(2,1)S(1)} %shard_map.95.refs_1_), channel_id=1, source_target_pairs={{0,18},{2,16},{4,22},{6,20},{8,26},{10,24},{12,30},{14,28},{16,2},... | collective-permute-start | bytes 399368 | tf_op jit(solution)/shard_map/ppermute | solution.py:444
  26.6 14.1 %collective-permute-start.11 = (bf16[520,128]{1,0:T(8,128)(2,1)S(1)}, bf16[520,128]{1,0:T(8,128)(2,1)S(1)}, u32[]{:S(2)}, u32[]{:S(2)}) collective-permute-start(bf16[520,128]{1,0:T(8,128)(2,1)S(1)} %shard_map.96.refs_1_), channel_id=1, source_target_pairs={{0,14},{2,12},{4,10},{6,8},{8,6},{10,4},{12,2},{14,0},{16,30},{18,... | collective-permute-start | bytes 399368 | tf_op jit(solution)/shard_map/ppermute | solution.py:444
  30.1 10.6 %collective-permute-start.12 = (bf16[520,128]{1,0:T(8,128)(2,1)S(1)}, bf16[520,128]{1,0:T(8,128)(2,1)S(1)}, u32[]{:S(2)}, u32[]{:S(2)}) collective-permute-start(bf16[520,128]{1,0:T(8,128)(2,1)S(1)} %shard_map.98.refs_1_), channel_id=1, source_target_pairs={{0,12},{2,14},{4,8},{6,10},{8,4},{10,6},{12,0},{14,2},{16,28},{18,... | collective-permute-start | bytes 399368 | tf_op jit(solution)/shard_map/ppermute | solution.py:444
  30.2 17.6 %collective-permute-start.13 = (bf16[520,128]{1,0:T(8,128)(2,1)S(1)}, bf16[520,128]{1,0:T(8,128)(2,1)S(1)}, u32[]{:S(2)}, u32[]{:S(2)}) collective-permute-start(bf16[520,128]{1,0:T(8,128)(2,1)S(1)} %shard_map.99.refs_1_), channel_id=1, source_target_pairs={{0,20},{2,22},{4,16},{6,18},{8,28},{10,30},{12,24},{14,26},{16,4},... | collective-permute-start | bytes 399368 | tf_op jit(solution)/shard_map/ppermute | solution.py:444
  40.6 12.2 %collective-permute-start.14 = (bf16[520,128]{1,0:T(8,128)(2,1)S(1)}, bf16[520,128]{1,0:T(8,128)(2,1)S(1)}, u32[]{:S(2)}, u32[]{:S(2)}) collective-permute-start(bf16[520,128]{1,0:T(8,128)(2,1)S(1)} %shard_map.101), channel_id=1, source_target_pairs={{0,26},{2,24},{4,30},{6,28},{8,18},{10,16},{12,22},{14,20},{16,10}... | collective-permute-start | bytes 399368 | tf_op jit(solution)/shard_map/ppermute | solution.py:444
  54.7 2.4 %collective-permute-start.15 = (f32[4,128]{1,0:T(4,128)S(1)}, f32[4,128]{1,0:T(4,128)S(1)}, u32[]{:S(2)}, u32[]{:S(2)}) collective-permute-start(f32[4,128]{1,0:T(4,128)S(1)} %get-tuple-element.73), channel_id=1, source_target_pairs={{0,1},{1,0},{2,3},{3,2},{4,5},{5,4},{6,7},{7,6},{8,9},{9,8},{10,11... | collective-permute-start | bytes 6152 | tf_op jit(solution)/shard_map/ppermute | solution.py:483
